TPU v7x, 128 devices: a whole 4x4x4 slice. The times are simulated.
128 devices in a mesh: zon: 32 (over z, x_hi, y), mer: 4 (over x_lo, core).
Axes of the slice: x: 4 (x_hi: 2, x_lo: 2; x = x_hi * 2 + x_lo), y: 4, z: 4, core: 2. Of those that a mesh axis runs over, the one named last changes fastest.
Arguments:
- sea_level: float32 [512, 16384], P('mer', 'zon'), may hold values from -6 to 6
- forcing: float32 [512, 16384], P('mer', 'zon'), may hold values from -6 to 6
- link_weights: float32 [8, 512, 16384], P(None, 'mer', 'zon'), may hold values from 0.1 to 2
- excess: float32 [512, 16384], P('mer', 'zon'), may hold values from 0.05 to 0.5
- ocean_mask: int32 [512, 16384], P('mer', 'zon'), may hold values 0 or 1
- current: float32 [2, 512, 16384], P(None, 'mer', 'zon'), may hold values from -6 to 6
- intersection_block: int32 [128, 128, 8], P(('zon', 'mer')), may hold values from -1 to 511, as said below
- intersection_cols: int32 [128, 128, 8, 128], P(('zon', 'mer')), may hold values from -1 to 127, as said below
- ice_mass: float32 [128, 128, 8, 128], P(('zon', 'mer')), may hold values from 0.2 to 3
- coriolis: float32 [128, 128, 8, 128], P(('zon', 'mer')), may hold values from -1.5 to 1.5
- ice_start: float32 [2, 128, 128, 8, 128], P(None, ('zon', 'mer')), may hold values from -6 to 6
- wind_stress: float32 [2, 128, 128, 8, 128], P(None, ('zon', 'mer')), may hold values from -6 to 6
Outputs:
- surface: float32 [512, 16384], P('mer', 'zon')
- velocity: float32 [2, 128, 128, 8, 128], P(None, ('zon', 'mer'))
Inputs may be any that keep to these rules, and one draw needn't show every extreme that they name: `intersection_block`: for each owner device and ice device, the live ocean block numbers come first among the 8 slots and empty slots hold -1; in every draw one ice device receives 8 live blocks from every owner device. `intersection_cols`: within a live intersection block the cells named by different rows are distinct; rows of empty slots are all -1.
All inputs are finite; a program needn't handle non-finite values. No bound on the sum of `ocean_mask` on one device may be relied on, other than what follows from the above.
Results may differ from a plain program's by a relative error of at most 0.00002.
Values sent between devices are 32-bit elements; how exact they have to be, the bound alone decides.
No kernel may reach another device: no remote copies, remote signals or barrier semaphores. Data moves between devices by JAX's collectives and lax.ppermute only.
A program may use at most 256 MiB of HBM per device.

v0:
```python
import jax
import jax.numpy as jnp
from jax import lax
from jax.sharding import PartitionSpec as P

SWEEPS = 2
ICE_SWEEPS = 3


drag_coeff = 1.0
link_coeff = 0.5
neighbour_steps = ((0, 1), (0, -1), (1, 0), (-1, 0), (1, 1), (1, -1), (-1, 1), (-1, -1))


def padded_2(shard, sides, width, wrap):
    for axis, dim in sides:
        count, length = (lax.axis_size(axis), shard.shape[dim])
        up = [(i, (i + 1) % count) for i in range(count if wrap else count - 1)]
        down = [(j, i) for i, j in up]
        last = lax.slice_in_dim(shard, length - width, length, axis=dim)
        first = lax.slice_in_dim(shard, 0, width, axis=dim)
        before = lax.ppermute(last, axis, up)
        after = lax.ppermute(first, axis, down)
        shard = jnp.concatenate([before, shard, after], axis=dim)
    return shard


def colour_sequence(sweep_count):
    return [0] + [1, 2, 3, 2, 1, 0] * sweep_count


def gauss_seidel(surface, source, link_weights, diagonal, is_ocean, pad_fn):
    row_count, col_count = surface.shape
    row_parity = lax.broadcasted_iota(jnp.int32, (row_count, col_count), 0) % 2
    col_parity = lax.broadcasted_iota(jnp.int32, (row_count, col_count), 1) % 2
    colours = 2 * row_parity + col_parity
    for colour in colour_sequence(SWEEPS):
        padded = pad_fn(surface)
        gathered = source
        for position, (row_step, col_step) in enumerate(neighbour_steps):
            gathered = (
                gathered
                + link_weights[position]
                * padded[
                    1 + row_step : 1 + row_step + row_count, 1 + col_step : 1 + col_step + col_count
                ]
            )
        surface = jnp.where(is_ocean & (colours == colour), gathered / diagonal, surface)
    return surface


def zero_pad(surface):
    return jnp.pad(surface, 1)


def along_block(values):
    padded = jnp.pad(values, [(0, 0)] * (values.ndim - 1) + [(1, 1)])
    return padded[..., :-2] + padded[..., 2:]


def ice_momentum(ice_mass, coriolis, ice_start, wind_stress, current):
    diagonal = ice_mass + drag_coeff + 2.0 * link_coeff
    turning = coriolis * ice_mass
    determinant = diagonal * diagonal + turning * turning
    base_east = ice_mass * ice_start[0] + wind_stress[0] + drag_coeff * current[0]
    base_north = ice_mass * ice_start[1] + wind_stress[1] + drag_coeff * current[1]
    velocity = ice_start
    for sweep_index in range(ICE_SWEEPS):
        beside = along_block(velocity)
        right_east = base_east + link_coeff * beside[0]
        right_north = base_north + link_coeff * beside[1]
        velocity = jnp.stack(
            [
                (diagonal * right_east + turning * right_north) / determinant,
                (diagonal * right_north - turning * right_east) / determinant,
            ]
        )
    return velocity


def to_ice(values):
    moved = lax.all_to_all(values, ("zon", "mer"), split_axis=2, concat_axis=1, tiled=True)
    return moved.reshape(values.shape)


def to_ocean(values):
    moved = lax.all_to_all(values, ("zon", "mer"), split_axis=2, concat_axis=1, tiled=True)
    return moved.reshape(values.shape)


def local(
    sea_level,
    forcing,
    link_weights,
    excess,
    ocean_mask,
    current,
    intersection_block,
    intersection_cols,
    ice_mass,
    coriolis,
    ice_start,
    wind_stress,
):
    row_count, col_count = sea_level.shape
    block = intersection_cols.shape[-1]
    cell_count = row_count * col_count
    slot_shape = intersection_block.shape[1:]
    slot_count = slot_shape[0] * slot_shape[1]
    slot_blocks = intersection_block[0].reshape(slot_count)
    slot_cols = intersection_cols[0].reshape(slot_count, block)
    is_valid = slot_cols >= 0
    target = jnp.where(
        is_valid, jnp.maximum(slot_blocks, 0)[:, None] * block + slot_cols, cell_count
    )
    flat_target = target.reshape(slot_count * block)
    flat_current = current.reshape(2, cell_count)
    fetched = jnp.take(flat_current, jnp.minimum(flat_target, cell_count - 1), axis=1)
    values = jnp.where(is_valid.reshape(1, slot_count * block), fetched, 0.0)
    values = values.reshape(2, slot_shape[0], slot_shape[1], block)
    ice_current = to_ice(values[:, None])
    velocity = ice_momentum(ice_mass, coriolis, ice_start, wind_stress, ice_current)
    ice_drag = drag_coeff * (velocity - ice_current)
    returned = to_ocean(ice_drag)[:, 0].reshape(2, slot_count * block)
    stress_grid = (
        jnp.zeros((2, cell_count), jnp.float32).at[:, flat_target].add(returned, mode="drop")
    )
    stress_grid = stress_grid.reshape(2, row_count, col_count)
    cycle_north = padded_2(stress_grid[1], (("zon", 1),), 1, True)
    lat_east = padded_2(stress_grid[0], (("mer", 0),), 1, False)
    zonal_diff = cycle_north[:, 2:] - cycle_north[:, :-2]
    meridional_diff = lat_east[2:] - lat_east[:-2]
    source = forcing + zonal_diff - meridional_diff
    is_ocean = ocean_mask > 0
    surface = jnp.where(is_ocean, sea_level, 0.0)
    rim_width = 6 * SWEEPS + 2
    stacked = jnp.concatenate(
        [
            surface[None],
            source[None],
            link_weights,
            excess[None],
            ocean_mask.astype(jnp.float32)[None],
        ],
        axis=0,
    )
    cycle_ext = padded_2(stacked, (("zon", 2),), rim_width, True)
    widened = padded_2(cycle_ext, (("mer", 1),), rim_width, False)
    wide_ocean = widened[11] > 0.5
    wide_diagonal = jnp.where(wide_ocean, (1.0 + widened[10]) * jnp.sum(widened[2:10], axis=0), 1.0)
    result = gauss_seidel(
        widened[0], widened[1], widened[2:10], wide_diagonal, wide_ocean, zero_pad
    )
    surface = result[rim_width : rim_width + row_count, rim_width : rim_width + col_count]
    return (surface, velocity)


def solution(mesh):
    return jax.shard_map(
        local,
        mesh=mesh,
        in_specs=(
            P("mer", "zon"),
            P("mer", "zon"),
            P(None, "mer", "zon"),
            P("mer", "zon"),
            P("mer", "zon"),
            P(None, "mer", "zon"),
            P(("zon", "mer"), None, None),
            P(("zon", "mer"), None, None, None),
            P(("zon", "mer"), None, None, None),
            P(("zon", "mer"), None, None, None),
            P(None, ("zon", "mer"), None, None, None),
            P(None, ("zon", "mer"), None, None, None),
        ),
        out_specs=(P("mer", "zon"), P(None, ("zon", "mer"), None, None, None)),
        check_vma=False,
    )
```

profile of v0, /device:TPU:1, one launch (start us, length us, event | category | flops | bytes accessed | tf_op | source)
XLA Modules:
  0.0 1442.8 jit_solution(10808669147539427486)
XLA Ops:
  1.8 2.3 compare_select_fusion
  4.2 16.5 %copy.67 = f32[2,128,512]{0,2,1:T(8,128)} copy(f32[2,128,512]{2,1,0:T(8,128)S(1)} %copy-done.3) | data formatting | bytes 1048576 | tf_op args[5]
  20.7 441.0 %gather_fusion = f32[131072,2]{1,0:T(8,128)} fusion(f32[2,65536]{0,1:T(8,128)} %bitcast.390, s32[131072]{0:T(1024)S(1)} %broadcast_clamp_fusion), kind=kCustom, calls=%fused_computation | custom fusion | bytes 2621440 | tf_op jit(solution)/shard_map/jit(_take)/gather | solution.py:118
  461.6 35.0 %copy.68 = f32[2,1,128,8,128]{4,3,1,0,2:T(8,128)S(1)} copy(f32[2,1,128,8,128]{0,4,3,2,1:T(8,128)} %bitcast.11) | data formatting | bytes 2097152 | tf_op jit(solution)/shard_map/jit(_take)/gather | solution.py:118
  498.3 11.5 all-to-all-start
  512.0 17.2 %all-to-all-done = f32[2,1,128,8,128]{4,3,1,0,2:T(8,128)S(1)} async-done(((f32[2,1,128,8,128]{4,3,1,0,2:T(8,128)}), f32[2,1,128,8,128]{4,3,1,0,2:T(8,128)S(1)}, u32[]{:S(2)}, u32[]{:S(2)}) %all-to-all-start) | async-done | bytes 1048608 | tf_op jit(solution)/shard_map/all_to_all | solution.py:82
  535.6 16.7 %all-to-all-start.1 = ((f32[2,1,128,8,128]{4,3,1,0,2:T(8,128)}), f32[2,1,128,8,128]{4,3,1,0,2:T(8,128)}, u32[]{:S(2)}, u32[]{:S(2)}) async-start(f32[2,1,128,8,128]{4,3,1,0,2:T(8,128)} %get-tuple-element.37), calls=%async_computation.1 | async-start | bytes 2097152 | tf_op jit(solution)/shard_map/all_to_all | solution.py:87
  555.7 15.6 %all-to-all-done.1 = f32[2,1,128,8,128]{4,3,1,0,2:T(8,128)} async-done(((f32[2,1,128,8,128]{4,3,1,0,2:T(8,128)}), f32[2,1,128,8,128]{4,3,1,0,2:T(8,128)}, u32[]{:S(2)}, u32[]{:S(2)}) %all-to-all-start.1) | async-done | bytes 1048608 | tf_op jit(solution)/shard_map/all_to_all | solution.py:87
  573.6 2.9 reshape.263
  576.4 30.1 %copy.73 = f32[131072,2]{1,0:T(8,128)} copy(f32[131072,2]{0,1:T(2,128)} %bitcast.391) | data formatting | bytes 2097152 | tf_op jit(solution)/shard_map/reshape;squeeze;reshape | solution.py:124
  606.5 706.8 %scatter_custom_fusion = f32[2,65536]{0,1:T(8,128)} fusion(s32[131072]{0:T(1024)} %bitcast.395, f32[131072,2]{1,0:T(8,128)} %copy.73, f32[]{:T(128)} %constant.24.clone.1), kind=kCustom, calls=%fused_computation.4 | custom fusion | flops 262144 | bytes 524800 | tf_op jit(solution)/shard_map/scatter-add | solution.py:126
  1313.4 34.7 %slice_reduce_fusion.1 = (f32[65536]{0:T(1024)}, f32[65536]{0:T(1024)}) fusion(f32[2,65536]{0,1:T(8,128)} %scatter_custom_fusion), kind=kLoop, calls=%fused_computation.3 | loop fusion | bytes 1048576 | tf_op jit(solution)/shard_map/slice | solution.py:129
  1351.7 2.8 collective-permute-start.2
  1354.5 2.7 collective-permute-start.3
  1360.4 2.9 copy.79
  1377.0 7.2 collective-permute-start.5
  1386.6 3.8 fusion.197
  1390.4 3.3 copy.80
  1393.7 4.2 collective-permute-start.6
  1397.9 3.3 copy.81
  1405.4 3.2 copy.82
  1408.6 3.0 collective-permute-done.7
  1411.7 3.2 copy.83
  1414.9 6.0 pad_maximum_fusion
  (83 shorter events, 65.3 us)
Async XLA Ops:
  0.6 3.5 copy-start.3
  461.6 35.1 %copy-start.1 = (s32[1,128,8,128]{3,2,1,0:T(8,128)S(1)}, s32[1,128,8,128]{3,2,1,0:T(8,128)}, u32[]{:S(2)}) copy-start(s32[1,128,8,128]{3,2,1,0:T(8,128)} %param.19) | copy-start | bytes 1572868
  497.1 32.1 %copy-start = (f32[1,128,8,128]{3,2,1,0:T(8,128)S(1)}, f32[1,128,8,128]{3,2,1,0:T(8,128)}, u32[]{:S(2)}) copy-start(f32[1,128,8,128]{3,2,1,0:T(8,128)} %param.20) | copy-start | bytes 1572868
  498.3 30.8 %all-to-all-start = ((f32[2,1,128,8,128]{4,3,1,0,2:T(8,128)}), f32[2,1,128,8,128]{4,3,1,0,2:T(8,128)S(1)}, u32[]{:S(2)}, u32[]{:S(2)}) async-start(f32[2,1,128,8,128]{4,3,1,0,2:T(8,128)} %select_select_fusion), calls=%async_computation | async-start | bytes 2097152 | tf_op jit(solution)/shard_map/all_to_all | solution.py:82
  534.1 19.6 %copy-start.4 = (s32[128,512]{1,0:T(8,128)S(1)}, s32[128,512]{1,0:T(8,128)}, u32[]{:S(2)}) copy-start(s32[128,512]{1,0:T(8,128)} %param.16) | copy-start | bytes 786436
  534.1 19.7 %copy-start.5 = (f32[128,512]{1,0:T(8,128)S(1)}, f32[128,512]{1,0:T(8,128)}, u32[]{:S(2)}) copy-start(f32[128,512]{1,0:T(8,128)} %param.12) | copy-start | bytes 786436
  535.6 35.7 %all-to-all-start.1 = ((f32[2,1,128,8,128]{4,3,1,0,2:T(8,128)}), f32[2,1,128,8,128]{4,3,1,0,2:T(8,128)}, u32[]{:S(2)}, u32[]{:S(2)}) async-start(f32[2,1,128,8,128]{4,3,1,0,2:T(8,128)} %get-tuple-element.37), calls=%async_computation.1 | async-start | bytes 2097152 | tf_op jit(solution)/shard_map/all_to_all | solution.py:87
  1351.7 15.1 %collective-permute-start.2 = (f32[1,512]{0,1:T(8,128)}, f32[1,512]{0,1:T(8,128)}, u32[]{:S(2)}, u32[]{:S(2)}) collective-permute-start(f32[1,512]{0,1:T(8,128)} %get-tuple-element.20), channel_id=1, source_target_pairs={{1,0},{2,1},{3,2},{5,4},{6,5},{7,6},{9,8},{10,9},{11,10},{13,12},{... | collective-permute-start | bytes 6152 | tf_op jit(solution)/shard_map/ppermute | solution.py:23
  1354.5 13.3 collective-permute-start.3
  1358.8 10.1 collective-permute-start
  1360.4 9.8 collective-permute-start.1
  1374.1 2.8 copy-start.2
  1377.0 9.3 collective-permute-start.4
  1377.0 9.2 collective-permute-start.5
  1393.7 11.7 collective-permute-start.6
  1401.2 10.5 collective-permute-start.7
where the time goes:
time: 1450 us; the launch traced here: 1440 us
  other arithmetic  751 us (52%)
  local copies, waits for them, and re-layouts  602 us (42%)
  starting transfers between devices  48.7 us (3%)
  waiting for transfers between devices  39.1 us (3%)
    scatter-add x1, other arithmetic, local(): jnp.zeros((2, cell_count), jnp.float32).at[:, flat_target]  707 us
    gather x2, local copies, waits for them, and re-layouts, local(): jnp.take(flat_current, jnp.minimum(flat_target, cell_count - 1), axis=1)  476 us
    slice x1, local copies, waits for them, and re-layouts, local(): cycle_north = padded_2(stress_grid[1], (('zon', 1),), 1, True)  34.7 us
    another operation x2, local copies, waits for them, and re-layouts, local(): returned = to_ocean(ice_drag)[:, 0].reshape(2, slot_count * block)  33 us
  transfers between devices with their start and end apart: 10, of which 5 were waited for; matrix products, arithmetic and copies ran while one was open for 2% of the time, Pallas kernels for 0%

commit v1 on v0

v1 whole, which is shorter than its diff:
```python
import jax
import jax.numpy as jnp
from jax import lax
from jax.experimental import pallas as pl
from jax.experimental.pallas import tpu as pltpu
from jax.sharding import PartitionSpec as P

SWEEPS = 2
ICE_SWEEPS = 3
DRAG = 1.0
LINK = 0.5
STEPS = ((0, 1), (0, -1), (1, 0), (-1, 0), (1, 1), (1, -1), (-1, 1), (-1, -1))
COLOURS = (0,) + (1, 2, 3, 2, 1, 0) * SWEEPS
F32, BF16, I32 = jnp.float32, jnp.bfloat16, jnp.int32
MIB = 1 << 20
ROWS, COLS, XROWS, XCOLS = 64, 256, 72, 384


def params(vmem=48):
    return pltpu.CompilerParams(vmem_limit_bytes=vmem * MIB)


def cost(flops, moved):
    return pl.CostEstimate(flops=flops, bytes_accessed=moved, transcendentals=0)


def iota(shape, dim):
    return lax.broadcasted_iota(I32, shape, dim)


def lane_gather(values, index):
    return jnp.take_along_axis(values, index, axis=1, mode="promise_in_bounds")


def split3(values):
    high = values.astype(BF16)
    rest = values - high.astype(F32)
    middle = rest.astype(BF16)
    low = (rest - middle.astype(F32)).astype(BF16)
    return high, middle, low


def dot(a, b):
    return jnp.dot(a, b, preferred_element_type=F32)


def fetch_kernel(current, key, cols, out, table, rows):
    count = cols.shape[0]
    for c in range(2):
        for k in range(4):
            parts = split3(current[c, :, 128 * k : 128 * k + 128])
            for part in range(3):
                table[part, 128 * k : 128 * k + 128, 128 * c : 128 * c + 128] = parts[part]
    step = min(8 * count, 256)
    for start in range(0, 8 * count, step):
        hot = jnp.where(key[start : start + step] == iota((step, 512), 1), 1.0, 0.0).astype(BF16)
        rows[start : start + step] = dot(hot, table[0]) + dot(hot, table[1]) + dot(hot, table[2])

    def body(i, carry):
        index = cols[i]
        inside = jnp.maximum(index, 0)
        tile = rows[pl.ds(pl.multiple_of(8 * i, 8), 8)]
        for c in range(2):
            out[i, c] = jnp.where(index >= 0, lane_gather(tile[:, 128 * c : 128 * c + 128], inside), 0.0)
        return carry

    lax.fori_loop(0, count, body, 0, unroll=8)


def fetch(current, key, cols):
    count = cols.shape[0]
    return pl.pallas_call(
        fetch_kernel,
        out_shape=jax.ShapeDtypeStruct((count, 2, 8, 128), F32),
        scratch_shapes=[pltpu.VMEM((3, 512, 256), BF16), pltpu.VMEM((8 * count, 256), F32)],
        compiler_params=params(),
        cost_estimate=cost(10**9, 2 * MIB),
        name="fetch",
    )(current, key, cols)


def invert_kernel(cols, key, inverse, hot):
    count = cols.shape[0]
    hot[...] = jnp.where(iota((512, 8 * count), 0) == key[...], 1.0, 0.0).astype(BF16)
    lane = iota((8, 1024), 1)
    weights = jnp.where(lane // 128 == iota((8, 1024), 0), lane % 128 + 1, 0).astype(F32).astype(BF16)
    place = iota((128, 128), 0)

    def body(i, carry):
        index = cols[i]
        target = jnp.where(index >= 0, (index >> 1) + 64 * (index & 1), -1)
        masks = [
            jnp.where(place == jnp.broadcast_to(target[s : s + 1], (128, 128)), 1.0, 0.0).astype(BF16)
            for s in range(8)
        ]
        found = lax.dot_general(
            weights, jnp.concatenate(masks, axis=1), (((1,), (1,)), ((), ())), preferred_element_type=F32
        )
        inverse[i] = found.astype(I32) - 1
        return carry

    lax.fori_loop(0, count, body, 0, unroll=2)


def invert(cols, key):
    count = cols.shape[0]
    return pl.pallas_call(
        invert_kernel,
        out_shape=(jax.ShapeDtypeStruct((count, 8, 128), I32), jax.ShapeDtypeStruct((512, 8 * count), BF16)),
        compiler_params=params(),
        cost_estimate=cost(10**10, 2 * MIB),
        name="invert",
    )(cols, key)


def ice_kernel(mass_ref, coriolis_ref, start_ref, wind_ref, current_ref, velocity_ref, drag_ref):
    lane = iota((8, 128), 1)

    def beside(v):
        before = jnp.where(lane == 0, 0.0, pltpu.roll(v, 1, 1))
        after = jnp.where(lane == 127, 0.0, pltpu.roll(v, 127, 1))
        return before + after

    def body(i, carry):
        mass = mass_ref[i]
        a = mass + DRAG + 2.0 * LINK
        t = coriolis_ref[i] * mass
        inverse = 1.0 / (a * a + t * t)
        a = a * inverse
        t = t * inverse
        east, north = start_ref[0, i], start_ref[1, i]
        current = (current_ref[i, 0], current_ref[i, 1])
        base_east = mass * east + wind_ref[0, i] + DRAG * current[0]
        base_north = mass * north + wind_ref[1, i] + DRAG * current[1]
        for _ in range(ICE_SWEEPS):
            right_east = base_east + LINK * beside(east)
            right_north = base_north + LINK * beside(north)
            east = a * right_east + t * right_north
            north = a * right_north - t * right_east
        velocity_ref[0, i] = east
        velocity_ref[1, i] = north
        drag_ref[i, 0] = DRAG * (east - current[0])
        drag_ref[i, 1] = DRAG * (north - current[1])
        return carry

    lax.fori_loop(0, mass_ref.shape[0], body, 0, unroll=4)


def ice(mass, coriolis, start, wind, current):
    count = mass.shape[0]
    step = min(count, 32)
    one = pl.BlockSpec((step, 8, 128), lambda i: (i, 0, 0))
    two = pl.BlockSpec((2, step, 8, 128), lambda i: (0, i, 0, 0))
    pair = pl.BlockSpec((step, 2, 8, 128), lambda i: (i, 0, 0, 0))
    return pl.pallas_call(
        ice_kernel,
        grid=(count // step,),
        in_specs=[one, one, two, two, pair],
        out_specs=(two, pair),
        out_shape=(
            jax.ShapeDtypeStruct((2, count, 8, 128), F32),
            jax.ShapeDtypeStruct((count, 2, 8, 128), F32),
        ),
        compiler_params=params(),
        cost_estimate=cost(10**7, 6 * MIB),
        name="ice",
    )(mass, coriolis, start, wind, current)


def scatter_kernel(drag, inverse, hot, planes, side, ends, corner, parts):
    count = inverse.shape[0]
    zero = jnp.zeros((8, 128), F32)

    def body(j, carry):
        rows = pl.ds(pl.multiple_of(16 * j, 16), 16)
        for c in range(2):
            halves = []
            for i in (2 * j, 2 * j + 1):
                index = inverse[i]
                halves.append(jnp.where(index >= 0, lane_gather(drag[i, c], jnp.maximum(index, 0)), zero))
            pieces = split3(jnp.concatenate(halves, axis=0))
            for part in range(3):
                parts[part, rows, 128 * c : 128 * c + 128] = pieces[part]
        return carry

    lax.fori_loop(0, count // 2, body, 0, unroll=4)
    total = dot(hot[...], parts[0]) + dot(hot[...], parts[1]) + dot(hot[...], parts[2])
    low = iota((ROWS, 128), 1) < 64
    lane = iota((ROWS, 128), 1)
    edge = jnp.zeros((ROWS, 128), F32)
    for c in range(2):
        for py in range(2):
            for h in range(2):
                first = 256 * h + 64 * py
                a = total[first : first + 64, 128 * c : 128 * c + 128]
                b = total[first + 128 : first + 192, 128 * c : 128 * c + 128]
                even = jnp.where(low, a, pltpu.roll(b, 64, 1))
                odd = jnp.where(low, pltpu.roll(a, 64, 1), b)
                for px, value in ((0, even), (1, odd)):
                    plane = 2 * py + px
                    planes[c, plane, :, 128 * h : 128 * h + 128] = value
                    ends[c, plane, :, 128 * h : 128 * h + 128] = jnp.where(
                        iota((8, 128), 0) < 4, value[:8], value[56:]
                    )
                    item = 4 * c + plane
                    if h == 0:
                        moved = pltpu.roll(value, 8 * item, 1) if item else value
                        edge = jnp.where(lane // 8 == item, moved, edge)
                    else:
                        moved = pltpu.roll(value, (64 + 8 * item + 8) % 128, 1) if item != 7 else value
                        edge = jnp.where(lane // 8 == 8 + item, moved, edge)
    side[...] = edge
    corner[...] = jnp.where(iota((8, 128), 0) < 4, edge[:8], edge[56:])


def scatter(drag, inverse, hot):
    count = inverse.shape[0]
    return pl.pallas_call(
        scatter_kernel,
        out_shape=(
            jax.ShapeDtypeStruct((2, 4, ROWS, COLS), F32),
            jax.ShapeDtypeStruct((ROWS, 128), F32),
            jax.ShapeDtypeStruct((2, 4, 8, COLS), F32),
            jax.ShapeDtypeStruct((8, 128), F32),
        ),
        scratch_shapes=[pltpu.VMEM((3, 8 * count, 256), BF16)],
        compiler_params=params(),
        cost_estimate=cost(10**9, 3 * MIB),
        name="scatter",
    )(drag, inverse, hot)


ARRAYS = 11


def prepare_kernel(
    sea, forcing, weights, excess, mask, planes, left, right, ends, left_corner, right_corner, halves
):
    lane = iota((8, 128), 1)
    low = lane < 64
    order = jnp.where(low, 2 * lane, 2 * lane - 127)
    swapped = jnp.where(low, 2 * lane + 1, 2 * lane - 128)

    def split(t, carry):
        rows = pl.ds(pl.multiple_of(8 * t, 8), 8)
        w = [weights[k, rows, :] for k in range(8)]
        total = ((w[0] + w[1]) + (w[2] + w[3])) + ((w[4] + w[5]) + (w[6] + w[7]))
        ocean = mask[rows, :] > 0
        inverse = jnp.where(ocean, 1.0 / ((1.0 + excess[rows, :]) * total), 0.0)
        arrays = [v * inverse for v in w]
        arrays += [inverse, forcing[rows, :], jnp.where(ocean, sea[rows, :], 0.0)]
        for n, array in enumerate(arrays):
            for h in range(2):
                a = lane_gather(array[:, 256 * h : 256 * h + 128], order)
                b = lane_gather(array[:, 256 * h + 128 : 256 * h + 256], swapped)
                halves[4 * n + h, rows, :] = jnp.where(low, a, b)
                halves[4 * n + 2 + h, rows, :] = pltpu.roll(jnp.where(low, b, a), 64, 1)
        return carry

    lax.fori_loop(0, 2 * ROWS // 8, split, 0)

    def pack(t, carry):
        out_rows = pl.ds(pl.multiple_of(8 * t, 8), 8)
        for py in range(2):
            rows = pl.ds(16 * t + py, 8, stride=2)
            packed = [[jnp.zeros((8, 128), F32)] * 2, [jnp.zeros((8, 128), F32)] * 2]
            for n in range(ARRAYS):
                for px in range(2):
                    for h in range(2):
                        value = halves[4 * n + 2 * px + h, rows, :]
                        planes[n, 2 * py + px, out_rows, 128 * h : 128 * h + 128] = value
                        item = 2 * n + px
                        shift = (8 * (item % 16) + (8 if h else 0)) % 128
                        moved = pltpu.roll(value, shift, 1) if shift else value
                        packed[h][item // 16] = jnp.where(lane // 8 == item % 16, moved, packed[h][item // 16])
            for g in range(2):
                left[py, out_rows, 128 * g : 128 * g + 128] = packed[0][g]
                right[py, out_rows, 128 * g : 128 * g + 128] = packed[1][g]
        return carry

    lax.fori_loop(0, ROWS // 8, pack, 0)
    top = iota((8, 256), 0) < 4
    for n in range(ARRAYS):
        for p in range(4):
            ends[n, p] = jnp.where(top, planes[n, p, 0:8], planes[n, p, 56:64])
    for py in range(2):
        left_corner[py] = jnp.where(top, left[py, 0:8], left[py, 56:64])
        right_corner[py] = jnp.where(top, right[py, 0:8], right[py, 56:64])


def prepare(sea, forcing, weights, excess, mask):
    return pl.pallas_call(
        prepare_kernel,
        out_shape=(
            jax.ShapeDtypeStruct((ARRAYS, 4, ROWS, COLS), F32),
            jax.ShapeDtypeStruct((2, ROWS, 256), F32),
            jax.ShapeDtypeStruct((2, ROWS, 256), F32),
            jax.ShapeDtypeStruct((ARRAYS, 4, 8, COLS), F32),
            jax.ShapeDtypeStruct((2, 8, 256), F32),
            jax.ShapeDtypeStruct((2, 8, 256), F32),
        ),
        scratch_shapes=[pltpu.VMEM((4 * ARRAYS, 2 * ROWS, 128), F32)],
        compiler_params=params(),
        cost_estimate=cost(10**7, 7 * MIB),
        name="prepare",
    )(sea, forcing, weights, excess, mask)


def extend_kernel(planes, right, left, below, above, below_right, below_left, above_right, above_left, out):
    lane = iota((ROWS, 128), 1)
    lane8 = lane[:8]
    top = iota((8, 128), 0) < 4
    for n in range(ARRAYS):
        for p in range(4):
            py, px = p // 2, p % 2
            item = 2 * n + px
            group, slot = item // 16, item % 16
            span = slice(128 * group, 128 * group + 128)

            def place(from_right, from_left, lanes):
                r = pltpu.roll(from_right, (128 - 8 * slot) % 128, 1) if slot else from_right
                s = pltpu.roll(from_left, (120 - 8 * slot) % 128, 1) if slot != 15 else from_left
                return jnp.where(lanes < 8, r, jnp.where(lanes >= 120, s, 0.0))

            out[n, p, 0:ROWS, 0:COLS] = planes[n, p]
            out[n, p, 0:ROWS, COLS:XCOLS] = place(right[py, :, span], left[py, :, span], lane)
            out[n, p, ROWS:XROWS, 0:COLS] = jnp.where(iota((8, 256), 0) < 4, below[n, p], above[n, p])
            out[n, p, ROWS:XROWS, COLS:XCOLS] = place(
                jnp.where(top, below_right[py, :, span], above_right[py, :, span]),
                jnp.where(top, below_left[py, :, span], above_left[py, :, span]),
                lane8,
            )


def extend(*arrays):
    return pl.pallas_call(
        extend_kernel,
        out_shape=jax.ShapeDtypeStruct((ARRAYS, 4, XROWS, XCOLS), F32),
        compiler_params=params(),
        cost_estimate=cost(10**7, 8 * MIB),
        name="extend",
    )(*arrays)


def row_shift(value, step):
    return pltpu.roll(value, (-step) % XROWS, 0) if step else value


def col_shift(value, step):
    return pltpu.roll(value, (-step) % XCOLS, 1) if step else value


def neighbour(step, parity):
    return (step + parity) // 2


def sweep_kernel(operator, stress, right, left, below, above, below_right, below_left, above_right, above_left, out, wide, source, field, natural):
    lane = iota((ROWS, 128), 1)
    top = iota((8, 128), 0) < 4
    for c in range(2):
        for p in range(4):
            item = 4 * c + p

            def place(from_right, from_left, lanes):
                r = pltpu.roll(from_right, (128 - 8 * item) % 128, 1) if item else from_right
                s = pltpu.roll(from_left, (56 - 8 * item) % 128, 1) if item != 7 else from_left
                return jnp.where(lanes < 64, r, s)

            wide[c, p, 0:ROWS, 0:COLS] = stress[c, p]
            wide[c, p, 0:ROWS, COLS:XCOLS] = place(right[...], left[...], lane)
            wide[c, p, ROWS:XROWS, 0:COLS] = jnp.where(iota((8, 256), 0) < 4, below[c, p], above[c, p])
            wide[c, p, ROWS:XROWS, COLS:XCOLS] = place(
                jnp.where(top, below_right[...], above_right[...]),
                jnp.where(top, below_left[...], above_left[...]),
                lane[:8],
            )
    for p in range(4):
        py, px = p // 2, p % 2
        north = wide[1, 2 * py + 1 - px]
        east = wide[0, 2 * (1 - py) + px]
        zonal = col_shift(north, neighbour(1, px)) - col_shift(north, neighbour(-1, px))
        meridional = row_shift(east, neighbour(1, py)) - row_shift(east, neighbour(-1, py))
        source[p] = (operator[9, p] + zonal - meridional) * operator[8, p]
        field[p] = operator[10, p]
    for colour in COLOURS:
        py, px = colour // 2, colour % 2
        value = source[colour]
        for k, (dy, dx) in enumerate(STEPS):
            plane = 2 * (py ^ (dy & 1)) + (px ^ (dx & 1))
            v = field[plane]
            if dy:
                v = row_shift(v, neighbour(dy, py))
            if dx:
                v = col_shift(v, neighbour(dx, px))
            value = value + operator[k, colour] * v
        field[colour] = value
    lane = iota((ROWS, 128), 1)
    even_lane = lane % 2 == 0
    first = lane // 2
    for py in range(2):
        for h in range(2):
            even = field[2 * py, 0:ROWS, 128 * h : 128 * h + 128]
            odd = field[2 * py + 1, 0:ROWS, 128 * h : 128 * h + 128]
            for b in range(2):
                for t in range(ROWS // 8):
                    index = first[:8] + 64 * b
                    e = lane_gather(even[8 * t : 8 * t + 8], index)
                    o = lane_gather(odd[8 * t : 8 * t + 8], index)
                    natural[2 * h + b, pl.ds(16 * t + py, 8, stride=2), :] = jnp.where(even_lane[:8], e, o)
    for k in range(4):
        out[:, 128 * k : 128 * k + 128] = natural[k]


def sweep(*arrays):
    return pl.pallas_call(
        sweep_kernel,
        out_shape=jax.ShapeDtypeStruct((128, 512), F32),
        scratch_shapes=[
            pltpu.VMEM((2, 4, XROWS, XCOLS), F32),
            pltpu.VMEM((4, XROWS, XCOLS), F32),
            pltpu.VMEM((4, XROWS, XCOLS), F32),
            pltpu.VMEM((4, 128, 128), F32),
        ],
        compiler_params=params(),
        cost_estimate=cost(10**8, 6 * MIB),
        name="sweep",
    )(*arrays)


AXES = ("zon", "mer")


def exchange(values):
    return lax.all_to_all(values, AXES, split_axis=0, concat_axis=0, tiled=True)


def from_neighbour(values, dz, dm):
    nz, nm = lax.axis_size("zon"), lax.axis_size("mer")
    pairs = [
        (((z + dz) % nz) * nm + m + dm, z * nm + m)
        for z in range(nz)
        for m in range(nm)
        if 0 <= m + dm < nm
    ]
    return lax.ppermute(values, AXES, pairs)


def surround(left_edge, right_edge, ends, left_corner, right_corner):
    return (
        from_neighbour(left_edge, 1, 0),
        from_neighbour(right_edge, -1, 0),
        from_neighbour(ends, 0, 1),
        from_neighbour(ends, 0, -1),
        from_neighbour(left_corner, 1, 1),
        from_neighbour(right_corner, -1, 1),
        from_neighbour(left_corner, 1, -1),
        from_neighbour(right_corner, -1, -1),
    )


def local(
    sea_level,
    forcing,
    link_weights,
    excess,
    ocean_mask,
    current,
    intersection_block,
    intersection_cols,
    ice_mass,
    coriolis,
    ice_start,
    wind_stress,
):
    blocks = intersection_block[0]
    cols = intersection_cols[0]
    slots = blocks.size
    row, part = blocks >> 2, blocks & 3
    fetch_key = jnp.where(blocks >= 0, part * 128 + row, -1).reshape(slots, 1)
    scatter_key = jnp.where(blocks >= 0, part * 128 + (row & 1) * 64 + (row >> 1), -1).reshape(1, slots)

    ice_current = exchange(fetch(current, fetch_key, cols))
    planes, *edges = prepare(sea_level, forcing, link_weights, excess, ocean_mask)
    operator = extend(planes, *surround(*edges))
    inverse, hot = invert(cols, scatter_key)
    velocity, drag = ice(ice_mass[0], coriolis[0], ice_start[:, 0], wind_stress[:, 0], ice_current)
    stress, side, ends, corner = scatter(exchange(drag), inverse, hot)
    surface = sweep(operator, stress, *surround(side, side, ends, corner, corner))
    return surface, velocity[:, None]


def solution(mesh):
    return jax.shard_map(
        local,
        mesh=mesh,
        in_specs=(
            P("mer", "zon"),
            P("mer", "zon"),
            P(None, "mer", "zon"),
            P("mer", "zon"),
            P("mer", "zon"),
            P(None, "mer", "zon"),
            P(("zon", "mer"), None, None),
            P(("zon", "mer"), None, None, None),
            P(("zon", "mer"), None, None, None),
            P(("zon", "mer"), None, None, None),
            P(None, ("zon", "mer"), None, None, None),
            P(None, ("zon", "mer"), None, None, None),
        ),
        out_specs=(P("mer", "zon"), P(None, ("zon", "mer"), None, None, None)),
        check_vma=False,
    )
```

time: 1450 us -> 170 us (0.12)
  other arithmetic: 751 us -> 0.69 us
  local copies, waits for them, and re-layouts: 602 us -> 10.7 us
  Pallas kernels: 0 us -> 47.3 us
  blocking collectives: 0 us -> 30.6 us
  waiting for transfers between devices: 39.1 us -> 18.3 us
    scatter-add x1 -> x0, other arithmetic: 707 us -> none  [local(): jnp.zeros((2, cell_count), jnp.float32).at[:, flat_target]]
    gather x2 -> x0, local copies, waits for them, and re-layouts: 476 us -> none  [local(): jnp.take(flat_current, jnp.minimum(flat_target, cell_count - 1), axis=1)]
    slice x7 -> x0, local copies, waits for them, and re-layouts: 48.7 us -> none  [the longest x1 34.7 us: local(): cycle_north = padded_2(stress_grid[1], (('zon', 1),), 1, True)]
    pallas_call x0 -> x7, Pallas kernels: none -> 47.3 us  [the longest x1 16.8 us: invert(): pl.pallas_call(invert_kernel, out_shape=(jax.ShapeDtypeStruct((count, 8,...]
    ppermute x8 -> x16, starting transfers between devices: 20.4 us -> 55.5 us  [from_neighbour(): return lax.ppermute(values, AXES, pairs)]
    another operation x2 -> x0, local copies, waits for them, and re-layouts: 33 us -> none  [local(): returned = to_ocean(ice_drag)[:, 0].reshape(2, slot_count * block)]
    all_to_all x2 -> x1, waiting for transfers between devices: 32.8 us -> 0.01 us  [exchange(): return lax.all_to_all(values, AXES, split_axis=0, concat_axis=0, tiled=True)]
    all_to_all x0 -> x1, blocking collectives: none -> 30.6 us  [exchange(): return lax.all_to_all(values, AXES, split_axis=0, concat_axis=0, tiled=True)]
  transfers between devices with their start and end apart: 10 -> 17, of which waited for: 5 -> 5; matrix products, arithmetic and copies ran while one was open for 2% -> 0% of each run, Pallas kernels for 0% -> 19%
where the time goes in v1:
time: 170 us
  starting transfers between devices  60.9 us (36%)
  Pallas kernels  47.3 us (28%)
  blocking collectives  30.6 us (18%)
  waiting for transfers between devices  18.3 us (11%)
  local copies, waits for them, and re-layouts  10.7 us (6%)
    ppermute x16, starting transfers between devices, from_neighbour(): return lax.ppermute(values, AXES, pairs)  55.5 us
    all_to_all x1, blocking collectives, exchange(): return lax.all_to_all(values, AXES, split_axis=0, concat_axis=0, tiled=True)  30.6 us
    ppermute x16, waiting for transfers between devices, from_neighbour(): return lax.ppermute(values, AXES, pairs)  18.3 us
    pallas_call x1, Pallas kernels, invert(): pl.pallas_call(invert_kernel, out_shape=(jax.ShapeDtypeStruct((count, 8,...  16.8 us
    unnamed x38, local copies, waits for them, and re-layouts  10.3 us
    pallas_call x1, Pallas kernels, ice(): pl.pallas_call(ice_kernel, grid=(count // step,), in_specs=[one, one, two...  8.82 us
    pallas_call x1, Pallas kernels, prepare(): pl.pallas_call(prepare_kernel, out_shape=(jax.ShapeDtypeStruct((ARRAYS, 4...  7.12 us
    all_to_all x1, starting transfers between devices, exchange(): return lax.all_to_all(values, AXES, split_axis=0, concat_axis=0, tiled=True)  5.39 us
  transfers between devices with their start and end apart: 17, of which 5 were waited for; matrix products, arithmetic and copies ran while one was open for 0% of the time, Pallas kernels for 19%

profile of v1, /device:TPU:1, one launch (start us, length us, event | category | flops | bytes accessed | tf_op | source)
XLA Modules:
  0.0 169.6 jit_solution(9362452622168757697)
XLA Ops:
  3.7 2.8 %fetch.1 = f32[128,2,8,128]{3,2,1,0:T(8,128)S(1)} custom-call(f32[2,128,512]{2,1,0:T(8,128)S(1)} %copy-done.11, s32[1024,1]{1,0:T(8,128)S(1)} %select_n.28.key, s32[128,8,128]{2,1,0:T(8,128)S(1)} %bitcast.12), custom_call_target="tpu_custom_call" | custom-call | flops 1000000000 | bytes 2097152 | tf_op jit(solution)/shard_map/fetch/pallas_call | solution.py:72
  6.5 30.6 %all_to_all.10.current_ref = f32[128,2,8,128]{3,2,1,0:T(8,128)S(1)} all-to-all(f32[128,2,8,128]{3,2,1,0:T(8,128)S(1)} %fetch.1), channel_id=1, replica_groups=mesh['zon'=32,'mer'=4] {'zon','mer'}, dimensions={0} | all-to-all | bytes 2097152 | tf_op jit(solution)/shard_map/all_to_all | solution.py:434
  37.2 8.8 %ice.1 = (f32[2,128,8,128]{3,2,1,0:T(8,128)}, f32[128,2,8,128]{3,2,1,0:T(8,128)}) custom-call(f32[128,8,128]{2,1,0:T(8,128)S(1)} %bitcast.10, f32[128,8,128]{2,1,0:T(8,128)S(1)} %bitcast.11, f32[2,128,8,128]{3,2,1,0:T(8,128)S(1)} %bitcast.8, f32[2,128,8,128]{3,2,1,0:T(8,128)S(1)} %bitcast.9, f32[128,2,8,128]{3,2,1,0:T(8,128)S(1)} %all_to_all.10.current_ref), custom_call_target="tpu_custom_call" | custom-call | flops 10000000 | bytes 6291456 | tf_op jit(solution)/shard_map/ice/pallas_call | solution.py:155
  46.0 5.4 %all-to-all-start.1 = ((f32[128,2,8,128]{3,2,1,0:T(8,128)}), f32[128,2,8,128]{3,2,1,0:T(8,128)}, u32[]{:S(2)}, u32[]{:S(2)}) async-start(f32[128,2,8,128]{3,2,1,0:T(8,128)} %get-tuple-element.22), calls=%async_computation.1 | async-start | bytes 2097152 | tf_op jit(solution)/shard_map/all_to_all | solution.py:434
  51.5 7.1 %prepare.1 = (f32[11,4,64,256]{3,2,1,0:T(8,128)}, f32[2,64,256]{2,1,0:T(8,128)}, f32[2,64,256]{2,1,0:T(8,128)S(1)}, f32[11,4,8,256]{3,2,1,0:T(8,128)}, f32[2,8,256]{2,1,0:T(8,128)}, /*index=5*/f32[2,8,256]{2,1,0:T(8,128)}) custom-call(f32[128,512]{1,0:T(8,128)S(1)} %copy-done.7, f32[128,512]{1,0:T(8,128)S(1)} %copy-done.8, f32[8,128,512]{2,1,0:T(8,128)S(1)} %copy-done.2, ...), custom_call_target="tpu_custom_call" | custom-call | flops 10000000 | bytes 7340032 | tf_op jit(solution)/shard_map/prepare/pallas_call | solution.py:292
  59.3 10.3 %collective-permute-start.4 = (f32[2,8,256]{2,1,0:T(8,128)}, f32[2,8,256]{2,1,0:T(8,128)S(1)}, u32[]{:S(2)}, u32[]{:S(2)}) collective-permute-start(f32[2,8,256]{2,1,0:T(8,128)} %get-tuple-element.20), channel_id=1, source_target_pairs={{5,0},{6,1},{7,2},{9,4},{10,5},{11,6},{13,8},{14,9},{15,10},{17,12... | collective-permute-start | bytes 49160 | tf_op jit(solution)/shard_map/ppermute | solution.py:445
  69.5 1.9 %collective-permute-start.5 = (f32[2,8,256]{2,1,0:T(8,128)}, f32[2,8,256]{2,1,0:T(8,128)S(1)}, u32[]{:S(2)}, u32[]{:S(2)}) collective-permute-start(f32[2,8,256]{2,1,0:T(8,128)} %get-tuple-element.21), channel_id=1, source_target_pairs={{125,0},{126,1},{127,2},{1,4},{2,5},{3,6},{5,8},{6,9},{7,10},{9,12... | collective-permute-start | bytes 49160 | tf_op jit(solution)/shard_map/ppermute | solution.py:445
  71.5 1.9 %collective-permute-start.2 = (f32[11,4,8,256]{3,2,1,0:T(8,128)}, f32[11,4,8,256]{3,2,1,0:T(8,128)S(1)}, u32[]{:S(2)}, u32[]{:S(2)}) collective-permute-start(f32[11,4,8,256]{3,2,1,0:T(8,128)} %get-tuple-element.19), channel_id=1, source_target_pairs={{1,0},{2,1},{3,2},{5,4},{6,5},{7,6},{9,8},{10,9},{11,10},{13,12},{... | collective-permute-start | bytes 1081352 | tf_op jit(solution)/shard_map/ppermute | solution.py:445
  73.4 3.6 %collective-permute-start.3 = (f32[11,4,8,256]{3,2,1,0:T(8,128)}, f32[11,4,8,256]{3,2,1,0:T(8,128)}, u32[]{:S(2)}, u32[]{:S(2)}) collective-permute-start(f32[11,4,8,256]{3,2,1,0:T(8,128)} %get-tuple-element.19), channel_id=1, source_target_pairs={{0,1},{1,2},{2,3},{4,5},{5,6},{6,7},{8,9},{9,10},{10,11},{12,13},{... | collective-permute-start | bytes 1081352 | tf_op jit(solution)/shard_map/ppermute | solution.py:445
  77.1 7.9 %collective-permute-start.6 = (f32[2,8,256]{2,1,0:T(8,128)}, f32[2,8,256]{2,1,0:T(8,128)S(1)}, u32[]{:S(2)}, u32[]{:S(2)}) collective-permute-start(f32[2,8,256]{2,1,0:T(8,128)} %get-tuple-element.20), channel_id=1, source_target_pairs={{4,1},{5,2},{6,3},{8,5},{9,6},{10,7},{12,9},{13,10},{14,11},{16,13... | collective-permute-start | bytes 49160 | tf_op jit(solution)/shard_map/ppermute | solution.py:445
  87.7 16.8 %invert.1 = (s32[128,8,128]{2,1,0:T(8,128)S(1)}, bf16[512,1024]{1,0:T(8,128)(2,1)S(1)}) custom-call(s32[128,8,128]{2,1,0:T(8,128)S(1)} %bitcast.13, s32[1,1024]{1,0:T(1,128)S(1)} %reshape.120.key), custom_call_target="tpu_custom_call" | custom-call | flops 10000000000 | bytes 2097152 | tf_op jit(solution)/shard_map/invert/pallas_call | solution.py:107
  106.3 2.2 %collective-permute-start.7 = (f32[2,8,256]{2,1,0:T(8,128)}, f32[2,8,256]{2,1,0:T(8,128)}, u32[]{:S(2)}, u32[]{:S(2)}) collective-permute-start(f32[2,8,256]{2,1,0:T(8,128)} %get-tuple-element.21), channel_id=1, source_target_pairs={{124,1},{125,2},{126,3},{0,5},{1,6},{2,7},{4,9},{5,10},{6,11},{8,1... | collective-permute-start | bytes 49160 | tf_op jit(solution)/shard_map/ppermute | solution.py:445
  110.8 4.3 %scatter.1 = (f32[2,4,64,256]{3,2,1,0:T(8,128)S(1)}, f32[64,128]{1,0:T(8,128)S(1)}, f32[2,4,8,256]{3,2,1,0:T(8,128)S(1)}, f32[8,128]{1,0:T(8,128)S(1)}) custom-call(f32[128,2,8,128]{3,2,1,0:T(8,128)} %all-to-all-done.1.drag, s32[128,8,128]{2,1,0:T(8,128)S(1)} %copy-done.18, bf16[512,1024]{1,0:T(8,128)(2,1)S(1)} %copy-done.16), custom_call_target="tpu_custom_call" | custom-call | flops 1000000000 | bytes 3145728 | tf_op jit(solution)/shard_map/scatter/pallas_call | solution.py:218
  115.1 2.6 %collective-permute-done.7.above_left = f32[2,8,256]{2,1,0:T(8,128)} collective-permute-done((f32[2,8,256]{2,1,0:T(8,128)}, f32[2,8,256]{2,1,0:T(8,128)}, u32[]{:S(2)}, u32[]{:S(2)}) %collective-permute-start.7) | collective-permute-done | bytes 16416 | tf_op jit(solution)/shard_map/ppermute | solution.py:445
  119.6 3.6 %collective-permute-start.11 = (f32[2,4,8,256]{3,2,1,0:T(8,128)S(1)}, f32[2,4,8,256]{3,2,1,0:T(8,128)S(1)}, u32[]{:S(2)}, u32[]{:S(2)}) collective-permute-start(f32[2,4,8,256]{3,2,1,0:T(8,128)S(1)} %get-tuple-element.27), channel_id=1, source_target_pairs={{0,1},{1,2},{2,3},{4,5},{5,6},{6,7},{8,9},{9,10},{10,11},{12,13},{... | collective-permute-start | bytes 196616 | tf_op jit(solution)/shard_map/ppermute | solution.py:445
  123.3 3.9 %collective-permute-start.8 = (f32[64,128]{1,0:T(8,128)S(1)}, f32[64,128]{1,0:T(8,128)S(1)}, u32[]{:S(2)}, u32[]{:S(2)}) collective-permute-start(f32[64,128]{1,0:T(8,128)S(1)} %get-tuple-element.26), channel_id=1, source_target_pairs={{4,0},{5,1},{6,2},{7,3},{8,4},{9,5},{10,6},{11,7},{12,8},{13,9},{1... | collective-permute-start | bytes 98312 | tf_op jit(solution)/shard_map/ppermute | solution.py:445
  127.2 10.0 %collective-permute-start.12 = (f32[8,128]{1,0:T(8,128)S(1)}, f32[8,128]{1,0:T(8,128)S(1)}, u32[]{:S(2)}, u32[]{:S(2)}) collective-permute-start(f32[8,128]{1,0:T(8,128)S(1)} %get-tuple-element.28), channel_id=1, source_target_pairs={{5,0},{6,1},{7,2},{9,4},{10,5},{11,6},{13,8},{14,9},{15,10},{17,12... | collective-permute-start | bytes 12296 | tf_op jit(solution)/shard_map/ppermute | solution.py:445
  139.9 8.4 %collective-permute-done.13.below_left = f32[8,128]{1,0:T(8,128)S(1)} collective-permute-done((f32[8,128]{1,0:T(8,128)S(1)}, f32[8,128]{1,0:T(8,128)S(1)}, u32[]{:S(2)}, u32[]{:S(2)}) %collective-permute-start.13) | collective-permute-done | bytes 4128 | tf_op jit(solution)/shard_map/ppermute | solution.py:445
  148.3 2.9 %collective-permute-start.14 = (f32[8,128]{1,0:T(8,128)S(1)}, f32[8,128]{1,0:T(8,128)S(1)}, u32[]{:S(2)}, u32[]{:S(2)}) collective-permute-start(f32[8,128]{1,0:T(8,128)S(1)} %get-tuple-element.28), channel_id=1, source_target_pairs={{4,1},{5,2},{6,3},{8,5},{9,6},{10,7},{12,9},{13,10},{14,11},{16,13... | collective-permute-start | bytes 12296 | tf_op jit(solution)/shard_map/ppermute | solution.py:445
  151.2 2.0 %collective-permute-done.14.above_right = f32[8,128]{1,0:T(8,128)S(1)} collective-permute-done((f32[8,128]{1,0:T(8,128)S(1)}, f32[8,128]{1,0:T(8,128)S(1)}, u32[]{:S(2)}, u32[]{:S(2)}) %collective-permute-start.14) | collective-permute-done | bytes 4128 | tf_op jit(solution)/shard_map/ppermute | solution.py:445
  155.2 4.2 %extend.1.operator = f32[11,4,72,384]{3,2,1,0:T(8,128)} custom-call(f32[11,4,64,256]{3,2,1,0:T(8,128)S(1)} %copy-done.1, f32[2,64,256]{2,1,0:T(8,128)S(1)} %collective-permute-done.right, f32[2,64,256]{2,1,0:T(8,128)S(1)} %collective-permute-done.1.left, f32[11,4,8,256]{3,2,1,0:T(8,128)S(1)} %collective-permute-done.2.below, ...), custom_call_target="tpu_custom_call" | custom-call | flops 10000000 | bytes 8388608 | tf_op jit(solution)/shard_map/extend/pallas_call | solution.py:336
  159.3 4.5 %collective-permute-done.15.above_left = f32[8,128]{1,0:T(8,128)S(1)} collective-permute-done((f32[8,128]{1,0:T(8,128)S(1)}, f32[8,128]{1,0:T(8,128)S(1)}, u32[]{:S(2)}, u32[]{:S(2)}) %collective-permute-start.15) | collective-permute-done | bytes 4128 | tf_op jit(solution)/shard_map/ppermute | solution.py:445
  163.9 2.4 %copy-done = f32[11,4,72,384]{3,2,1,0:T(8,128)S(1)} copy-done((f32[11,4,72,384]{3,2,1,0:T(8,128)S(1)}, f32[11,4,72,384]{3,2,1,0:T(8,128)}, u32[]{:S(2)}) %copy-start) | copy-done | bytes 4866072
  166.3 3.4 %sweep.1 = f32[128,512]{1,0:T(8,128)} custom-call(f32[11,4,72,384]{3,2,1,0:T(8,128)S(1)} %copy-done, f32[2,4,64,256]{3,2,1,0:T(8,128)S(1)} %get-tuple-element.25.stress, f32[64,128]{1,0:T(8,128)S(1)} %collective-permute-done.8.right, f32[64,128]{1,0:T(8,128)S(1)} %collective-permute-done.9.left, f32[2,4,8,256]{3,2,1,0:T(8,128)S(1)} %collective-permute-done.10.below, ...), custom_call_target="tpu_custom_call" | custom-call | flops 100000000 | bytes 6291456 | tf_op jit(solution)/shard_map/sweep/pallas_call | solution.py:415
  (61 shorter events, 17.1 us)
Async XLA Ops:
  3.7 33.4 %copy-start.3 = (f32[2,1,128,8,128]{4,3,2,1,0:T(8,128)S(1)}, f32[2,1,128,8,128]{4,3,2,1,0:T(8,128)}, u32[]{:S(2)}) copy-start(f32[2,1,128,8,128]{4,3,2,1,0:T(8,128)} %param.22) | copy-start | bytes 3145732
  3.7 33.4 %copy-start.4 = (f32[2,1,128,8,128]{4,3,2,1,0:T(8,128)S(1)}, f32[2,1,128,8,128]{4,3,2,1,0:T(8,128)}, u32[]{:S(2)}) copy-start(f32[2,1,128,8,128]{4,3,2,1,0:T(8,128)} %param.23) | copy-start | bytes 3145732
  3.7 33.4 %copy-start.5 = (f32[1,128,8,128]{3,2,1,0:T(8,128)S(1)}, f32[1,128,8,128]{3,2,1,0:T(8,128)}, u32[]{:S(2)}) copy-start(f32[1,128,8,128]{3,2,1,0:T(8,128)} %param.20) | copy-start | bytes 1572868
  3.7 33.4 %copy-start.6 = (f32[1,128,8,128]{3,2,1,0:T(8,128)S(1)}, f32[1,128,8,128]{3,2,1,0:T(8,128)}, u32[]{:S(2)}) copy-start(f32[1,128,8,128]{3,2,1,0:T(8,128)} %param.21) | copy-start | bytes 1572868
  37.2 14.3 %copy-start.2 = (f32[8,128,512]{2,1,0:T(8,128)S(1)}, f32[8,128,512]{2,1,0:T(8,128)}, u32[]{:S(2)}) copy-start(f32[8,128,512]{2,1,0:T(8,128)} %weights.1) | copy-start | bytes 6291460
  37.2 14.3 %copy-start.7 = (f32[128,512]{1,0:T(8,128)S(1)}, f32[128,512]{1,0:T(8,128)}, u32[]{:S(2)}) copy-start(f32[128,512]{1,0:T(8,128)} %sea.1) | copy-start | bytes 786436
  46.0 62.5 %all-to-all-start.1 = ((f32[128,2,8,128]{3,2,1,0:T(8,128)}), f32[128,2,8,128]{3,2,1,0:T(8,128)}, u32[]{:S(2)}, u32[]{:S(2)}) async-start(f32[128,2,8,128]{3,2,1,0:T(8,128)} %get-tuple-element.22), calls=%async_computation.1 | async-start | bytes 2097152 | tf_op jit(solution)/shard_map/all_to_all | solution.py:434
  59.3 25.9 %collective-permute-start.4 = (f32[2,8,256]{2,1,0:T(8,128)}, f32[2,8,256]{2,1,0:T(8,128)S(1)}, u32[]{:S(2)}, u32[]{:S(2)}) collective-permute-start(f32[2,8,256]{2,1,0:T(8,128)} %get-tuple-element.20), channel_id=1, source_target_pairs={{5,0},{6,1},{7,2},{9,4},{10,5},{11,6},{13,8},{14,9},{15,10},{17,12... | collective-permute-start | bytes 49160 | tf_op jit(solution)/shard_map/ppermute | solution.py:445
  69.5 16.3 %collective-permute-start.5 = (f32[2,8,256]{2,1,0:T(8,128)}, f32[2,8,256]{2,1,0:T(8,128)S(1)}, u32[]{:S(2)}, u32[]{:S(2)}) collective-permute-start(f32[2,8,256]{2,1,0:T(8,128)} %get-tuple-element.21), channel_id=1, source_target_pairs={{125,0},{126,1},{127,2},{1,4},{2,5},{3,6},{5,8},{6,9},{7,10},{9,12... | collective-permute-start | bytes 49160 | tf_op jit(solution)/shard_map/ppermute | solution.py:445
  71.5 55.7 %collective-permute-start.2 = (f32[11,4,8,256]{3,2,1,0:T(8,128)}, f32[11,4,8,256]{3,2,1,0:T(8,128)S(1)}, u32[]{:S(2)}, u32[]{:S(2)}) collective-permute-start(f32[11,4,8,256]{3,2,1,0:T(8,128)} %get-tuple-element.19), channel_id=1, source_target_pairs={{1,0},{2,1},{3,2},{5,4},{6,5},{7,6},{9,8},{10,9},{11,10},{13,12},{... | collective-permute-start | bytes 1081352 | tf_op jit(solution)/shard_map/ppermute | solution.py:445
  73.4 53.8 %collective-permute-start.3 = (f32[11,4,8,256]{3,2,1,0:T(8,128)}, f32[11,4,8,256]{3,2,1,0:T(8,128)}, u32[]{:S(2)}, u32[]{:S(2)}) collective-permute-start(f32[11,4,8,256]{3,2,1,0:T(8,128)} %get-tuple-element.19), channel_id=1, source_target_pairs={{0,1},{1,2},{2,3},{4,5},{5,6},{6,7},{8,9},{9,10},{10,11},{12,13},{... | collective-permute-start | bytes 1081352 | tf_op jit(solution)/shard_map/ppermute | solution.py:445
  77.1 29.3 %collective-permute-start.6 = (f32[2,8,256]{2,1,0:T(8,128)}, f32[2,8,256]{2,1,0:T(8,128)S(1)}, u32[]{:S(2)}, u32[]{:S(2)}) collective-permute-start(f32[2,8,256]{2,1,0:T(8,128)} %get-tuple-element.20), channel_id=1, source_target_pairs={{4,1},{5,2},{6,3},{8,5},{9,6},{10,7},{12,9},{13,10},{14,11},{16,13... | collective-permute-start | bytes 49160 | tf_op jit(solution)/shard_map/ppermute | solution.py:445
  85.1 34.5 %collective-permute-start = (f32[2,64,256]{2,1,0:T(8,128)}, f32[2,64,256]{2,1,0:T(8,128)S(1)}, u32[]{:S(2)}, u32[]{:S(2)}) collective-permute-start(f32[2,64,256]{2,1,0:T(8,128)} %get-tuple-element.17), channel_id=1, source_target_pairs={{4,0},{5,1},{6,2},{7,3},{8,4},{9,5},{10,6},{11,7},{12,8},{13,9},{1... | collective-permute-start | bytes 393224 | tf_op jit(solution)/shard_map/ppermute | solution.py:445
  85.9 37.4 %collective-permute-start.1 = (f32[2,64,256]{2,1,0:T(8,128)}, f32[2,64,256]{2,1,0:T(8,128)S(1)}, u32[]{:S(2)}, u32[]{:S(2)}) collective-permute-start(f32[2,64,256]{2,1,0:T(8,128)} %copy-done.14), channel_id=1, source_target_pairs={{124,0},{125,1},{126,2},{127,3},{0,4},{1,5},{2,6},{3,7},{4,8},{5,9... | collective-permute-start | bytes 393224 | tf_op jit(solution)/shard_map/ppermute | solution.py:445
  106.3 48.8 %copy-start.1 = (f32[11,4,64,256]{3,2,1,0:T(8,128)S(1)}, f32[11,4,64,256]{3,2,1,0:T(8,128)}, u32[]{:S(2)}) copy-start(f32[11,4,64,256]{3,2,1,0:T(8,128)} %get-tuple-element.16.planes) | copy-start | bytes 8650756
  106.3 11.3 %collective-permute-start.7 = (f32[2,8,256]{2,1,0:T(8,128)}, f32[2,8,256]{2,1,0:T(8,128)}, u32[]{:S(2)}, u32[]{:S(2)}) collective-permute-start(f32[2,8,256]{2,1,0:T(8,128)} %get-tuple-element.21), channel_id=1, source_target_pairs={{124,1},{125,2},{126,3},{0,5},{1,6},{2,7},{4,9},{5,10},{6,11},{8,1... | collective-permute-start | bytes 49160 | tf_op jit(solution)/shard_map/ppermute | solution.py:445
  117.7 46.2 %collective-permute-start.10 = (f32[2,4,8,256]{3,2,1,0:T(8,128)S(1)}, f32[2,4,8,256]{3,2,1,0:T(8,128)S(1)}, u32[]{:S(2)}, u32[]{:S(2)}) collective-permute-start(f32[2,4,8,256]{3,2,1,0:T(8,128)S(1)} %get-tuple-element.27), channel_id=1, source_target_pairs={{1,0},{2,1},{3,2},{5,4},{6,5},{7,6},{9,8},{10,9},{11,10},{13,12},{... | collective-permute-start | bytes 196616 | tf_op jit(solution)/shard_map/ppermute | solution.py:445
  119.6 44.3 %collective-permute-start.11 = (f32[2,4,8,256]{3,2,1,0:T(8,128)S(1)}, f32[2,4,8,256]{3,2,1,0:T(8,128)S(1)}, u32[]{:S(2)}, u32[]{:S(2)}) collective-permute-start(f32[2,4,8,256]{3,2,1,0:T(8,128)S(1)} %get-tuple-element.27), channel_id=1, source_target_pairs={{0,1},{1,2},{2,3},{4,5},{5,6},{6,7},{8,9},{9,10},{10,11},{12,13},{... | collective-permute-start | bytes 196616 | tf_op jit(solution)/shard_map/ppermute | solution.py:445
  123.3 40.6 %collective-permute-start.8 = (f32[64,128]{1,0:T(8,128)S(1)}, f32[64,128]{1,0:T(8,128)S(1)}, u32[]{:S(2)}, u32[]{:S(2)}) collective-permute-start(f32[64,128]{1,0:T(8,128)S(1)} %get-tuple-element.26), channel_id=1, source_target_pairs={{4,0},{5,1},{6,2},{7,3},{8,4},{9,5},{10,6},{11,7},{12,8},{13,9},{1... | collective-permute-start | bytes 98312 | tf_op jit(solution)/shard_map/ppermute | solution.py:445
  127.2 36.7 %collective-permute-start.9 = (f32[64,128]{1,0:T(8,128)S(1)}, f32[64,128]{1,0:T(8,128)S(1)}, u32[]{:S(2)}, u32[]{:S(2)}) collective-permute-start(f32[64,128]{1,0:T(8,128)S(1)} %get-tuple-element.26), channel_id=1, source_target_pairs={{124,0},{125,1},{126,2},{127,3},{0,4},{1,5},{2,6},{3,7},{4,8},{5,9... | collective-permute-start | bytes 98312 | tf_op jit(solution)/shard_map/ppermute | solution.py:445
  127.2 10.8 %collective-permute-start.12 = (f32[8,128]{1,0:T(8,128)S(1)}, f32[8,128]{1,0:T(8,128)S(1)}, u32[]{:S(2)}, u32[]{:S(2)}) collective-permute-start(f32[8,128]{1,0:T(8,128)S(1)} %get-tuple-element.28), channel_id=1, source_target_pairs={{5,0},{6,1},{7,2},{9,4},{10,5},{11,6},{13,8},{14,9},{15,10},{17,12... | collective-permute-start | bytes 12296 | tf_op jit(solution)/shard_map/ppermute | solution.py:445
  138.0 10.3 %collective-permute-start.13 = (f32[8,128]{1,0:T(8,128)S(1)}, f32[8,128]{1,0:T(8,128)S(1)}, u32[]{:S(2)}, u32[]{:S(2)}) collective-permute-start(f32[8,128]{1,0:T(8,128)S(1)} %get-tuple-element.28), channel_id=1, source_target_pairs={{125,0},{126,1},{127,2},{1,4},{2,5},{3,6},{5,8},{6,9},{7,10},{9,12... | collective-permute-start | bytes 12296 | tf_op jit(solution)/shard_map/ppermute | solution.py:445
  148.3 4.9 %collective-permute-start.14 = (f32[8,128]{1,0:T(8,128)S(1)}, f32[8,128]{1,0:T(8,128)S(1)}, u32[]{:S(2)}, u32[]{:S(2)}) collective-permute-start(f32[8,128]{1,0:T(8,128)S(1)} %get-tuple-element.28), channel_id=1, source_target_pairs={{4,1},{5,2},{6,3},{8,5},{9,6},{10,7},{12,9},{13,10},{14,11},{16,13... | collective-permute-start | bytes 12296 | tf_op jit(solution)/shard_map/ppermute | solution.py:445
  153.2 10.6 %collective-permute-start.15 = (f32[8,128]{1,0:T(8,128)S(1)}, f32[8,128]{1,0:T(8,128)S(1)}, u32[]{:S(2)}, u32[]{:S(2)}) collective-permute-start(f32[8,128]{1,0:T(8,128)S(1)} %get-tuple-element.28), channel_id=1, source_target_pairs={{124,1},{125,2},{126,3},{0,5},{1,6},{2,7},{4,9},{5,10},{6,11},{8,1... | collective-permute-start | bytes 12296 | tf_op jit(solution)/shard_map/ppermute | solution.py:445
  (12 other events, 53.1 us)

commit v2 on v1

v2 whole, which is shorter than its diff:
```python
import jax
import jax.numpy as jnp
from jax import lax
from jax.experimental import pallas as pl
from jax.experimental.pallas import tpu as pltpu
from jax.sharding import PartitionSpec as P

SWEEPS = 2
ICE_SWEEPS = 3
DRAG = 1.0
LINK = 0.5
STEPS = ((0, 1), (0, -1), (1, 0), (-1, 0), (1, 1), (1, -1), (-1, 1), (-1, -1))
COLOURS = (0,) + (1, 2, 3, 2, 1, 0) * SWEEPS
F32, BF16, I32 = jnp.float32, jnp.bfloat16, jnp.int32
MIB = 1 << 20
ROWS, COLS, XROWS, XCOLS = 64, 256, 72, 384


def params(vmem=48):
    return pltpu.CompilerParams(vmem_limit_bytes=vmem * MIB)


def cost(flops, moved):
    return pl.CostEstimate(flops=flops, bytes_accessed=moved, transcendentals=0)


def iota(shape, dim):
    return lax.broadcasted_iota(I32, shape, dim)


def lane_gather(values, index):
    return jnp.take_along_axis(values, index, axis=1, mode="promise_in_bounds")


def split3(values):
    high = values.astype(BF16)
    rest = values - high.astype(F32)
    middle = rest.astype(BF16)
    low = (rest - middle.astype(F32)).astype(BF16)
    return high, middle, low


def dot(a, b):
    return jnp.dot(a, b, preferred_element_type=F32)


def beside(values, lane):
    before = jnp.where(lane == 0, 0.0, pltpu.roll(values, 1, 1))
    after = jnp.where(lane == 127, 0.0, pltpu.roll(values, 127, 1))
    return LINK * (before + after)


def turn(a, t, east, north):
    return a * east + t * north, a * north - t * east


def sweep_ice(a, t, east, north, base_east, base_north, lane):
    return turn(a, t, base_east + beside(east, lane), base_north + beside(north, lane))


def respond(a, t, current_east, current_north, lane):
    east, north = turn(a, t, current_east, current_north)
    for _ in range(ICE_SWEEPS - 1):
        east, north = sweep_ice(a, t, east, north, current_east, current_north, lane)
    return east, north


GROUP = 8


def send_kernel(current, key, cols, mass_ref, coriolis_ref, start_ref, wind_ref, out, table, rows):
    count = cols.shape[0]

    @pl.when(pl.program_id(0) == 0)
    def _():
        for c in range(2):
            for k in range(4):
                parts = split3(current[c, :, 128 * k : 128 * k + 128])
                for part in range(3):
                    table[part, 128 * k : 128 * k + 128, 128 * c : 128 * c + 128] = parts[part]

    hot = jnp.where(key[...] == iota((8 * count, 512), 1), 1.0, 0.0).astype(BF16)
    rows[...] = dot(hot, table[0]) + dot(hot, table[1]) + dot(hot, table[2])
    tall = 8 * GROUP
    lane = iota((tall, 128), 1)

    def body(g, carry):
        group = pl.ds(GROUP * g, GROUP)
        tile = rows[pl.ds(pl.multiple_of(tall * g, tall), tall)]
        index = cols[group].reshape(tall, 128)
        inside = jnp.maximum(index, 0)
        for c in range(2):
            got = jnp.concatenate(
                [lane_gather(tile[8 * i : 8 * i + 8, 128 * c : 128 * c + 128], inside[8 * i : 8 * i + 8]) for i in range(GROUP)],
                axis=0,
            )
            out[group, 4 + c] = jnp.where(index >= 0, DRAG * got, 0.0).reshape(GROUP, 8, 128)
        mass = mass_ref[group].reshape(tall, 128)
        a = mass + DRAG + 2.0 * LINK
        t = coriolis_ref[group].reshape(tall, 128) * mass
        inverse = 1.0 / (a * a + t * t)
        a = a * inverse
        t = t * inverse
        east = start_ref[0, group].reshape(tall, 128)
        north = start_ref[1, group].reshape(tall, 128)
        base_east = mass * east + wind_ref[0, group].reshape(tall, 128)
        base_north = mass * north + wind_ref[1, group].reshape(tall, 128)
        for _ in range(ICE_SWEEPS):
            east, north = sweep_ice(a, t, east, north, base_east, base_north, lane)
        for n, value in enumerate((east, north, a, t)):
            out[group, n] = value.reshape(GROUP, 8, 128)
        return carry

    lax.fori_loop(0, count // GROUP, body, 0)


def chunked(count):
    step = min(count, 32)
    one = pl.BlockSpec((step, 8, 128), lambda i: (i, 0, 0))
    two = pl.BlockSpec((2, step, 8, 128), lambda i: (0, i, 0, 0))
    response = pl.BlockSpec((step, 4, 8, 128), lambda i: (i, 0, 0, 0))
    current = pl.BlockSpec((step, 2, 8, 128), lambda i: (i, 2, 0, 0))
    return step, count // step, one, two, response, current


def send(current, key, cols, mass, coriolis, start, wind):
    count = cols.shape[0]
    step, grid, one, two, _, _ = chunked(count)
    return pl.pallas_call(
        send_kernel,
        grid=(grid,),
        in_specs=[
            pl.BlockSpec((2, 128, 512), lambda i: (0, 0, 0)),
            pl.BlockSpec((8 * step, 1), lambda i: (i, 0)),
            one,
            one,
            one,
            two,
            two,
        ],
        out_specs=pl.BlockSpec((step, 6, 8, 128), lambda i: (i, 0, 0, 0)),
        out_shape=jax.ShapeDtypeStruct((count, 6, 8, 128), F32),
        scratch_shapes=[pltpu.VMEM((3, 512, 256), BF16), pltpu.VMEM((8 * step, 256), F32)],
        compiler_params=params(16),
        cost_estimate=cost(10**9, 8 * MIB),
        name="send",
    )(current, key, cols, mass, coriolis, start, wind)


def velocity_kernel(response, current_ref, out):
    tall = 8 * GROUP
    lane = iota((tall, 128), 1)

    def body(g, carry):
        group = pl.ds(GROUP * g, GROUP)
        base_east, base_north, a, t = (response[group, n].reshape(tall, 128) for n in range(4))
        current = [current_ref[group, c].reshape(tall, 128) for c in range(2)]
        east, north = respond(a, t, *current, lane)
        out[0, group] = (base_east + east).reshape(GROUP, 8, 128)
        out[1, group] = (base_north + north).reshape(GROUP, 8, 128)
        return carry

    lax.fori_loop(0, response.shape[0] // GROUP, body, 0)


def velocities(sent, received):
    count = sent.shape[0]
    _, grid, _, two, response, current = chunked(count)
    return pl.pallas_call(
        velocity_kernel,
        grid=(grid,),
        in_specs=[response, current],
        out_specs=two,
        out_shape=jax.ShapeDtypeStruct((2, count, 8, 128), F32),
        compiler_params=params(16),
        cost_estimate=cost(10**7, 4 * MIB),
        name="velocities",
    )(sent, received)


def invert_kernel(cols, key, inverse, hot):
    count = cols.shape[0]
    hot[...] = jnp.where(iota((512, 8 * count), 0) == key[...], 1.0, 0.0).astype(BF16)
    lane = iota((8, 1024), 1)
    weights = jnp.where(lane // 128 == iota((8, 1024), 0), lane % 128 + 1, 0).astype(F32).astype(BF16)
    place = iota((128, 128), 0)

    def body(i, carry):
        index = cols[i]
        target = jnp.where(index >= 0, (index >> 1) + 64 * (index & 1), -1)
        masks = [
            jnp.where(place == jnp.broadcast_to(target[s : s + 1], (128, 128)), 1.0, 0.0).astype(BF16)
            for s in range(8)
        ]
        found = lax.dot_general(
            weights, jnp.concatenate(masks, axis=1), (((1,), (1,)), ((), ())), preferred_element_type=F32
        )
        inverse[i] = found.astype(I32) - 1
        return carry

    lax.fori_loop(0, count, body, 0, unroll=2)


def invert(cols, key):
    count = cols.shape[0]
    return pl.pallas_call(
        invert_kernel,
        out_shape=(jax.ShapeDtypeStruct((count, 8, 128), I32), jax.ShapeDtypeStruct((512, 8 * count), BF16)),
        compiler_params=params(16),
        cost_estimate=cost(10**10, 2 * MIB),
        name="invert",
    )(cols, key)


def stress_kernel(response, current_ref, inverse, hot, planes, side, ends, parts):
    count = inverse.shape[0]
    tall = 8 * GROUP
    lane = iota((tall, 128), 1)
    chunk = pl.program_id(0)

    def body(g, carry):
        group = pl.ds(GROUP * g, GROUP)
        rows = pl.ds(pl.multiple_of(8 * count * chunk + tall * g, tall), tall)
        base_east, base_north, a, t = (response[group, n].reshape(tall, 128) for n in range(4))
        current = [current_ref[group, c].reshape(tall, 128) for c in range(2)]
        east, north = respond(a, t, *current, lane)
        index = inverse[group].reshape(tall, 128)
        inside = jnp.maximum(index, 0)
        for c, drag in enumerate((base_east + east - current[0], base_north + north - current[1])):
            drag = DRAG * drag
            got = jnp.concatenate(
                [lane_gather(drag[8 * i : 8 * i + 8], inside[8 * i : 8 * i + 8]) for i in range(GROUP)], axis=0
            )
            pieces = split3(jnp.where(index >= 0, got, 0.0))
            for part in range(3):
                parts[part, rows, 128 * c : 128 * c + 128] = pieces[part]
        return carry

    lax.fori_loop(0, count // GROUP, body, 0)

    @pl.when(chunk == pl.num_programs(0) - 1)
    def _():
        total = dot(hot[...], parts[0]) + dot(hot[...], parts[1]) + dot(hot[...], parts[2])
        lane = iota((ROWS, 128), 1)
        low = lane < 64
        top = iota((8, 128), 0) < 4
        edge = jnp.zeros((ROWS, 128), F32)
        for c in range(2):
            for py in range(2):
                for h in range(2):
                    first = 256 * h + 64 * py
                    a = total[first : first + 64, 128 * c : 128 * c + 128]
                    b = total[first + 128 : first + 192, 128 * c : 128 * c + 128]
                    even = jnp.where(low, a, pltpu.roll(b, 64, 1))
                    odd = jnp.where(low, pltpu.roll(a, 64, 1), b)
                    for px, value in ((0, even), (1, odd)):
                        plane = 2 * py + px
                        planes[c, plane, :, 128 * h : 128 * h + 128] = value
                        ends[c, plane, :, 128 * h : 128 * h + 128] = jnp.where(top, value[:8], value[56:])
                        item = 4 * c + plane
                        if h == 0:
                            moved = pltpu.roll(value, 8 * item, 1) if item else value
                            edge = jnp.where(lane // 8 == item, moved, edge)
                        else:
                            moved = pltpu.roll(value, (64 + 8 * item + 8) % 128, 1) if item != 7 else value
                            edge = jnp.where(lane // 8 == 8 + item, moved, edge)
        side[...] = edge


def stresses(sent, received, inverse, hot):
    count = inverse.shape[0]
    step, grid, one, _, response, current = chunked(count)

    def whole(shape):
        return pl.BlockSpec(shape, lambda i: (0,) * len(shape))

    shapes = ((2, 4, ROWS, COLS), (ROWS, 128), (2, 4, 8, COLS))
    return pl.pallas_call(
        stress_kernel,
        grid=(grid,),
        in_specs=[response, current, one, whole((512, 8 * count))],
        out_specs=tuple(whole(shape) for shape in shapes),
        out_shape=tuple(jax.ShapeDtypeStruct(shape, F32) for shape in shapes),
        scratch_shapes=[pltpu.VMEM((3, 8 * count, 256), BF16)],
        compiler_params=params(16),
        cost_estimate=cost(10**9, 4 * MIB),
        name="stresses",
    )(received, sent, inverse, hot)


def widen_kernel(ends, right, left, out):
    lane = iota((8, 128), 1)
    top = iota((8, 128), 0) < 4
    from_right = jnp.where(top, right[0:8], right[56:64])
    from_left = jnp.where(top, left[0:8], left[56:64])
    for c in range(2):
        for p in range(4):
            item = 4 * c + p
            r = pltpu.roll(from_right, (128 - 8 * item) % 128, 1) if item else from_right
            s = pltpu.roll(from_left, (56 - 8 * item) % 128, 1) if item != 7 else from_left
            out[c, p, :, 0:COLS] = ends[c, p]
            out[c, p, :, COLS:XCOLS] = jnp.where(lane < 64, r, s)


def widen(ends, right, left):
    return pl.pallas_call(
        widen_kernel,
        out_shape=jax.ShapeDtypeStruct((2, 4, 8, XCOLS), F32),
        compiler_params=params(4),
        cost_estimate=cost(10**5, MIB // 4),
        name="widen",
    )(ends, right, left)


ARRAYS = 11


def prepare_kernel(
    sea, forcing, weights, excess, mask, planes, left, right, ends, halves
):
    lane = iota((8, 128), 1)
    low = lane < 64
    order = jnp.where(low, 2 * lane, 2 * lane - 127)
    swapped = jnp.where(low, 2 * lane + 1, 2 * lane - 128)

    def split(t, carry):
        rows = pl.ds(pl.multiple_of(8 * t, 8), 8)
        w = [weights[k, rows, :] for k in range(8)]
        total = ((w[0] + w[1]) + (w[2] + w[3])) + ((w[4] + w[5]) + (w[6] + w[7]))
        ocean = mask[rows, :] > 0
        inverse = jnp.where(ocean, 1.0 / ((1.0 + excess[rows, :]) * total), 0.0)
        arrays = [v * inverse for v in w]
        arrays += [inverse, forcing[rows, :], jnp.where(ocean, sea[rows, :], 0.0)]
        for n, array in enumerate(arrays):
            for h in range(2):
                a = lane_gather(array[:, 256 * h : 256 * h + 128], order)
                b = lane_gather(array[:, 256 * h + 128 : 256 * h + 256], swapped)
                halves[4 * n + h, rows, :] = jnp.where(low, a, b)
                halves[4 * n + 2 + h, rows, :] = pltpu.roll(jnp.where(low, b, a), 64, 1)
        return carry

    lax.fori_loop(0, 2 * ROWS // 8, split, 0)

    def pack(t, carry):
        out_rows = pl.ds(pl.multiple_of(8 * t, 8), 8)
        for py in range(2):
            rows = pl.ds(16 * t + py, 8, stride=2)
            packed = [[jnp.zeros((8, 128), F32)] * 2, [jnp.zeros((8, 128), F32)] * 2]
            for n in range(ARRAYS):
                for px in range(2):
                    for h in range(2):
                        value = halves[4 * n + 2 * px + h, rows, :]
                        planes[n, 2 * py + px, out_rows, 128 * h : 128 * h + 128] = value
                        item = 2 * n + px
                        shift = (8 * (item % 16) + (8 if h else 0)) % 128
                        moved = pltpu.roll(value, shift, 1) if shift else value
                        packed[h][item // 16] = jnp.where(lane // 8 == item % 16, moved, packed[h][item // 16])
            for g in range(2):
                left[py, out_rows, 128 * g : 128 * g + 128] = packed[0][g]
                right[py, out_rows, 128 * g : 128 * g + 128] = packed[1][g]
        return carry

    lax.fori_loop(0, ROWS // 8, pack, 0)
    top = iota((8, 256), 0) < 4
    for n in range(ARRAYS):
        for p in range(4):
            ends[n, p] = jnp.where(top, planes[n, p, 0:8], planes[n, p, 56:64])


def prepare(sea, forcing, weights, excess, mask):
    return pl.pallas_call(
        prepare_kernel,
        out_shape=(
            jax.ShapeDtypeStruct((ARRAYS, 4, ROWS, COLS), F32),
            jax.ShapeDtypeStruct((2, ROWS, 256), F32),
            jax.ShapeDtypeStruct((2, ROWS, 256), F32),
            jax.ShapeDtypeStruct((ARRAYS, 4, 8, COLS), F32),
        ),
        scratch_shapes=[pltpu.VMEM((4 * ARRAYS, 2 * ROWS, 128), F32)],
        compiler_params=params(20),
        cost_estimate=cost(10**7, 7 * MIB),
        name="prepare",
    )(sea, forcing, weights, excess, mask)


def place_edges(n, p, right, left, rows, lane):
    item = 2 * n + p % 2
    span = slice(128 * (item // 16), 128 * (item // 16) + 128)
    slot = item % 16
    r, s = right[p // 2, rows, span], left[p // 2, rows, span]
    r = pltpu.roll(r, (128 - 8 * slot) % 128, 1) if slot else r
    s = pltpu.roll(s, (120 - 8 * slot) % 128, 1) if slot != 15 else s
    return jnp.where(lane < 8, r, jnp.where(lane >= 120, s, 0.0))


def widen_operator_kernel(ends, right, left, out):
    lane = iota((8, 128), 1)
    top = iota((8, 128), 0) < 4
    for n in range(ARRAYS):
        for p in range(4):
            out[n, p, :, 0:COLS] = ends[n, p]
            out[n, p, :, COLS:XCOLS] = jnp.where(
                top,
                place_edges(n, p, right, left, slice(0, 8), lane),
                place_edges(n, p, right, left, slice(56, 64), lane),
            )


def widen_operator(ends, right, left):
    return pl.pallas_call(
        widen_operator_kernel,
        out_shape=jax.ShapeDtypeStruct((ARRAYS, 4, 8, XCOLS), F32),
        compiler_params=params(8),
        cost_estimate=cost(10**6, 2 * MIB),
        name="widen_operator",
    )(ends, right, left)


def extend_kernel(planes, right, left, below, above, out):
    lane = iota((ROWS, 128), 1)
    top = iota((8, XCOLS), 0) < 4
    for n in range(ARRAYS):
        for p in range(4):
            out[n, p, 0:ROWS, 0:COLS] = planes[n, p]
            out[n, p, 0:ROWS, COLS:XCOLS] = place_edges(n, p, right, left, slice(0, ROWS), lane)
            out[n, p, ROWS:XROWS, :] = jnp.where(top, below[n, p], above[n, p])


def extend(*arrays):
    return pl.pallas_call(
        extend_kernel,
        out_shape=jax.ShapeDtypeStruct((ARRAYS, 4, XROWS, XCOLS), F32),
        compiler_params=params(20),
        cost_estimate=cost(10**7, 8 * MIB),
        name="extend",
    )(*arrays)


def row_shift(value, step):
    return pltpu.roll(value, (-step) % XROWS, 0) if step else value


def col_shift(value, step):
    return pltpu.roll(value, (-step) % XCOLS, 1) if step else value


def neighbour(step, parity):
    return (step + parity) // 2


def sweep_kernel(operator, stress, right, left, below, above, out, wide, source, field, natural):
    lane = iota((ROWS, 128), 1)
    top = iota((8, XCOLS), 0) < 4
    for c in range(2):
        for p in range(4):
            item = 4 * c + p
            r = pltpu.roll(right[...], (128 - 8 * item) % 128, 1) if item else right[...]
            s = pltpu.roll(left[...], (56 - 8 * item) % 128, 1) if item != 7 else left[...]
            wide[c, p, 0:ROWS, 0:COLS] = stress[c, p]
            wide[c, p, 0:ROWS, COLS:XCOLS] = jnp.where(lane < 64, r, s)
            wide[c, p, ROWS:XROWS, :] = jnp.where(top, below[c, p], above[c, p])
    for p in range(4):
        py, px = p // 2, p % 2
        north = wide[1, 2 * py + 1 - px]
        east = wide[0, 2 * (1 - py) + px]
        zonal = col_shift(north, neighbour(1, px)) - col_shift(north, neighbour(-1, px))
        meridional = row_shift(east, neighbour(1, py)) - row_shift(east, neighbour(-1, py))
        source[p] = (operator[9, p] + zonal - meridional) * operator[8, p]
        field[p] = operator[10, p]
    for colour in COLOURS:
        py, px = colour // 2, colour % 2
        value = source[colour]
        for k, (dy, dx) in enumerate(STEPS):
            plane = 2 * (py ^ (dy & 1)) + (px ^ (dx & 1))
            v = field[plane]
            if dy:
                v = row_shift(v, neighbour(dy, py))
            if dx:
                v = col_shift(v, neighbour(dx, px))
            value = value + operator[k, colour] * v
        field[colour] = value
    lane = iota((ROWS, 128), 1)
    even_lane = lane % 2 == 0
    first = lane // 2
    for py in range(2):
        for h in range(2):
            even = field[2 * py, 0:ROWS, 128 * h : 128 * h + 128]
            odd = field[2 * py + 1, 0:ROWS, 128 * h : 128 * h + 128]
            for b in range(2):
                for t in range(ROWS // 8):
                    index = first[:8] + 64 * b
                    e = lane_gather(even[8 * t : 8 * t + 8], index)
                    o = lane_gather(odd[8 * t : 8 * t + 8], index)
                    natural[2 * h + b, pl.ds(16 * t + py, 8, stride=2), :] = jnp.where(even_lane[:8], e, o)
    for k in range(4):
        out[:, 128 * k : 128 * k + 128] = natural[k]


def sweep(*arrays):
    return pl.pallas_call(
        sweep_kernel,
        out_shape=jax.ShapeDtypeStruct((128, 512), F32),
        scratch_shapes=[
            pltpu.VMEM((2, 4, XROWS, XCOLS), F32),
            pltpu.VMEM((4, XROWS, XCOLS), F32),
            pltpu.VMEM((4, XROWS, XCOLS), F32),
            pltpu.VMEM((4, 128, 128), F32),
        ],
        compiler_params=params(20),
        cost_estimate=cost(10**8, 6 * MIB),
        name="sweep",
    )(*arrays)


AXES = ("zon", "mer")


def exchange(values):
    return lax.all_to_all(values, AXES, split_axis=0, concat_axis=0, tiled=True)


def from_neighbour(values, dz, dm):
    nz, nm = lax.axis_size("zon"), lax.axis_size("mer")
    pairs = [
        (((z + dz) % nz) * nm + m + dm, z * nm + m)
        for z in range(nz)
        for m in range(nm)
        if 0 <= m + dm < nm
    ]
    return lax.ppermute(values, AXES, pairs)


def local(
    sea_level,
    forcing,
    link_weights,
    excess,
    ocean_mask,
    current,
    intersection_block,
    intersection_cols,
    ice_mass,
    coriolis,
    ice_start,
    wind_stress,
):
    blocks = intersection_block[0]
    cols = intersection_cols[0]
    slots = blocks.size
    row, part = blocks >> 2, blocks & 3
    fetch_key = jnp.where(blocks >= 0, part * 128 + row, -1).reshape(slots, 1)
    scatter_key = jnp.where(blocks >= 0, part * 128 + (row & 1) * 64 + (row >> 1), -1).reshape(1, slots)

    sent = send(current, fetch_key, cols, ice_mass[0], coriolis[0], ice_start[:, 0], wind_stress[:, 0])
    received = exchange(sent)
    planes, left_edge, right_edge, ends = prepare(sea_level, forcing, link_weights, excess, ocean_mask)
    right, left = from_neighbour(left_edge, 1, 0), from_neighbour(right_edge, -1, 0)
    rows = widen_operator(ends, right, left)
    operator = extend(planes, right, left, from_neighbour(rows, 0, 1), from_neighbour(rows, 0, -1))
    inverse, hot = invert(cols, scatter_key)
    inverse, operator = lax.optimization_barrier((inverse, operator))
    stress, side, ends = stresses(sent, received, inverse, hot)
    received, side = lax.optimization_barrier((received, side))
    right, left = from_neighbour(side, 1, 0), from_neighbour(side, -1, 0)
    rows = widen(ends, right, left)
    surface = sweep(operator, stress, right, left, from_neighbour(rows, 0, 1), from_neighbour(rows, 0, -1))
    velocity = velocities(sent, received)
    return surface, velocity[:, None]


def solution(mesh):
    return jax.shard_map(
        local,
        mesh=mesh,
        in_specs=(
            P("mer", "zon"),
            P("mer", "zon"),
            P(None, "mer", "zon"),
            P("mer", "zon"),
            P("mer", "zon"),
            P(None, "mer", "zon"),
            P(("zon", "mer"), None, None),
            P(("zon", "mer"), None, None, None),
            P(("zon", "mer"), None, None, None),
            P(("zon", "mer"), None, None, None),
            P(None, ("zon", "mer"), None, None, None),
            P(None, ("zon", "mer"), None, None, None),
        ),
        out_specs=(P("mer", "zon"), P(None, ("zon", "mer"), None, None, None)),
        check_vma=False,
    )
```

time: 170 us -> 138 us (0.81)
  blocking collectives: 30.6 us -> 0 us
  starting transfers between devices: 60.9 us -> 32.7 us
  local copies, waits for them, and re-layouts: 10.7 us -> 23.6 us
  waiting for transfers between devices: 18.3 us -> 30.2 us
    ppermute x16 -> x8, starting transfers between devices: 55.5 us -> 21.2 us  [from_neighbour(): return lax.ppermute(values, AXES, pairs)]
    all_to_all x1 -> x0, blocking collectives: 30.6 us -> none  [exchange(): return lax.all_to_all(values, AXES, split_axis=0, concat_axis=0, tiled=True)]
    ppermute x16 -> x8, waiting for transfers between devices: 18.3 us -> 30.2 us  [from_neighbour(): return lax.ppermute(values, AXES, pairs)]
    unnamed x38 -> x44, local copies, waits for them, and re-layouts: 10.3 us -> 21.6 us
    all_to_all x1, starting transfers between devices: 5.39 us -> 11.5 us  [exchange(): return lax.all_to_all(values, AXES, split_axis=0, concat_axis=0, tiled=True)]
    pallas_call x3 -> x5, Pallas kernels: 15.9 us -> 21.5 us  [the longest x1 8.22 us: send(): pl.pallas_call(send_kernel, grid=(grid,), in_specs=[pl.BlockSpec((2, 128,...]
    pallas_call x1, Pallas kernels: 4.17 us -> 0.87 us  [extend(): pl.pallas_call(extend_kernel, out_shape=jax.ShapeDtypeStruct((ARRAYS, 4,...]
  transfers between devices with their start and end apart: 17 -> 9, of which waited for: 5 -> 4; matrix products, arithmetic and copies ran while one was open for 0% -> 1% of each run, Pallas kernels for 19% -> 22%
where the time goes in v2:
time: 138 us; the launch traced here: 137 us
  Pallas kernels  48.6 us (35%)
  starting transfers between devices  32.7 us (24%)
  waiting for transfers between devices  30.2 us (22%)
  local copies, waits for them, and re-layouts  23.6 us (17%)
    ppermute x8, waiting for transfers between devices, from_neighbour(): return lax.ppermute(values, AXES, pairs)  30.2 us
    unnamed x44, local copies, waits for them, and re-layouts  21.6 us
    ppermute x8, starting transfers between devices, from_neighbour(): return lax.ppermute(values, AXES, pairs)  21.2 us
    pallas_call x1, Pallas kernels, invert(): pl.pallas_call(invert_kernel, out_shape=(jax.ShapeDtypeStruct((count, 8,...  16.8 us
    all_to_all x1, starting transfers between devices, exchange(): return lax.all_to_all(values, AXES, split_axis=0, concat_axis=0, tiled=True)  11.5 us
    pallas_call x1, Pallas kernels, send(): pl.pallas_call(send_kernel, grid=(grid,), in_specs=[pl.BlockSpec((2, 128,...  8.22 us
    pallas_call x1, Pallas kernels, stresses(): pl.pallas_call(stress_kernel, grid=(grid,), in_specs=[response, current,...  7.45 us
    pallas_call x1, Pallas kernels, prepare(): pl.pallas_call(prepare_kernel, out_shape=(jax.ShapeDtypeStruct((ARRAYS, 4...  6.05 us
  transfers between devices with their start and end apart: 9, of which 4 were waited for; matrix products, arithmetic and copies ran while one was open for 1% of the time, Pallas kernels for 22%

profile of v2, /device:TPU:1, one launch (start us, length us, event | category | flops | bytes accessed | tf_op | source)
XLA Modules:
  0.0 136.5 jit_solution(1210671421390957446)
XLA Ops:
  1.6 1.2 copy-done.5
  2.8 1.2 copy-done.6
  4.1 1.0 copy-done.9
  6.2 1.0 copy-done.11
  8.2 8.2 %send.1.current_ref.response = f32[128,6,8,128]{3,2,1,0:T(8,128)} custom-call(f32[2,128,512]{2,1,0:T(8,128)S(1)} %copy-done.9, s32[1024,1]{1,0:T(8,128)S(1)} %select_n.28.key, s32[128,8,128]{2,1,0:T(8,128)S(1)} %bitcast.12, f32[128,8,128]{2,1,0:T(8,128)S(1)} %bitcast.10, f32[128,8,128]{2,1,0:T(8,128)S(1)} %bitcast.11, f32[2,128,8,128]{3,2,1,0:T(8,128)S(1)} %bitcast.8, ...), custom_call_target="tpu_custom_call" | custom-call | flops 1000000000 | bytes 8388608 | tf_op jit(solution)/shard_map/send/pallas_call | solution.py:129
  16.5 11.5 %all-to-all-start = ((f32[128,6,8,128]{3,2,1,0:T(8,128)}), f32[128,6,8,128]{3,2,1,0:T(8,128)S(1)}, u32[]{:S(2)}, u32[]{:S(2)}) async-start(f32[128,6,8,128]{3,2,1,0:T(8,128)} %send.1.current_ref.response), calls=%async_computation | async-start | bytes 6291456 | tf_op jit(solution)/shard_map/all_to_all | solution.py:519
  28.0 1.6 %copy-done.4 = f32[8,128,512]{2,1,0:T(8,128)S(1)} copy-done((f32[8,128,512]{2,1,0:T(8,128)S(1)}, f32[8,128,512]{2,1,0:T(8,128)}, u32[]{:S(2)}) %copy-start.4) | copy-done | bytes 2097176
  32.4 6.1 %prepare.1 = (f32[11,4,64,256]{3,2,1,0:T(8,128)S(1)}, f32[2,64,256]{2,1,0:T(8,128)}, f32[2,64,256]{2,1,0:T(8,128)S(1)}, f32[11,4,8,256]{3,2,1,0:T(8,128)S(1)}) custom-call(f32[128,512]{1,0:T(8,128)S(1)} %copy-done.18, f32[128,512]{1,0:T(8,128)S(1)} %copy-done.19, f32[8,128,512]{2,1,0:T(8,128)S(1)} %copy-done.4, f32[128,512]{1,0:T(8,128)S(1)} %copy-done.20, ...), custom_call_target="tpu_custom_call" | custom-call | flops 10000000 | bytes 7340032 | tf_op jit(solution)/shard_map/prepare/pallas_call | solution.py:371
  38.5 1.6 %copy-done.2 = f32[11,4,64,256]{3,2,1,0:T(8,128)} copy-done((f32[11,4,64,256]{3,2,1,0:T(8,128)}, f32[11,4,64,256]{3,2,1,0:T(8,128)S(1)}, u32[]{:S(2)}) %copy-start.2) | copy-done | bytes 2883608
  40.8 8.0 %collective-permute-start = (f32[2,64,256]{2,1,0:T(8,128)}, f32[2,64,256]{2,1,0:T(8,128)S(1)}, u32[]{:S(2)}, u32[]{:S(2)}) collective-permute-start(f32[2,64,256]{2,1,0:T(8,128)} %get-tuple-element.17), channel_id=1, source_target_pairs={{4,0},{5,1},{6,2},{7,3},{8,4},{9,5},{10,6},{11,7},{12,8},{13,9},{1... | collective-permute-start | bytes 393224 | tf_op jit(solution)/shard_map/ppermute | solution.py:530
  50.4 15.8 %collective-permute-done.right = f32[2,64,256]{2,1,0:T(8,128)S(1)} collective-permute-done((f32[2,64,256]{2,1,0:T(8,128)}, f32[2,64,256]{2,1,0:T(8,128)S(1)}, u32[]{:S(2)}, u32[]{:S(2)}) %collective-permute-start) | collective-permute-done | bytes 131104 | tf_op jit(solution)/shard_map/ppermute | solution.py:530
  66.2 6.4 %collective-permute-done.1.left = f32[2,64,256]{2,1,0:T(8,128)S(1)} collective-permute-done((f32[2,64,256]{2,1,0:T(8,128)S(1)}, f32[2,64,256]{2,1,0:T(8,128)S(1)}, u32[]{:S(2)}, u32[]{:S(2)}) %collective-permute-start.1) | collective-permute-done | bytes 131104 | tf_op jit(solution)/shard_map/ppermute | solution.py:530
  73.8 3.0 %collective-permute-start.2 = (f32[11,4,8,384]{3,2,1,0:T(8,128)S(1)}, f32[11,4,8,384]{3,2,1,0:T(8,128)S(1)}, u32[]{:S(2)}, u32[]{:S(2)}) collective-permute-start(f32[11,4,8,384]{3,2,1,0:T(8,128)S(1)} %widen_operator.1), channel_id=1, source_target_pairs={{1,0},{2,1},{3,2},{5,4},{6,5},{7,6},{9,8},{10,9},{11,10},{13,12},{... | collective-permute-start | bytes 1622024 | tf_op jit(solution)/shard_map/ppermute | solution.py:530
  76.9 2.8 %collective-permute-start.3 = (f32[11,4,8,384]{3,2,1,0:T(8,128)S(1)}, f32[11,4,8,384]{3,2,1,0:T(8,128)S(1)}, u32[]{:S(2)}, u32[]{:S(2)}) collective-permute-start(f32[11,4,8,384]{3,2,1,0:T(8,128)S(1)} %widen_operator.1), channel_id=1, source_target_pairs={{0,1},{1,2},{2,3},{4,5},{5,6},{6,7},{8,9},{9,10},{10,11},{12,13},{... | collective-permute-start | bytes 1622024 | tf_op jit(solution)/shard_map/ppermute | solution.py:530
  80.7 16.8 %invert.1 = (s32[128,8,128]{2,1,0:T(8,128)S(1)}, bf16[512,1024]{1,0:T(8,128)(2,1)S(1)}) custom-call(s32[128,8,128]{2,1,0:T(8,128)S(1)} %bitcast.13, s32[1,1024]{1,0:T(1,128)S(1)} %reshape.120.key), custom_call_target="tpu_custom_call" | custom-call | flops 10000000000 | bytes 2097152 | tf_op jit(solution)/shard_map/invert/pallas_call | solution.py:206
  100.2 2.2 %copy-done = f32[11,4,72,384]{3,2,1,0:T(8,128)} copy-done((f32[11,4,72,384]{3,2,1,0:T(8,128)}, f32[11,4,72,384]{3,2,1,0:T(8,128)S(1)}, u32[]{:S(2)}) %copy-start) | copy-done | bytes 4866072
  102.4 1.2 copy-done.8
  104.7 7.4 %stresses.1 = (f32[2,4,64,256]{3,2,1,0:T(8,128)S(1)}, f32[64,128]{1,0:T(8,128)S(1)}, f32[2,4,8,256]{3,2,1,0:T(8,128)S(1)}) custom-call(f32[128,6,8,128]{3,2,1,0:T(8,128)S(1)} %all-to-all-done.response.current_ref, f32[128,6,8,128]{3,2,1,0:T(8,128)} %send.1.current_ref.response, s32[128,8,128]{2,1,0:T(8,128)S(1)} %copy-done.15, bf16[512,1024]{1,0:T(8,128)(2,1)S(1)} %copy-done.8), custom_call_target="tpu_custom_call" | custom-call | flops 1000000000 | bytes 4194304 | tf_op jit(solution)/shard_map/stresses/pallas_call | solution.py:278
  113.7 1.8 %collective-permute-done.4.right = f32[64,128]{1,0:T(8,128)S(1)} collective-permute-done((f32[64,128]{1,0:T(8,128)S(1)}, f32[64,128]{1,0:T(8,128)S(1)}, u32[]{:S(2)}, u32[]{:S(2)}) %collective-permute-start.4) | collective-permute-done | bytes 32800 | tf_op jit(solution)/shard_map/ppermute | solution.py:530
  115.5 6.2 %collective-permute-done.5.left = f32[64,128]{1,0:T(8,128)S(1)} collective-permute-done((f32[64,128]{1,0:T(8,128)S(1)}, f32[64,128]{1,0:T(8,128)S(1)}, u32[]{:S(2)}, u32[]{:S(2)}) %collective-permute-start.5) | collective-permute-done | bytes 32800 | tf_op jit(solution)/shard_map/ppermute | solution.py:530
  121.8 2.9 %collective-permute-start.6 = (f32[2,4,8,384]{3,2,1,0:T(8,128)S(1)}, f32[2,4,8,384]{3,2,1,0:T(8,128)S(1)}, u32[]{:S(2)}, u32[]{:S(2)}) collective-permute-start(f32[2,4,8,384]{3,2,1,0:T(8,128)S(1)} %widen.1), channel_id=1, source_target_pairs={{1,0},{2,1},{3,2},{5,4},{6,5},{7,6},{9,8},{10,9},{11,10},{13,12},{... | collective-permute-start | bytes 294920 | tf_op jit(solution)/shard_map/ppermute | solution.py:530
  124.7 2.9 %collective-permute-start.7 = (f32[2,4,8,384]{3,2,1,0:T(8,128)S(1)}, f32[2,4,8,384]{3,2,1,0:T(8,128)S(1)}, u32[]{:S(2)}, u32[]{:S(2)}) collective-permute-start(f32[2,4,8,384]{3,2,1,0:T(8,128)S(1)} %widen.1), channel_id=1, source_target_pairs={{0,1},{1,2},{2,3},{4,5},{5,6},{6,7},{8,9},{9,10},{10,11},{12,13},{... | collective-permute-start | bytes 294920 | tf_op jit(solution)/shard_map/ppermute | solution.py:530
  127.6 5.5 %velocities.1 = f32[2,128,8,128]{3,2,1,0:T(8,128)} custom-call(f32[128,6,8,128]{3,2,1,0:T(8,128)} %send.1.current_ref.response, f32[128,6,8,128]{3,2,1,0:T(8,128)S(1)} %all-to-all-done.response.current_ref), custom_call_target="tpu_custom_call" | custom-call | flops 10000000 | bytes 4194304 | tf_op jit(solution)/shard_map/velocities/pallas_call | solution.py:169
  133.2 3.4 %sweep.1 = f32[128,512]{1,0:T(8,128)} custom-call(f32[11,4,72,384]{3,2,1,0:T(8,128)S(1)} %copy-done.1, f32[2,4,64,256]{3,2,1,0:T(8,128)S(1)} %get-tuple-element.23.stress, f32[64,128]{1,0:T(8,128)S(1)} %collective-permute-done.4.right, f32[64,128]{1,0:T(8,128)S(1)} %collective-permute-done.5.left, f32[2,4,8,384]{3,2,1,0:T(8,128)S(1)} %collective-permute-done.6.below, ...), custom_call_target="tpu_custom_call" | custom-call | flops 100000000 | bytes 6291456 | tf_op jit(solution)/shard_map/sweep/pallas_call | solution.py:500
  (52 shorter events, 15.9 us)
Async XLA Ops:
  1.6 1.2 copy-start.5
  2.8 1.2 copy-start.6
  4.1 1.0 copy-start.9
  5.1 1.0 copy-start.10
  6.2 1.0 copy-start.11
  7.2 1.0 copy-start.12
  16.5 11.5 %copy-start.18 = (f32[128,512]{1,0:T(8,128)S(1)}, f32[128,512]{1,0:T(8,128)}, u32[]{:S(2)}) copy-start(f32[128,512]{1,0:T(8,128)} %sea.1) | copy-start | bytes 786436
  16.5 86.0 %all-to-all-start = ((f32[128,6,8,128]{3,2,1,0:T(8,128)}), f32[128,6,8,128]{3,2,1,0:T(8,128)S(1)}, u32[]{:S(2)}, u32[]{:S(2)}) async-start(f32[128,6,8,128]{3,2,1,0:T(8,128)} %send.1.current_ref.response), calls=%async_computation | async-start | bytes 6291456 | tf_op jit(solution)/shard_map/all_to_all | solution.py:519
  28.0 1.6 %copy-start.4 = (f32[8,128,512]{2,1,0:T(8,128)S(1)}, f32[8,128,512]{2,1,0:T(8,128)}, u32[]{:S(2)}) copy-start(f32[8,128,512]{2,1,0:T(8,128)} %weights.1) | copy-start | bytes 6291460
  38.5 1.6 %copy-start.2 = (f32[11,4,64,256]{3,2,1,0:T(8,128)}, f32[11,4,64,256]{3,2,1,0:T(8,128)S(1)}, u32[]{:S(2)}) copy-start(f32[11,4,64,256]{3,2,1,0:T(8,128)S(1)} %get-tuple-element.16.planes) | copy-start | bytes 8650756
  40.8 25.4 %collective-permute-start = (f32[2,64,256]{2,1,0:T(8,128)}, f32[2,64,256]{2,1,0:T(8,128)S(1)}, u32[]{:S(2)}, u32[]{:S(2)}) collective-permute-start(f32[2,64,256]{2,1,0:T(8,128)} %get-tuple-element.17), channel_id=1, source_target_pairs={{4,0},{5,1},{6,2},{7,3},{8,4},{9,5},{10,6},{11,7},{12,8},{13,9},{1... | collective-permute-start | bytes 393224 | tf_op jit(solution)/shard_map/ppermute | solution.py:530
  48.8 23.8 %collective-permute-start.1 = (f32[2,64,256]{2,1,0:T(8,128)S(1)}, f32[2,64,256]{2,1,0:T(8,128)S(1)}, u32[]{:S(2)}, u32[]{:S(2)}) collective-permute-start(f32[2,64,256]{2,1,0:T(8,128)S(1)} %get-tuple-element.18), channel_id=1, source_target_pairs={{124,0},{125,1},{126,2},{127,3},{0,4},{1,5},{2,6},{3,7},{4,8},{5,9... | collective-permute-start | bytes 393224 | tf_op jit(solution)/shard_map/ppermute | solution.py:530
  73.8 25.5 %copy-start.3 = (f32[11,4,64,256]{3,2,1,0:T(8,128)S(1)}, f32[11,4,64,256]{3,2,1,0:T(8,128)}, u32[]{:S(2)}) copy-start(f32[11,4,64,256]{3,2,1,0:T(8,128)} %copy-done.2) | copy-start | bytes 8650756
  73.8 25.5 %collective-permute-start.2 = (f32[11,4,8,384]{3,2,1,0:T(8,128)S(1)}, f32[11,4,8,384]{3,2,1,0:T(8,128)S(1)}, u32[]{:S(2)}, u32[]{:S(2)}) collective-permute-start(f32[11,4,8,384]{3,2,1,0:T(8,128)S(1)} %widen_operator.1), channel_id=1, source_target_pairs={{1,0},{2,1},{3,2},{5,4},{6,5},{7,6},{9,8},{10,9},{11,10},{13,12},{... | collective-permute-start | bytes 1622024 | tf_op jit(solution)/shard_map/ppermute | solution.py:530
  76.9 22.5 %collective-permute-start.3 = (f32[11,4,8,384]{3,2,1,0:T(8,128)S(1)}, f32[11,4,8,384]{3,2,1,0:T(8,128)S(1)}, u32[]{:S(2)}, u32[]{:S(2)}) collective-permute-start(f32[11,4,8,384]{3,2,1,0:T(8,128)S(1)} %widen_operator.1), channel_id=1, source_target_pairs={{0,1},{1,2},{2,3},{4,5},{5,6},{6,7},{8,9},{9,10},{10,11},{12,13},{... | collective-permute-start | bytes 1622024 | tf_op jit(solution)/shard_map/ppermute | solution.py:530
  79.7 1.0 copy-start.13
  100.2 2.2 %copy-start = (f32[11,4,72,384]{3,2,1,0:T(8,128)}, f32[11,4,72,384]{3,2,1,0:T(8,128)S(1)}, u32[]{:S(2)}) copy-start(f32[11,4,72,384]{3,2,1,0:T(8,128)S(1)} %extend.1.operator) | copy-start | bytes 14598148
  102.4 1.2 copy-start.8
  103.6 1.0 copy-start.15
  112.1 3.4 %collective-permute-start.4 = (f32[64,128]{1,0:T(8,128)S(1)}, f32[64,128]{1,0:T(8,128)S(1)}, u32[]{:S(2)}, u32[]{:S(2)}) collective-permute-start(f32[64,128]{1,0:T(8,128)S(1)} %get-tuple-element.25), channel_id=1, source_target_pairs={{4,0},{5,1},{6,2},{7,3},{8,4},{9,5},{10,6},{11,7},{12,8},{13,9},{1... | collective-permute-start | bytes 98312 | tf_op jit(solution)/shard_map/ppermute | solution.py:530
  112.9 8.8 %collective-permute-start.5 = (f32[64,128]{1,0:T(8,128)S(1)}, f32[64,128]{1,0:T(8,128)S(1)}, u32[]{:S(2)}, u32[]{:S(2)}) collective-permute-start(f32[64,128]{1,0:T(8,128)S(1)} %get-tuple-element.25), channel_id=1, source_target_pairs={{124,0},{125,1},{126,2},{127,3},{0,4},{1,5},{2,6},{3,7},{4,8},{5,9... | collective-permute-start | bytes 98312 | tf_op jit(solution)/shard_map/ppermute | solution.py:530
  121.8 11.4 %copy-start.1 = (f32[11,4,72,384]{3,2,1,0:T(8,128)S(1)}, f32[11,4,72,384]{3,2,1,0:T(8,128)}, u32[]{:S(2)}) copy-start(f32[11,4,72,384]{3,2,1,0:T(8,128)} %copy-done) | copy-start | bytes 14598148
  121.8 11.4 %collective-permute-start.6 = (f32[2,4,8,384]{3,2,1,0:T(8,128)S(1)}, f32[2,4,8,384]{3,2,1,0:T(8,128)S(1)}, u32[]{:S(2)}, u32[]{:S(2)}) collective-permute-start(f32[2,4,8,384]{3,2,1,0:T(8,128)S(1)} %widen.1), channel_id=1, source_target_pairs={{1,0},{2,1},{3,2},{5,4},{6,5},{7,6},{9,8},{10,9},{11,10},{13,12},{... | collective-permute-start | bytes 294920 | tf_op jit(solution)/shard_map/ppermute | solution.py:530
  124.7 8.5 %collective-permute-start.7 = (f32[2,4,8,384]{3,2,1,0:T(8,128)S(1)}, f32[2,4,8,384]{3,2,1,0:T(8,128)S(1)}, u32[]{:S(2)}, u32[]{:S(2)}) collective-permute-start(f32[2,4,8,384]{3,2,1,0:T(8,128)S(1)} %widen.1), channel_id=1, source_target_pairs={{0,1},{1,2},{2,3},{4,5},{5,6},{6,7},{8,9},{9,10},{10,11},{12,13},{... | collective-permute-start | bytes 294920 | tf_op jit(solution)/shard_map/ppermute | solution.py:530
  (7 other events, 6.4 us)

commit v3 on v2

--- a/solution.py
+++ b/solution.py
@@ -65,10 +65,10 @@
     return east, north
 
 
-GROUP = 8
-
-
-def send_kernel(current, key, cols, mass_ref, coriolis_ref, start_ref, wind_ref, out, table, rows):
+GROUP = 16
+
+
+def send_kernel(current, key, cols, mass_ref, coriolis_ref, start_ref, wind_ref, out, own, table, rows):
     count = cols.shape[0]
 
     @pl.when(pl.program_id(0) == 0)
@@ -94,7 +94,9 @@
                 [lane_gather(tile[8 * i : 8 * i + 8, 128 * c : 128 * c + 128], inside[8 * i : 8 * i + 8]) for i in range(GROUP)],
                 axis=0,
             )
-            out[group, 4 + c] = jnp.where(index >= 0, DRAG * got, 0.0).reshape(GROUP, 8, 128)
+            got = jnp.where(index >= 0, DRAG * got, 0.0).reshape(GROUP, 8, 128)
+            out[group, 4 + c] = got
+            own[group, c] = got
         mass = mass_ref[group].reshape(tall, 128)
         a = mass + DRAG + 2.0 * LINK
         t = coriolis_ref[group].reshape(tall, 128) * mass
@@ -115,7 +117,7 @@
 
 
 def chunked(count):
-    step = min(count, 32)
+    step = min(count, 64)
     one = pl.BlockSpec((step, 8, 128), lambda i: (i, 0, 0))
     two = pl.BlockSpec((2, step, 8, 128), lambda i: (0, i, 0, 0))
     response = pl.BlockSpec((step, 4, 8, 128), lambda i: (i, 0, 0, 0))
@@ -138,16 +140,23 @@
             two,
             two,
         ],
-        out_specs=pl.BlockSpec((step, 6, 8, 128), lambda i: (i, 0, 0, 0)),
-        out_shape=jax.ShapeDtypeStruct((count, 6, 8, 128), F32),
+        out_specs=(
+            pl.BlockSpec((step, 6, 8, 128), lambda i: (i, 0, 0, 0)),
+            pl.BlockSpec((step, 2, 8, 128), lambda i: (i, 0, 0, 0)),
+        ),
+        out_shape=(
+            jax.ShapeDtypeStruct((count, 6, 8, 128), F32),
+            jax.ShapeDtypeStruct((count, 2, 8, 128), F32),
+        ),
         scratch_shapes=[pltpu.VMEM((3, 512, 256), BF16), pltpu.VMEM((8 * step, 256), F32)],
-        compiler_params=params(16),
+        compiler_params=params(60),
         cost_estimate=cost(10**9, 8 * MIB),
         name="send",
     )(current, key, cols, mass, coriolis, start, wind)
 
 
-def velocity_kernel(response, current_ref, out):
+def velocity_kernel(response, current_ref, _, out, done):
+    done[...] = jnp.zeros((8, 128), F32)
     tall = 8 * GROUP
     lane = iota((tall, 128), 1)
 
@@ -163,19 +172,22 @@
     lax.fori_loop(0, response.shape[0] // GROUP, body, 0)
 
 
-def velocities(sent, received):
+ORDER = pl.BlockSpec(memory_space=pl.ANY)
+
+
+def velocities(sent, received, after):
     count = sent.shape[0]
     _, grid, _, two, response, current = chunked(count)
     return pl.pallas_call(
         velocity_kernel,
         grid=(grid,),
-        in_specs=[response, current],
-        out_specs=two,
-        out_shape=jax.ShapeDtypeStruct((2, count, 8, 128), F32),
-        compiler_params=params(16),
+        in_specs=[response, current, ORDER],
+        out_specs=(two, pl.BlockSpec((8, 128), lambda i: (0, 0))),
+        out_shape=(jax.ShapeDtypeStruct((2, count, 8, 128), F32), jax.ShapeDtypeStruct((8, 128), F32)),
+        compiler_params=params(60),
         cost_estimate=cost(10**7, 4 * MIB),
         name="velocities",
-    )(sent, received)
+    )(sent, received, after)
 
 
 def invert_kernel(cols, key, inverse, hot):
@@ -206,21 +218,40 @@
     return pl.pallas_call(
         invert_kernel,
         out_shape=(jax.ShapeDtypeStruct((count, 8, 128), I32), jax.ShapeDtypeStruct((512, 8 * count), BF16)),
-        compiler_params=params(16),
+        compiler_params=params(60),
         cost_estimate=cost(10**10, 2 * MIB),
         name="invert",
     )(cols, key)
 
 
-def stress_kernel(response, current_ref, inverse, hot, planes, side, ends, parts):
-    count = inverse.shape[0]
+def stress_kernel(response_in, own_in, inverse_in, hot_in, *refs):
+    planes, side, ends, parts, response, current_ref, inverse, hot, arrived, listed = refs[-10:]
+    groups = inverse.shape[0] // GROUP
+
+    def transfer(g):
+        group = pl.ds(GROUP * g, GROUP)
+        return (
+            pltpu.make_async_copy(response_in.at[group, pl.ds(0, 4)], response.at[group], arrived.at[0, g]),
+            pltpu.make_async_copy(own_in.at[group], current_ref.at[group], arrived.at[1, g]),
+        )
+
+    inverse_copy = pltpu.make_async_copy(inverse_in, inverse, listed.at[0])
+    hot_copy = pltpu.make_async_copy(hot_in, hot, listed.at[1])
+    for g in range(groups):
+        for copy in transfer(g):
+            copy.start()
+        if g == 0:
+            inverse_copy.start()
+    hot_copy.start()
+    inverse_copy.wait()
     tall = 8 * GROUP
     lane = iota((tall, 128), 1)
-    chunk = pl.program_id(0)
 
     def body(g, carry):
+        for copy in transfer(g):
+            copy.wait()
         group = pl.ds(GROUP * g, GROUP)
-        rows = pl.ds(pl.multiple_of(8 * count * chunk + tall * g, tall), tall)
+        rows = pl.ds(pl.multiple_of(tall * g, tall), tall)
         base_east, base_north, a, t = (response[group, n].reshape(tall, 128) for n in range(4))
         current = [current_ref[group, c].reshape(tall, 128) for c in range(2)]
         east, north = respond(a, t, *current, lane)
@@ -236,59 +267,60 @@
                 parts[part, rows, 128 * c : 128 * c + 128] = pieces[part]
         return carry
 
-    lax.fori_loop(0, count // GROUP, body, 0)
-
-    @pl.when(chunk == pl.num_programs(0) - 1)
-    def _():
-        total = dot(hot[...], parts[0]) + dot(hot[...], parts[1]) + dot(hot[...], parts[2])
-        lane = iota((ROWS, 128), 1)
-        low = lane < 64
-        top = iota((8, 128), 0) < 4
-        edge = jnp.zeros((ROWS, 128), F32)
-        for c in range(2):
-            for py in range(2):
-                for h in range(2):
-                    first = 256 * h + 64 * py
-                    a = total[first : first + 64, 128 * c : 128 * c + 128]
-                    b = total[first + 128 : first + 192, 128 * c : 128 * c + 128]
-                    even = jnp.where(low, a, pltpu.roll(b, 64, 1))
-                    odd = jnp.where(low, pltpu.roll(a, 64, 1), b)
-                    for px, value in ((0, even), (1, odd)):
-                        plane = 2 * py + px
-                        planes[c, plane, :, 128 * h : 128 * h + 128] = value
-                        ends[c, plane, :, 128 * h : 128 * h + 128] = jnp.where(top, value[:8], value[56:])
-                        item = 4 * c + plane
-                        if h == 0:
-                            moved = pltpu.roll(value, 8 * item, 1) if item else value
-                            edge = jnp.where(lane // 8 == item, moved, edge)
-                        else:
-                            moved = pltpu.roll(value, (64 + 8 * item + 8) % 128, 1) if item != 7 else value
-                            edge = jnp.where(lane // 8 == 8 + item, moved, edge)
-        side[...] = edge
-
-
-def stresses(sent, received, inverse, hot):
+    lax.fori_loop(0, groups, body, 0)
+    hot_copy.wait()
+    total = dot(hot[...], parts[0]) + dot(hot[...], parts[1]) + dot(hot[...], parts[2])
+    lane = iota((ROWS, 128), 1)
+    low = lane < 64
+    top = iota((8, 128), 0) < 4
+    edge = jnp.zeros((ROWS, 128), F32)
+    for c in range(2):
+        for py in range(2):
+            for h in range(2):
+                first = 256 * h + 64 * py
+                a = total[first : first + 64, 128 * c : 128 * c + 128]
+                b = total[first + 128 : first + 192, 128 * c : 128 * c + 128]
+                even = jnp.where(low, a, pltpu.roll(b, 64, 1))
+                odd = jnp.where(low, pltpu.roll(a, 64, 1), b)
+                for px, value in ((0, even), (1, odd)):
+                    plane = 2 * py + px
+                    planes[c, plane, :, 128 * h : 128 * h + 128] = value
+                    ends[c, plane, :, 128 * h : 128 * h + 128] = jnp.where(top, value[:8], value[56:])
+                    item = 4 * c + plane
+                    if h == 0:
+                        moved = pltpu.roll(value, 8 * item, 1) if item else value
+                        edge = jnp.where(lane // 8 == item, moved, edge)
+                    else:
+                        moved = pltpu.roll(value, (64 + 8 * item + 8) % 128, 1) if item != 7 else value
+                        edge = jnp.where(lane // 8 == 8 + item, moved, edge)
+    side[...] = edge
+
+
+def stresses(received, own, inverse, hot, after):
     count = inverse.shape[0]
-    step, grid, one, _, response, current = chunked(count)
-
-    def whole(shape):
-        return pl.BlockSpec(shape, lambda i: (0,) * len(shape))
-
+    inside = pl.BlockSpec(memory_space=pltpu.VMEM)
     shapes = ((2, 4, ROWS, COLS), (ROWS, 128), (2, 4, 8, COLS))
     return pl.pallas_call(
         stress_kernel,
-        grid=(grid,),
-        in_specs=[response, current, one, whole((512, 8 * count))],
-        out_specs=tuple(whole(shape) for shape in shapes),
+        in_specs=[ORDER] * (4 + len(after)),
+        out_specs=(inside,) * 3,
         out_shape=tuple(jax.ShapeDtypeStruct(shape, F32) for shape in shapes),
-        scratch_shapes=[pltpu.VMEM((3, 8 * count, 256), BF16)],
-        compiler_params=params(16),
+        scratch_shapes=[
+            pltpu.VMEM((3, 8 * count, 256), BF16),
+            pltpu.VMEM((count, 4, 8, 128), F32),
+            pltpu.VMEM((count, 2, 8, 128), F32),
+            pltpu.VMEM((count, 8, 128), I32),
+            pltpu.VMEM((512, 8 * count), BF16),
+            pltpu.SemaphoreType.DMA((2, count // GROUP)),
+            pltpu.SemaphoreType.DMA((2,)),
+        ],
+        compiler_params=params(60),
         cost_estimate=cost(10**9, 4 * MIB),
         name="stresses",
-    )(received, sent, inverse, hot)
-
-
-def widen_kernel(ends, right, left, out):
+    )(received, own, inverse, hot, *after)
+
+
+def widen_kernel(ends, right, left, far_right, far_left, _, out):
     lane = iota((8, 128), 1)
     top = iota((8, 128), 0) < 4
     from_right = jnp.where(top, right[0:8], right[56:64])
@@ -298,18 +330,26 @@
             item = 4 * c + p
             r = pltpu.roll(from_right, (128 - 8 * item) % 128, 1) if item else from_right
             s = pltpu.roll(from_left, (56 - 8 * item) % 128, 1) if item != 7 else from_left
-            out[c, p, :, 0:COLS] = ends[c, p]
-            out[c, p, :, COLS:XCOLS] = jnp.where(lane < 64, r, s)
-
-
-def widen(ends, right, left):
+            out[item, :, 0:COLS] = ends[c, p]
+            out[item, :, COLS:XCOLS] = jnp.where(lane < 64, r, s)
+    for py in range(2):
+        for g in range(2):
+            for n, edge in enumerate((far_right, far_left)):
+                span = slice(128 * g, 128 * g + 128)
+                out[8 + 2 * py + n, :, span] = jnp.where(top, edge[py, 0:8, span], edge[py, 56:64, span])
+            out[8 + 2 * py + g, :, COLS:XCOLS] = jnp.zeros((8, 128), F32)
+
+
+def widen(ends, right, left, far_right, far_left, after):
+    inside = pl.BlockSpec(memory_space=pltpu.VMEM)
     return pl.pallas_call(
         widen_kernel,
-        out_shape=jax.ShapeDtypeStruct((2, 4, 8, XCOLS), F32),
+        in_specs=[inside] * 5 + [ORDER],
+        out_shape=jax.ShapeDtypeStruct((12, 8, XCOLS), F32),
         compiler_params=params(4),
         cost_estimate=cost(10**5, MIB // 4),
         name="widen",
-    )(ends, right, left)
+    )(ends, right, left, far_right, far_left, after)
 
 
 ARRAYS = 11
@@ -377,63 +417,43 @@
             jax.ShapeDtypeStruct((ARRAYS, 4, 8, COLS), F32),
         ),
         scratch_shapes=[pltpu.VMEM((4 * ARRAYS, 2 * ROWS, 128), F32)],
-        compiler_params=params(20),
+        compiler_params=params(60),
         cost_estimate=cost(10**7, 7 * MIB),
         name="prepare",
     )(sea, forcing, weights, excess, mask)
 
 
-def place_edges(n, p, right, left, rows, lane):
-    item = 2 * n + p % 2
-    span = slice(128 * (item // 16), 128 * (item // 16) + 128)
-    slot = item % 16
-    r, s = right[p // 2, rows, span], left[p // 2, rows, span]
-    r = pltpu.roll(r, (128 - 8 * slot) % 128, 1) if slot else r
-    s = pltpu.roll(s, (120 - 8 * slot) % 128, 1) if slot != 15 else s
+def place_edges(n, p, right, left, lane):
+    slot = (2 * n + p % 2) % 16
+    r = pltpu.roll(right, (128 - 8 * slot) % 128, 1) if slot else right
+    s = pltpu.roll(left, (120 - 8 * slot) % 128, 1) if slot != 15 else left
     return jnp.where(lane < 8, r, jnp.where(lane >= 120, s, 0.0))
 
 
-def widen_operator_kernel(ends, right, left, out):
-    lane = iota((8, 128), 1)
-    top = iota((8, 128), 0) < 4
+def packed_at(n, p):
+    group = (2 * n + p % 2) // 16
+    return slice(128 * group, 128 * group + 128)
+
+
+def extend_kernel(planes, right, left, _, out):
+    lane = iota((ROWS, 128), 1)
     for n in range(ARRAYS):
         for p in range(4):
-            out[n, p, :, 0:COLS] = ends[n, p]
-            out[n, p, :, COLS:XCOLS] = jnp.where(
-                top,
-                place_edges(n, p, right, left, slice(0, 8), lane),
-                place_edges(n, p, right, left, slice(56, 64), lane),
-            )
-
-
-def widen_operator(ends, right, left):
-    return pl.pallas_call(
-        widen_operator_kernel,
-        out_shape=jax.ShapeDtypeStruct((ARRAYS, 4, 8, XCOLS), F32),
-        compiler_params=params(8),
-        cost_estimate=cost(10**6, 2 * MIB),
-        name="widen_operator",
-    )(ends, right, left)
-
-
-def extend_kernel(planes, right, left, below, above, out):
-    lane = iota((ROWS, 128), 1)
-    top = iota((8, XCOLS), 0) < 4
-    for n in range(ARRAYS):
-        for p in range(4):
-            out[n, p, 0:ROWS, 0:COLS] = planes[n, p]
-            out[n, p, 0:ROWS, COLS:XCOLS] = place_edges(n, p, right, left, slice(0, ROWS), lane)
-            out[n, p, ROWS:XROWS, :] = jnp.where(top, below[n, p], above[n, p])
-
-
-def extend(*arrays):
+            span = packed_at(n, p)
+            out[n, p, :, 0:COLS] = planes[n, p]
+            out[n, p, :, COLS:XCOLS] = place_edges(n, p, right[p // 2, :, span], left[p // 2, :, span], lane)
+
+
+def extend(planes, right, left, after):
+    inside = pl.BlockSpec(memory_space=pltpu.VMEM)
     return pl.pallas_call(
         extend_kernel,
-        out_shape=jax.ShapeDtypeStruct((ARRAYS, 4, XROWS, XCOLS), F32),
+        in_specs=[inside] * 3 + [ORDER],
+        out_shape=jax.ShapeDtypeStruct((ARRAYS, 4, ROWS, XCOLS), F32),
         compiler_params=params(20),
         cost_estimate=cost(10**7, 8 * MIB),
         name="extend",
-    )(*arrays)
+    )(planes, right, left, after)
 
 
 def row_shift(value, step):
@@ -448,7 +468,9 @@
     return (step + parity) // 2
 
 
-def sweep_kernel(operator, stress, right, left, below, above, out, wide, source, field, natural):
+def sweep_kernel(
+    operator, far_below, far_above, stress, right, left, below, above, out, wide, source, field, natural, rim
+):
     lane = iota((ROWS, 128), 1)
     top = iota((8, XCOLS), 0) < 4
     for c in range(2):
@@ -458,15 +480,26 @@
             s = pltpu.roll(left[...], (56 - 8 * item) % 128, 1) if item != 7 else left[...]
             wide[c, p, 0:ROWS, 0:COLS] = stress[c, p]
             wide[c, p, 0:ROWS, COLS:XCOLS] = jnp.where(lane < 64, r, s)
-            wide[c, p, ROWS:XROWS, :] = jnp.where(top, below[c, p], above[c, p])
+            wide[c, p, ROWS:XROWS, :] = jnp.where(top, below[item], above[item])
+    corners = [jnp.where(top, below[8 + n], above[8 + n]) for n in range(4)]
+    for n in range(ARRAYS):
+        for p in range(4):
+            span = packed_at(n, p)
+            far_right, far_left = corners[2 * (p // 2)], corners[2 * (p // 2) + 1]
+            rim[n, p, :, 0:COLS] = jnp.where(top[:, :COLS], far_below[n, p], far_above[n, p])
+            rim[n, p, :, COLS:XCOLS] = place_edges(n, p, far_right[:, span], far_left[:, span], lane[:8])
+
+    def entry(n, p):
+        return jnp.concatenate([operator[n, p], rim[n, p]], axis=0)
+
     for p in range(4):
         py, px = p // 2, p % 2
         north = wide[1, 2 * py + 1 - px]
         east = wide[0, 2 * (1 - py) + px]
         zonal = col_shift(north, neighbour(1, px)) - col_shift(north, neighbour(-1, px))
         meridional = row_shift(east, neighbour(1, py)) - row_shift(east, neighbour(-1, py))
-        source[p] = (operator[9, p] + zonal - meridional) * operator[8, p]
-        field[p] = operator[10, p]
+        source[p] = (entry(9, p) + zonal - meridional) * entry(8, p)
+        field[p] = entry(10, p)
     for colour in COLOURS:
         py, px = colour // 2, colour % 2
         value = source[colour]
@@ -477,7 +510,7 @@
                 v = row_shift(v, neighbour(dy, py))
             if dx:
                 v = col_shift(v, neighbour(dx, px))
-            value = value + operator[k, colour] * v
+            value = value + entry(k, colour) * v
         field[colour] = value
     lane = iota((ROWS, 128), 1)
     even_lane = lane % 2 == 0
@@ -505,6 +538,7 @@
             pltpu.VMEM((4, XROWS, XCOLS), F32),
             pltpu.VMEM((4, XROWS, XCOLS), F32),
             pltpu.VMEM((4, 128, 128), F32),
+            pltpu.VMEM((ARRAYS, 4, 8, XCOLS), F32),
         ],
         compiler_params=params(20),
         cost_estimate=cost(10**8, 6 * MIB),
@@ -551,20 +585,19 @@
     fetch_key = jnp.where(blocks >= 0, part * 128 + row, -1).reshape(slots, 1)
     scatter_key = jnp.where(blocks >= 0, part * 128 + (row & 1) * 64 + (row >> 1), -1).reshape(1, slots)
 
-    sent = send(current, fetch_key, cols, ice_mass[0], coriolis[0], ice_start[:, 0], wind_stress[:, 0])
+    sent, own = send(current, fetch_key, cols, ice_mass[0], coriolis[0], ice_start[:, 0], wind_stress[:, 0])
     received = exchange(sent)
     planes, left_edge, right_edge, ends = prepare(sea_level, forcing, link_weights, excess, ocean_mask)
-    right, left = from_neighbour(left_edge, 1, 0), from_neighbour(right_edge, -1, 0)
-    rows = widen_operator(ends, right, left)
-    operator = extend(planes, right, left, from_neighbour(rows, 0, 1), from_neighbour(rows, 0, -1))
+    far_right, far_left = from_neighbour(left_edge, 1, 0), from_neighbour(right_edge, -1, 0)
+    far_below, far_above = from_neighbour(ends, 0, 1), from_neighbour(ends, 0, -1)
     inverse, hot = invert(cols, scatter_key)
-    inverse, operator = lax.optimization_barrier((inverse, operator))
-    stress, side, ends = stresses(sent, received, inverse, hot)
-    received, side = lax.optimization_barrier((received, side))
+    stress, side, ends = stresses(received, own, inverse, hot, (far_right, far_left, far_below, far_above))
     right, left = from_neighbour(side, 1, 0), from_neighbour(side, -1, 0)
-    rows = widen(ends, right, left)
-    surface = sweep(operator, stress, right, left, from_neighbour(rows, 0, 1), from_neighbour(rows, 0, -1))
-    velocity = velocities(sent, received)
+    velocity, done = velocities(sent, received, side)
+    rows = widen(ends, right, left, far_right, far_left, done)
+    operator = extend(planes, far_right, far_left, rows)
+    below, above = from_neighbour(rows, 0, 1), from_neighbour(rows, 0, -1)
+    surface = sweep(operator, far_below, far_above, stress, right, left, below, above)
     return surface, velocity[:, None]
 
 

time: 138 us -> 105 us (0.76)
  local copies, waits for them, and re-layouts: 23.6 us -> 3.45 us
  waiting for transfers between devices: 30.2 us -> 10.4 us
  starting transfers between devices: 32.7 us -> 37.4 us
  Pallas kernels: 48.6 us -> 52 us
    unnamed x44 -> x24, local copies, waits for them, and re-layouts: 21.6 us -> 1.57 us
    ppermute x8, waiting for transfers between devices: 30.2 us -> 10.4 us  [from_neighbour(): return lax.ppermute(values, AXES, pairs)]
    ppermute x8, starting transfers between devices: 21.2 us -> 25.6 us  [from_neighbour(): return lax.ppermute(values, AXES, pairs)]
    pallas_call x1, Pallas kernels: 6.05 us -> 8.92 us  [prepare(): pl.pallas_call(prepare_kernel, out_shape=(jax.ShapeDtypeStruct((ARRAYS, 4...]
    pallas_call x1, Pallas kernels: 16.8 us -> 18.7 us  [invert(): pl.pallas_call(invert_kernel, out_shape=(jax.ShapeDtypeStruct((count, 8,...]
    pallas_call x4 -> x3, Pallas kernels: 8.64 us -> 8.31 us  [the longest x1 7.36 us: stresses(): pl.pallas_call(stress_kernel, in_specs=[ORDER] * (4 + len(after)), out_sp...]
  transfers between devices with their start and end apart: 9 -> 9, of which waited for: 4 -> 2; matrix products, arithmetic and copies ran while one was open for 1% -> 1% of each run, Pallas kernels for 22% -> 31%
where the time goes in v3:
time: 105 us
  Pallas kernels  52 us (50%)
  starting transfers between devices  37.4 us (36%)
  waiting for transfers between devices  10.4 us (10%)
  local copies, waits for them, and re-layouts  3.45 us (3%)
    ppermute x8, starting transfers between devices, from_neighbour(): return lax.ppermute(values, AXES, pairs)  25.6 us
    pallas_call x1, Pallas kernels, invert(): pl.pallas_call(invert_kernel, out_shape=(jax.ShapeDtypeStruct((count, 8,...  18.7 us
    all_to_all x1, starting transfers between devices, exchange(): return lax.all_to_all(values, AXES, split_axis=0, concat_axis=0, tiled=True)  11.9 us
    ppermute x8, waiting for transfers between devices, from_neighbour(): return lax.ppermute(values, AXES, pairs)  10.4 us
    pallas_call x1, Pallas kernels, prepare(): pl.pallas_call(prepare_kernel, out_shape=(jax.ShapeDtypeStruct((ARRAYS, 4...  8.92 us
    pallas_call x1, Pallas kernels, send(): pl.pallas_call(send_kernel, grid=(grid,), in_specs=[pl.BlockSpec((2, 128,...  8.27 us
    pallas_call x1, Pallas kernels, stresses(): pl.pallas_call(stress_kernel, in_specs=[ORDER] * (4 + len(after)), out_sp...  7.36 us
    pallas_call x1, Pallas kernels, velocities(): pl.pallas_call(velocity_kernel, grid=(grid,), in_specs=[response, current...  4.37 us
  transfers between devices with their start and end apart: 9, of which 2 were waited for; matrix products, arithmetic and copies ran while one was open for 1% of the time, Pallas kernels for 31%

profile of v3, /device:TPU:1, one launch (start us, length us, event | category | flops | bytes accessed | tf_op | source)
XLA Modules:
  0.0 104.9 jit_solution(7814561975151460646)
XLA Ops:
  0.6 0.7 add_select_fusion
  1.3 0.1 copy.17
  1.4 1.0 select_n.28.key
  2.4 8.3 %send.1 = (f32[128,6,8,128]{3,2,1,0:T(8,128)}, f32[128,2,8,128]{3,2,1,0:T(8,128)}) custom-call(f32[2,128,512]{2,1,0:T(8,128)} %current.1, s32[1024,1]{1,0:T(8,128)} %select_n.28.key, s32[128,8,128]{2,1,0:T(8,128)} %bitcast.12, f32[128,8,128]{2,1,0:T(8,128)} %bitcast.10, f32[128,8,128]{2,1,0:T(8,128)} %bitcast.11, f32[2,128,8,128]{3,2,1,0:T(8,128)} %bitcast.8, ...), custom_call_target="tpu_custom_call" | custom-call | flops 1000000000 | bytes 8388608 | tf_op jit(solution)/shard_map/send/pallas_call | solution.py:131
  10.7 11.9 %all-to-all-start = ((f32[128,6,8,128]{3,2,1,0:T(8,128)}), f32[128,6,8,128]{3,2,1,0:T(8,128)}, u32[]{:S(2)}, u32[]{:S(2)}) async-start(f32[128,6,8,128]{3,2,1,0:T(8,128)} %get-tuple-element.18.response), calls=%async_computation | async-start | bytes 6291456 | tf_op jit(solution)/shard_map/all_to_all | solution.py:553
  22.6 8.9 %prepare.1 = (f32[11,4,64,256]{3,2,1,0:T(8,128)}, f32[2,64,256]{2,1,0:T(8,128)}, f32[2,64,256]{2,1,0:T(8,128)}, f32[11,4,8,256]{3,2,1,0:T(8,128)}) custom-call(f32[128,512]{1,0:T(8,128)} %sea.1, f32[128,512]{1,0:T(8,128)} %forcing.1, f32[8,128,512]{2,1,0:T(8,128)} %weights.1, f32[128,512]{1,0:T(8,128)} %excess.1, s32[128,512]{1,0:T(8,128)} %mask.1), custom_call_target="tpu_custom_call" | custom-call | flops 10000000 | bytes 7340032 | tf_op jit(solution)/shard_map/prepare/pallas_call | solution.py:411
  31.5 3.5 %collective-permute-start.3 = (f32[11,4,8,256]{3,2,1,0:T(8,128)}, f32[11,4,8,256]{3,2,1,0:T(8,128)S(1)}, u32[]{:S(2)}, u32[]{:S(2)}) collective-permute-start(f32[11,4,8,256]{3,2,1,0:T(8,128)} %get-tuple-element.22), channel_id=1, source_target_pairs={{0,1},{1,2},{2,3},{4,5},{5,6},{6,7},{8,9},{9,10},{10,11},{12,13},{... | collective-permute-start | bytes 1081352 | tf_op jit(solution)/shard_map/ppermute | solution.py:564
  35.0 1.9 %collective-permute-start.2 = (f32[11,4,8,256]{3,2,1,0:T(8,128)}, f32[11,4,8,256]{3,2,1,0:T(8,128)S(1)}, u32[]{:S(2)}, u32[]{:S(2)}) collective-permute-start(f32[11,4,8,256]{3,2,1,0:T(8,128)} %get-tuple-element.22), channel_id=1, source_target_pairs={{1,0},{2,1},{3,2},{5,4},{6,5},{7,6},{9,8},{10,9},{11,10},{13,12},{... | collective-permute-start | bytes 1081352 | tf_op jit(solution)/shard_map/ppermute | solution.py:564
  37.0 7.6 %collective-permute-start = (f32[2,64,256]{2,1,0:T(8,128)}, f32[2,64,256]{2,1,0:T(8,128)S(1)}, u32[]{:S(2)}, u32[]{:S(2)}) collective-permute-start(f32[2,64,256]{2,1,0:T(8,128)} %get-tuple-element.16), channel_id=1, source_target_pairs={{4,0},{5,1},{6,2},{7,3},{8,4},{9,5},{10,6},{11,7},{12,8},{13,9},{1... | collective-permute-start | bytes 393224 | tf_op jit(solution)/shard_map/ppermute | solution.py:564
  44.7 0.7 reshape.120.key
  45.4 18.7 %invert.1 = (s32[128,8,128]{2,1,0:T(8,128)}, bf16[512,1024]{1,0:T(8,128)(2,1)}) custom-call(s32[128,8,128]{2,1,0:T(8,128)} %bitcast.13, s32[1,1024]{1,0:T(1,128)} %reshape.120.key), custom_call_target="tpu_custom_call" | custom-call | flops 10000000000 | bytes 2097152 | tf_op jit(solution)/shard_map/invert/pallas_call | solution.py:218
  64.1 6.8 %collective-permute-done.1.refs_1_.far_left.left = f32[2,64,256]{2,1,0:T(8,128)S(1)} collective-permute-done((f32[2,64,256]{2,1,0:T(8,128)}, f32[2,64,256]{2,1,0:T(8,128)S(1)}, u32[]{:S(2)}, u32[]{:S(2)}) %collective-permute-start.1) | collective-permute-done | bytes 131104 | tf_op jit(solution)/shard_map/ppermute | solution.py:564
  70.9 0.6 copy-done.7
  71.5 0.1 copy-done.1
  71.6 0.1 copy-done.3
  71.7 7.4 %stresses.1 = (f32[2,4,64,256]{3,2,1,0:T(8,128)}, f32[64,128]{1,0:T(8,128)}, f32[2,4,8,256]{3,2,1,0:T(8,128)}) custom-call(f32[128,6,8,128]{3,2,1,0:T(8,128)} %all-to-all-done.response_in.current_ref, f32[128,2,8,128]{3,2,1,0:T(8,128)} %get-tuple-element.19.own_in, s32[128,8,128]{2,1,0:T(8,128)} %get-tuple-element.20.inverse_in, ...), custom_call_target="tpu_custom_call" | custom-call | flops 1000000000 | bytes 4194304 | tf_op jit(solution)/shard_map/stresses/pallas_call | solution.py:303
  79.2 7.2 %collective-permute-start.4 = (f32[64,128]{1,0:T(8,128)}, f32[64,128]{1,0:T(8,128)S(1)}, u32[]{:S(2)}, u32[]{:S(2)}) collective-permute-start(f32[64,128]{1,0:T(8,128)} %get-tuple-element.24._), channel_id=1, source_target_pairs={{4,0},{5,1},{6,2},{7,3},{8,4},{9,5},{10,6},{11,7},{12,8},{13,9},{1... | collective-permute-start | bytes 98312 | tf_op jit(solution)/shard_map/ppermute | solution.py:564
  86.4 4.4 %velocities.1 = (f32[2,128,8,128]{3,2,1,0:T(8,128)}, f32[8,128]{1,0:T(8,128)}) custom-call(f32[128,6,8,128]{3,2,1,0:T(8,128)} %get-tuple-element.18.response, f32[128,6,8,128]{3,2,1,0:T(8,128)} %all-to-all-done.response_in.current_ref, f32[64,128]{1,0:T(8,128)} %get-tuple-element.24._), custom_call_target="tpu_custom_call" | custom-call | flops 10000000 | bytes 4194304 | tf_op jit(solution)/shard_map/velocities/pallas_call | solution.py:181
  90.8 0.7 copy-done.11
  91.6 3.3 %collective-permute-start.7 = (f32[12,8,384]{2,1,0:T(8,128)S(1)}, f32[12,8,384]{2,1,0:T(8,128)S(1)}, u32[]{:S(2)}, u32[]{:S(2)}) collective-permute-start(f32[12,8,384]{2,1,0:T(8,128)S(1)} %widen.1._), channel_id=1, source_target_pairs={{0,1},{1,2},{2,3},{4,5},{5,6},{6,7},{8,9},{9,10},{10,11},{12,13},{... | collective-permute-start | bytes 442376 | tf_op jit(solution)/shard_map/ppermute | solution.py:564
  95.0 1.9 %collective-permute-start.6 = (f32[12,8,384]{2,1,0:T(8,128)S(1)}, f32[12,8,384]{2,1,0:T(8,128)S(1)}, u32[]{:S(2)}, u32[]{:S(2)}) collective-permute-start(f32[12,8,384]{2,1,0:T(8,128)S(1)} %widen.1._), channel_id=1, source_target_pairs={{1,0},{2,1},{3,2},{5,4},{6,5},{7,6},{9,8},{10,9},{11,10},{13,12},{... | collective-permute-start | bytes 442376 | tf_op jit(solution)/shard_map/ppermute | solution.py:564
  96.9 0.9 extend.1.operator
  97.8 3.6 %collective-permute-done.6.below = f32[12,8,384]{2,1,0:T(8,128)S(1)} collective-permute-done((f32[12,8,384]{2,1,0:T(8,128)S(1)}, f32[12,8,384]{2,1,0:T(8,128)S(1)}, u32[]{:S(2)}, u32[]{:S(2)}) %collective-permute-start.6) | collective-permute-done | bytes 147488 | tf_op jit(solution)/shard_map/ppermute | solution.py:564
  101.4 3.4 %sweep.1 = f32[128,512]{1,0:T(8,128)} custom-call(f32[11,4,64,384]{3,2,1,0:T(8,128)S(1)} %extend.1.operator, f32[11,4,8,256]{3,2,1,0:T(8,128)S(1)} %copy-done.4, f32[11,4,8,256]{3,2,1,0:T(8,128)S(1)} %copy-done.2, f32[2,4,64,256]{3,2,1,0:T(8,128)S(1)} %copy-done.9, f32[64,128]{1,0:T(8,128)S(1)} %collective-permute-done.4.right, ...), custom_call_target="tpu_custom_call" | custom-call | flops 100000000 | bytes 6291456 | tf_op jit(solution)/shard_map/sweep/pallas_call | solution.py:533
  (31 shorter events, 0.3 us)
Async XLA Ops:
  10.7 60.2 %all-to-all-start = ((f32[128,6,8,128]{3,2,1,0:T(8,128)}), f32[128,6,8,128]{3,2,1,0:T(8,128)}, u32[]{:S(2)}, u32[]{:S(2)}) async-start(f32[128,6,8,128]{3,2,1,0:T(8,128)} %get-tuple-element.18.response), calls=%async_computation | async-start | bytes 6291456 | tf_op jit(solution)/shard_map/all_to_all | solution.py:553
  31.5 39.3 %collective-permute-start.3 = (f32[11,4,8,256]{3,2,1,0:T(8,128)}, f32[11,4,8,256]{3,2,1,0:T(8,128)S(1)}, u32[]{:S(2)}, u32[]{:S(2)}) collective-permute-start(f32[11,4,8,256]{3,2,1,0:T(8,128)} %get-tuple-element.22), channel_id=1, source_target_pairs={{0,1},{1,2},{2,3},{4,5},{5,6},{6,7},{8,9},{9,10},{10,11},{12,13},{... | collective-permute-start | bytes 1081352 | tf_op jit(solution)/shard_map/ppermute | solution.py:564
  35.0 35.8 %collective-permute-start.2 = (f32[11,4,8,256]{3,2,1,0:T(8,128)}, f32[11,4,8,256]{3,2,1,0:T(8,128)S(1)}, u32[]{:S(2)}, u32[]{:S(2)}) collective-permute-start(f32[11,4,8,256]{3,2,1,0:T(8,128)} %get-tuple-element.22), channel_id=1, source_target_pairs={{1,0},{2,1},{3,2},{5,4},{6,5},{7,6},{9,8},{10,9},{11,10},{13,12},{... | collective-permute-start | bytes 1081352 | tf_op jit(solution)/shard_map/ppermute | solution.py:564
  37.0 27.1 %collective-permute-start = (f32[2,64,256]{2,1,0:T(8,128)}, f32[2,64,256]{2,1,0:T(8,128)S(1)}, u32[]{:S(2)}, u32[]{:S(2)}) collective-permute-start(f32[2,64,256]{2,1,0:T(8,128)} %get-tuple-element.16), channel_id=1, source_target_pairs={{4,0},{5,1},{6,2},{7,3},{8,4},{9,5},{10,6},{11,7},{12,8},{13,9},{1... | collective-permute-start | bytes 393224 | tf_op jit(solution)/shard_map/ppermute | solution.py:564
  44.6 26.3 %collective-permute-start.1 = (f32[2,64,256]{2,1,0:T(8,128)}, f32[2,64,256]{2,1,0:T(8,128)S(1)}, u32[]{:S(2)}, u32[]{:S(2)}) collective-permute-start(f32[2,64,256]{2,1,0:T(8,128)} %get-tuple-element.17), channel_id=1, source_target_pairs={{124,0},{125,1},{126,2},{127,3},{0,4},{1,5},{2,6},{3,7},{4,8},{5,9... | collective-permute-start | bytes 393224 | tf_op jit(solution)/shard_map/ppermute | solution.py:564
  64.1 6.8 %copy-start.5 = (f32[2,64,256]{2,1,0:T(8,128)}, f32[2,64,256]{2,1,0:T(8,128)S(1)}, u32[]{:S(2)}) copy-start(f32[2,64,256]{2,1,0:T(8,128)S(1)} %collective-permute-done.refs_0_.far_right.right) | copy-start | bytes 393220
  70.8 0.7 copy-start.7
  70.9 0.8 copy-start.1
  70.9 0.9 copy-start.3
  79.1 11.7 %copy-start.6 = (f32[2,64,256]{2,1,0:T(8,128)S(1)}, f32[2,64,256]{2,1,0:T(8,128)}, u32[]{:S(2)}) copy-start(f32[2,64,256]{2,1,0:T(8,128)} %copy-done.5) | copy-start | bytes 393220
  79.1 11.7 %copy-start.8 = (f32[2,64,256]{2,1,0:T(8,128)S(1)}, f32[2,64,256]{2,1,0:T(8,128)}, u32[]{:S(2)}) copy-start(f32[2,64,256]{2,1,0:T(8,128)} %copy-done.7) | copy-start | bytes 393220
  79.1 11.7 %copy-start.10 = (f32[2,4,8,256]{3,2,1,0:T(8,128)S(1)}, f32[2,4,8,256]{3,2,1,0:T(8,128)}, u32[]{:S(2)}) copy-start(f32[2,4,8,256]{3,2,1,0:T(8,128)} %get-tuple-element.23.ends) | copy-start | bytes 196612
  79.2 17.7 %copy-start = (f32[11,4,64,256]{3,2,1,0:T(8,128)S(1)}, f32[11,4,64,256]{3,2,1,0:T(8,128)}, u32[]{:S(2)}) copy-start(f32[11,4,64,256]{3,2,1,0:T(8,128)} %get-tuple-element.15.planes) | copy-start | bytes 8650756
  79.2 11.6 %collective-permute-start.5 = (f32[64,128]{1,0:T(8,128)}, f32[64,128]{1,0:T(8,128)S(1)}, u32[]{:S(2)}, u32[]{:S(2)}) collective-permute-start(f32[64,128]{1,0:T(8,128)} %get-tuple-element.24._), channel_id=1, source_target_pairs={{124,0},{125,1},{126,2},{127,3},{0,4},{1,5},{2,6},{3,7},{4,8},{5,9... | collective-permute-start | bytes 98312 | tf_op jit(solution)/shard_map/ppermute | solution.py:564
  79.2 11.6 %collective-permute-start.4 = (f32[64,128]{1,0:T(8,128)}, f32[64,128]{1,0:T(8,128)S(1)}, u32[]{:S(2)}, u32[]{:S(2)}) collective-permute-start(f32[64,128]{1,0:T(8,128)} %get-tuple-element.24._), channel_id=1, source_target_pairs={{4,0},{5,1},{6,2},{7,3},{8,4},{9,5},{10,6},{11,7},{12,8},{13,9},{1... | collective-permute-start | bytes 98312 | tf_op jit(solution)/shard_map/ppermute | solution.py:564
  90.8 0.7 copy-start.11
  91.6 6.2 %collective-permute-start.7 = (f32[12,8,384]{2,1,0:T(8,128)S(1)}, f32[12,8,384]{2,1,0:T(8,128)S(1)}, u32[]{:S(2)}, u32[]{:S(2)}) collective-permute-start(f32[12,8,384]{2,1,0:T(8,128)S(1)} %widen.1._), channel_id=1, source_target_pairs={{0,1},{1,2},{2,3},{4,5},{5,6},{6,7},{8,9},{9,10},{10,11},{12,13},{... | collective-permute-start | bytes 442376 | tf_op jit(solution)/shard_map/ppermute | solution.py:564
  95.0 6.5 %collective-permute-start.6 = (f32[12,8,384]{2,1,0:T(8,128)S(1)}, f32[12,8,384]{2,1,0:T(8,128)S(1)}, u32[]{:S(2)}, u32[]{:S(2)}) collective-permute-start(f32[12,8,384]{2,1,0:T(8,128)S(1)} %widen.1._), channel_id=1, source_target_pairs={{1,0},{2,1},{3,2},{5,4},{6,5},{7,6},{9,8},{10,9},{11,10},{13,12},{... | collective-permute-start | bytes 442376 | tf_op jit(solution)/shard_map/ppermute | solution.py:564
  96.9 4.5 %copy-start.2 = (f32[11,4,8,256]{3,2,1,0:T(8,128)S(1)}, f32[11,4,8,256]{3,2,1,0:T(8,128)}, u32[]{:S(2)}) copy-start(f32[11,4,8,256]{3,2,1,0:T(8,128)} %copy-done.1) | copy-start | bytes 1081348
  96.9 4.5 %copy-start.4 = (f32[11,4,8,256]{3,2,1,0:T(8,128)S(1)}, f32[11,4,8,256]{3,2,1,0:T(8,128)}, u32[]{:S(2)}) copy-start(f32[11,4,8,256]{3,2,1,0:T(8,128)} %copy-done.3) | copy-start | bytes 1081348
  96.9 4.5 %copy-start.9 = (f32[2,4,64,256]{3,2,1,0:T(8,128)S(1)}, f32[2,4,64,256]{3,2,1,0:T(8,128)}, u32[]{:S(2)}) copy-start(f32[2,4,64,256]{3,2,1,0:T(8,128)} %get-tuple-element.26.stress) | copy-start | bytes 1572868

commit v4 on v3

--- a/solution.py
+++ b/solution.py
@@ -65,38 +65,74 @@
     return east, north
 
 
-GROUP = 16
-
-
-def send_kernel(current, key, cols, mass_ref, coriolis_ref, start_ref, wind_ref, out, own, table, rows):
-    count = cols.shape[0]
-
-    @pl.when(pl.program_id(0) == 0)
-    def _():
-        for c in range(2):
-            for k in range(4):
-                parts = split3(current[c, :, 128 * k : 128 * k + 128])
-                for part in range(3):
-                    table[part, 128 * k : 128 * k + 128, 128 * c : 128 * c + 128] = parts[part]
-
-    hot = jnp.where(key[...] == iota((8 * count, 512), 1), 1.0, 0.0).astype(BF16)
-    rows[...] = dot(hot, table[0]) + dot(hot, table[1]) + dot(hot, table[2])
-    tall = 8 * GROUP
+PIECE = 32
+
+
+def send_kernel(current_in, blocks, *refs):
+    ice_in, sent, (current, table, rows, hot), ice, out, (first, arrived, gone) = (
+        refs[:5],
+        refs[5],
+        refs[6:10],
+        refs[10:15],
+        refs[15],
+        refs[16:],
+    )
+    count = out.shape[0]
+    piece = min(count, PIECE)
+    current_copy = pltpu.make_async_copy(current_in, current, first.at[0])
+    current_copy.start()
+
+    def arrive(p):
+        span = pl.ds(piece * p, piece)
+        return [
+            pltpu.make_async_copy(source.at[span], target.at[span], arrived.at[n, p])
+            if n < 3
+            else pltpu.make_async_copy(source.at[:, span], target.at[:, span], arrived.at[n, p])
+            for n, (source, target) in enumerate(zip(ice_in, ice))
+        ]
+
+    def leave(p):
+        span = pl.ds(piece * p, piece)
+        return pltpu.make_async_copy(out.at[span], sent.at[span], gone.at[p])
+
+    for p in range(count // piece):
+        for copy in arrive(p):
+            copy.start()
+
+    key = jnp.where(blocks[...] >= 0, (blocks[...] & 3) * 128 + (blocks[...] >> 2), -1)
+    key = jnp.transpose(jnp.concatenate([key, jnp.zeros((120, 128), I32)], axis=0))
+    place = iota((128, 512), 1)
+    for s in range(8):
+        hot[128 * s : 128 * s + 128] = jnp.where(key[:, s : s + 1] == place, 1.0, 0.0).astype(BF16)
+    current_copy.wait()
+    for c in range(2):
+        for k in range(4):
+            parts = split3(current[c, :, 128 * k : 128 * k + 128])
+            for part in range(3):
+                table[part, 128 * k : 128 * k + 128, 128 * c : 128 * c + 128] = parts[part]
+    for q in range(4):
+        span = slice(256 * q, 256 * q + 256)
+        got = dot(hot[span], table[0]) + dot(hot[span], table[1]) + dot(hot[span], table[2])
+        rows[0, span] = got[:, :128]
+        rows[1, span] = got[:, 128:]
+
+    tall = 8 * piece
     lane = iota((tall, 128), 1)
-
-    def body(g, carry):
-        group = pl.ds(GROUP * g, GROUP)
-        tile = rows[pl.ds(pl.multiple_of(tall * g, tall), tall)]
+    cols, mass_ref, coriolis_ref, start_ref, wind_ref = ice
+
+    def body(g):
+        group = pl.ds(piece * g, piece)
         index = cols[group].reshape(tall, 128)
         inside = jnp.maximum(index, 0)
         for c in range(2):
             got = jnp.concatenate(
-                [lane_gather(tile[8 * i : 8 * i + 8, 128 * c : 128 * c + 128], inside[8 * i : 8 * i + 8]) for i in range(GROUP)],
+                [
+                    lane_gather(rows[c, pl.ds(piece * g + i, 8, stride=128), :], inside[8 * i : 8 * i + 8])
+                    for i in range(piece)
+                ],
                 axis=0,
             )
-            got = jnp.where(index >= 0, DRAG * got, 0.0).reshape(GROUP, 8, 128)
-            out[group, 4 + c] = got
-            own[group, c] = got
+            out[group, 4 + c] = jnp.where(index >= 0, DRAG * got, 0.0).reshape(piece, 8, 128)
         mass = mass_ref[group].reshape(tall, 128)
         a = mass + DRAG + 2.0 * LINK
         t = coriolis_ref[group].reshape(tall, 128) * mass
@@ -110,10 +146,21 @@
         for _ in range(ICE_SWEEPS):
             east, north = sweep_ice(a, t, east, north, base_east, base_north, lane)
         for n, value in enumerate((east, north, a, t)):
-            out[group, n] = value.reshape(GROUP, 8, 128)
+            out[group, n] = value.reshape(piece, 8, 128)
+
+    def move(p, carry):
+        for copy in arrive(p):
+            copy.wait()
+        body(p)
+        leave(p).start()
         return carry
 
-    lax.fori_loop(0, count // GROUP, body, 0)
+    lax.fori_loop(0, count // piece, move, 0)
+    for p in range(count // piece):
+        leave(p).wait()
+
+
+ORDER = pl.BlockSpec(memory_space=pl.ANY)
 
 
 def chunked(count):
@@ -125,54 +172,52 @@
     return step, count // step, one, two, response, current
 
 
-def send(current, key, cols, mass, coriolis, start, wind):
+def send(current, blocks, cols, mass, coriolis, start, wind):
     count = cols.shape[0]
-    step, grid, one, two, _, _ = chunked(count)
+    pieces = count // min(count, PIECE)
+    one, two = (count, 8, 128), (2, count, 8, 128)
     return pl.pallas_call(
         send_kernel,
-        grid=(grid,),
-        in_specs=[
-            pl.BlockSpec((2, 128, 512), lambda i: (0, 0, 0)),
-            pl.BlockSpec((8 * step, 1), lambda i: (i, 0)),
-            one,
-            one,
-            one,
-            two,
-            two,
+        in_specs=[ORDER, pl.BlockSpec(memory_space=pltpu.VMEM)] + [ORDER] * 5,
+        out_specs=ORDER,
+        out_shape=jax.ShapeDtypeStruct((count, 6, 8, 128), F32),
+        scratch_shapes=[
+            pltpu.VMEM((2, 128, 512), F32),
+            pltpu.VMEM((3, 512, 256), BF16),
+            pltpu.VMEM((2, 1024, 128), F32),
+            pltpu.VMEM((1024, 512), BF16),
+            pltpu.VMEM(one, I32),
+            pltpu.VMEM(one, F32),
+            pltpu.VMEM(one, F32),
+            pltpu.VMEM(two, F32),
+            pltpu.VMEM(two, F32),
+            pltpu.VMEM((count, 6, 8, 128), F32),
+            pltpu.SemaphoreType.DMA((1,)),
+            pltpu.SemaphoreType.DMA((5, pieces)),
+            pltpu.SemaphoreType.DMA((pieces,)),
         ],
-        out_specs=(
-            pl.BlockSpec((step, 6, 8, 128), lambda i: (i, 0, 0, 0)),
-            pl.BlockSpec((step, 2, 8, 128), lambda i: (i, 0, 0, 0)),
-        ),
-        out_shape=(
-            jax.ShapeDtypeStruct((count, 6, 8, 128), F32),
-            jax.ShapeDtypeStruct((count, 2, 8, 128), F32),
-        ),
-        scratch_shapes=[pltpu.VMEM((3, 512, 256), BF16), pltpu.VMEM((8 * step, 256), F32)],
         compiler_params=params(60),
         cost_estimate=cost(10**9, 8 * MIB),
         name="send",
-    )(current, key, cols, mass, coriolis, start, wind)
+    )(current, blocks, cols, mass, coriolis, start, wind)
 
 
 def velocity_kernel(response, current_ref, _, out, done):
     done[...] = jnp.zeros((8, 128), F32)
-    tall = 8 * GROUP
+    piece = min(response.shape[0], PIECE)
+    tall = 8 * piece
     lane = iota((tall, 128), 1)
 
     def body(g, carry):
-        group = pl.ds(GROUP * g, GROUP)
+        group = pl.ds(piece * g, piece)
         base_east, base_north, a, t = (response[group, n].reshape(tall, 128) for n in range(4))
         current = [current_ref[group, c].reshape(tall, 128) for c in range(2)]
         east, north = respond(a, t, *current, lane)
-        out[0, group] = (base_east + east).reshape(GROUP, 8, 128)
-        out[1, group] = (base_north + north).reshape(GROUP, 8, 128)
+        out[0, group] = (base_east + east).reshape(piece, 8, 128)
+        out[1, group] = (base_north + north).reshape(piece, 8, 128)
         return carry
 
-    lax.fori_loop(0, response.shape[0] // GROUP, body, 0)
-
-
-ORDER = pl.BlockSpec(memory_space=pl.ANY)
+    lax.fori_loop(0, response.shape[0] // piece, body, 0)
 
 
 def velocities(sent, received, after):
@@ -184,7 +229,7 @@
         in_specs=[response, current, ORDER],
         out_specs=(two, pl.BlockSpec((8, 128), lambda i: (0, 0))),
         out_shape=(jax.ShapeDtypeStruct((2, count, 8, 128), F32), jax.ShapeDtypeStruct((8, 128), F32)),
-        compiler_params=params(60),
+        compiler_params=params(50),
         cost_estimate=cost(10**7, 4 * MIB),
         name="velocities",
     )(sent, received, after)
@@ -195,22 +240,23 @@
     hot[...] = jnp.where(iota((512, 8 * count), 0) == key[...], 1.0, 0.0).astype(BF16)
     lane = iota((8, 1024), 1)
     weights = jnp.where(lane // 128 == iota((8, 1024), 0), lane % 128 + 1, 0).astype(F32).astype(BF16)
-    place = iota((128, 128), 0)
+    place = iota((128, 128), 0).astype(F32).astype(BF16)
+    one, zero = jnp.ones((128, 128), BF16), jnp.zeros((128, 128), BF16)
 
     def body(i, carry):
         index = cols[i]
-        target = jnp.where(index >= 0, (index >> 1) + 64 * (index & 1), -1)
-        masks = [
-            jnp.where(place == jnp.broadcast_to(target[s : s + 1], (128, 128)), 1.0, 0.0).astype(BF16)
-            for s in range(8)
-        ]
+        target = jnp.where(index >= 0, (index >> 1) + 64 * (index & 1), -1).astype(F32)
+        masks = []
+        for s in range(8):
+            row = jnp.broadcast_to(target[s : s + 1], (16, 128)).astype(BF16)
+            masks.append(jnp.where(place == jnp.concatenate([row] * 8, axis=0), one, zero))
         found = lax.dot_general(
             weights, jnp.concatenate(masks, axis=1), (((1,), (1,)), ((), ())), preferred_element_type=F32
         )
         inverse[i] = found.astype(I32) - 1
         return carry
 
-    lax.fori_loop(0, count, body, 0, unroll=2)
+    lax.fori_loop(0, count, body, 0, unroll=8)
 
 
 def invert(cols, key):
@@ -224,33 +270,32 @@
     )(cols, key)
 
 
-def stress_kernel(response_in, own_in, inverse_in, hot_in, *refs):
+def stress_kernel(response_in, sent_in, inverse_in, hot_in, *refs):
     planes, side, ends, parts, response, current_ref, inverse, hot, arrived, listed = refs[-10:]
-    groups = inverse.shape[0] // GROUP
-
-    def transfer(g):
-        group = pl.ds(GROUP * g, GROUP)
+    count = inverse.shape[0]
+    piece = min(count, PIECE)
+
+    def transfer(p):
+        span = pl.ds(piece * p, piece)
         return (
-            pltpu.make_async_copy(response_in.at[group, pl.ds(0, 4)], response.at[group], arrived.at[0, g]),
-            pltpu.make_async_copy(own_in.at[group], current_ref.at[group], arrived.at[1, g]),
+            pltpu.make_async_copy(response_in.at[span, pl.ds(0, 4)], response.at[span], arrived.at[0, p]),
+            pltpu.make_async_copy(sent_in.at[span, pl.ds(4, 2)], current_ref.at[span], arrived.at[1, p]),
         )
 
     inverse_copy = pltpu.make_async_copy(inverse_in, inverse, listed.at[0])
     hot_copy = pltpu.make_async_copy(hot_in, hot, listed.at[1])
-    for g in range(groups):
-        for copy in transfer(g):
+    for p in range(count // piece):
+        for copy in transfer(p):
             copy.start()
-        if g == 0:
+        if p == 0:
             inverse_copy.start()
     hot_copy.start()
     inverse_copy.wait()
-    tall = 8 * GROUP
+    tall = 8 * piece
     lane = iota((tall, 128), 1)
 
-    def body(g, carry):
-        for copy in transfer(g):
-            copy.wait()
-        group = pl.ds(GROUP * g, GROUP)
+    def body(g):
+        group = pl.ds(piece * g, piece)
         rows = pl.ds(pl.multiple_of(tall * g, tall), tall)
         base_east, base_north, a, t = (response[group, n].reshape(tall, 128) for n in range(4))
         current = [current_ref[group, c].reshape(tall, 128) for c in range(2)]
@@ -260,14 +305,19 @@
         for c, drag in enumerate((base_east + east - current[0], base_north + north - current[1])):
             drag = DRAG * drag
             got = jnp.concatenate(
-                [lane_gather(drag[8 * i : 8 * i + 8], inside[8 * i : 8 * i + 8]) for i in range(GROUP)], axis=0
+                [lane_gather(drag[8 * i : 8 * i + 8], inside[8 * i : 8 * i + 8]) for i in range(piece)], axis=0
             )
             pieces = split3(jnp.where(index >= 0, got, 0.0))
             for part in range(3):
                 parts[part, rows, 128 * c : 128 * c + 128] = pieces[part]
+
+    def move(p, carry):
+        for copy in transfer(p):
+            copy.wait()
+        body(p)
         return carry
 
-    lax.fori_loop(0, groups, body, 0)
+    lax.fori_loop(0, count // piece, move, 0)
     hot_copy.wait()
     total = dot(hot[...], parts[0]) + dot(hot[...], parts[1]) + dot(hot[...], parts[2])
     lane = iota((ROWS, 128), 1)
@@ -296,7 +346,7 @@
     side[...] = edge
 
 
-def stresses(received, own, inverse, hot, after):
+def stresses(received, sent, inverse, hot, after):
     count = inverse.shape[0]
     inside = pl.BlockSpec(memory_space=pltpu.VMEM)
     shapes = ((2, 4, ROWS, COLS), (ROWS, 128), (2, 4, 8, COLS))
@@ -311,13 +361,13 @@
             pltpu.VMEM((count, 2, 8, 128), F32),
             pltpu.VMEM((count, 8, 128), I32),
             pltpu.VMEM((512, 8 * count), BF16),
-            pltpu.SemaphoreType.DMA((2, count // GROUP)),
+            pltpu.SemaphoreType.DMA((2, count // min(count, PIECE))),
             pltpu.SemaphoreType.DMA((2,)),
         ],
         compiler_params=params(60),
         cost_estimate=cost(10**9, 4 * MIB),
         name="stresses",
-    )(received, own, inverse, hot, *after)
+    )(received, sent, inverse, hot, *after)
 
 
 def widen_kernel(ends, right, left, far_right, far_left, _, out):
@@ -582,16 +632,16 @@
     cols = intersection_cols[0]
     slots = blocks.size
     row, part = blocks >> 2, blocks & 3
-    fetch_key = jnp.where(blocks >= 0, part * 128 + row, -1).reshape(slots, 1)
     scatter_key = jnp.where(blocks >= 0, part * 128 + (row & 1) * 64 + (row >> 1), -1).reshape(1, slots)
-
-    sent, own = send(current, fetch_key, cols, ice_mass[0], coriolis[0], ice_start[:, 0], wind_stress[:, 0])
+    by_slot = jnp.pad(blocks.T, ((0, 0), (0, 128 - blocks.shape[0])), constant_values=-1)
+
+    sent = send(current, by_slot, cols, ice_mass[0], coriolis[0], ice_start[:, 0], wind_stress[:, 0])
     received = exchange(sent)
     planes, left_edge, right_edge, ends = prepare(sea_level, forcing, link_weights, excess, ocean_mask)
     far_right, far_left = from_neighbour(left_edge, 1, 0), from_neighbour(right_edge, -1, 0)
     far_below, far_above = from_neighbour(ends, 0, 1), from_neighbour(ends, 0, -1)
     inverse, hot = invert(cols, scatter_key)
-    stress, side, ends = stresses(received, own, inverse, hot, (far_right, far_left, far_below, far_above))
+    stress, side, ends = stresses(received, sent, inverse, hot, (far_right, far_left, far_below, far_above))
     right, left = from_neighbour(side, 1, 0), from_neighbour(side, -1, 0)
     velocity, done = velocities(sent, received, side)
     rows = widen(ends, right, left, far_right, far_left, done)

time: 105 us -> 102 us (0.971)
  Pallas kernels: 52 us -> 44.2 us
  waiting for transfers between devices: 10.4 us -> 16.4 us
    ppermute x8, waiting for transfers between devices: 10.4 us -> 16.4 us  [from_neighbour(): return lax.ppermute(values, AXES, pairs)]
    pallas_call x1, Pallas kernels: 18.7 us -> 12.8 us  [invert(): pl.pallas_call(invert_kernel, out_shape=(jax.ShapeDtypeStruct((count, 8,...]
    select_n x2 -> x0, local copies, waits for them, and re-layouts: 1.08 us -> none  [local(): fetch_key = jnp.where(blocks >= 0, part * 128 + row, -1).reshape(slots, 1)]
  transfers between devices with their start and end apart: 9 -> 9, of which waited for: 2 -> 3; matrix products, arithmetic and copies ran while one was open for 1% -> 1% of each run, Pallas kernels for 31% -> 26%
where the time goes in v4:
time: 102 us; the launch traced here: 101 us
  Pallas kernels  44.2 us (43%)
  starting transfers between devices  37.5 us (37%)
  waiting for transfers between devices  16.4 us (16%)
  local copies, waits for them, and re-layouts  2.51 us (2%)
    ppermute x8, starting transfers between devices, from_neighbour(): return lax.ppermute(values, AXES, pairs)  25.6 us
    ppermute x8, waiting for transfers between devices, from_neighbour(): return lax.ppermute(values, AXES, pairs)  16.4 us
    pallas_call x1, Pallas kernels, invert(): pl.pallas_call(invert_kernel, out_shape=(jax.ShapeDtypeStruct((count, 8,...  12.8 us
    all_to_all x1, starting transfers between devices, exchange(): return lax.all_to_all(values, AXES, split_axis=0, concat_axis=0, tiled=True)  11.9 us
    pallas_call x1, Pallas kernels, prepare(): pl.pallas_call(prepare_kernel, out_shape=(jax.ShapeDtypeStruct((ARRAYS, 4...  8.89 us
    pallas_call x1, Pallas kernels, send(): pl.pallas_call(send_kernel, in_specs=[ORDER, pl.BlockSpec(memory_space=pl...  8.12 us
    pallas_call x1, Pallas kernels, stresses(): pl.pallas_call(stress_kernel, in_specs=[ORDER] * (4 + len(after)), out_sp...  6.42 us
    pallas_call x1, Pallas kernels, velocities(): pl.pallas_call(velocity_kernel, grid=(grid,), in_specs=[response, current...  3.59 us
  transfers between devices with their start and end apart: 9, of which 3 were waited for; matrix products, arithmetic and copies ran while one was open for 1% of the time, Pallas kernels for 26%

profile of v4, /device:TPU:1, one launch (start us, length us, event | category | flops | bytes accessed | tf_op | source)
XLA Modules:
  0.0 101.3 jit_solution(11653594798956596353)
XLA Ops:
  0.6 8.1 %send.1.sent_in.response = f32[128,6,8,128]{3,2,1,0:T(8,128)} custom-call(f32[2,128,512]{2,1,0:T(8,128)} %current_in.1, s32[8,128]{1,0:T(8,128)} %bitcast.17, s32[128,8,128]{2,1,0:T(8,128)} %bitcast.15, f32[128,8,128]{2,1,0:T(8,128)} %bitcast.13, f32[128,8,128]{2,1,0:T(8,128)} %bitcast.14, f32[2,128,8,128]{3,2,1,0:T(8,128)} %bitcast.11, ...), custom_call_target="tpu_custom_call" | custom-call | flops 1000000000 | bytes 8388608 | tf_op jit(solution)/shard_map/send/pallas_call | solution.py:179
  8.8 11.9 %all-to-all-start = ((f32[128,6,8,128]{3,2,1,0:T(8,128)}), f32[128,6,8,128]{3,2,1,0:T(8,128)}, u32[]{:S(2)}, u32[]{:S(2)}) async-start(f32[128,6,8,128]{3,2,1,0:T(8,128)} %send.1.sent_in.response), calls=%async_computation | async-start | bytes 6291456 | tf_op jit(solution)/shard_map/all_to_all | solution.py:603
  20.7 8.9 %prepare.1 = (f32[11,4,64,256]{3,2,1,0:T(8,128)}, f32[2,64,256]{2,1,0:T(8,128)}, f32[2,64,256]{2,1,0:T(8,128)}, f32[11,4,8,256]{3,2,1,0:T(8,128)}) custom-call(f32[128,512]{1,0:T(8,128)} %sea.1, f32[128,512]{1,0:T(8,128)} %forcing.1, f32[8,128,512]{2,1,0:T(8,128)} %weights.1, f32[128,512]{1,0:T(8,128)} %excess.1, s32[128,512]{1,0:T(8,128)} %mask.1), custom_call_target="tpu_custom_call" | custom-call | flops 10000000 | bytes 7340032 | tf_op jit(solution)/shard_map/prepare/pallas_call | solution.py:461
  29.6 3.5 %collective-permute-start.3 = (f32[11,4,8,256]{3,2,1,0:T(8,128)}, f32[11,4,8,256]{3,2,1,0:T(8,128)S(1)}, u32[]{:S(2)}, u32[]{:S(2)}) collective-permute-start(f32[11,4,8,256]{3,2,1,0:T(8,128)} %get-tuple-element.18), channel_id=1, source_target_pairs={{0,1},{1,2},{2,3},{4,5},{5,6},{6,7},{8,9},{9,10},{10,11},{12,13},{... | collective-permute-start | bytes 1081352 | tf_op jit(solution)/shard_map/ppermute | solution.py:614
  33.1 1.9 %collective-permute-start.2 = (f32[11,4,8,256]{3,2,1,0:T(8,128)}, f32[11,4,8,256]{3,2,1,0:T(8,128)S(1)}, u32[]{:S(2)}, u32[]{:S(2)}) collective-permute-start(f32[11,4,8,256]{3,2,1,0:T(8,128)} %get-tuple-element.18), channel_id=1, source_target_pairs={{1,0},{2,1},{3,2},{5,4},{6,5},{7,6},{9,8},{10,9},{11,10},{13,12},{... | collective-permute-start | bytes 1081352 | tf_op jit(solution)/shard_map/ppermute | solution.py:614
  35.0 7.6 %collective-permute-start = (f32[2,64,256]{2,1,0:T(8,128)}, f32[2,64,256]{2,1,0:T(8,128)S(1)}, u32[]{:S(2)}, u32[]{:S(2)}) collective-permute-start(f32[2,64,256]{2,1,0:T(8,128)} %get-tuple-element.14), channel_id=1, source_target_pairs={{4,0},{5,1},{6,2},{7,3},{8,4},{9,5},{10,6},{11,7},{12,8},{13,9},{1... | collective-permute-start | bytes 393224 | tf_op jit(solution)/shard_map/ppermute | solution.py:614
  42.6 0.1 copy.16
  42.7 0.7 reshape.71.key
  43.4 12.8 %invert.1 = (s32[128,8,128]{2,1,0:T(8,128)}, bf16[512,1024]{1,0:T(8,128)(2,1)}) custom-call(s32[128,8,128]{2,1,0:T(8,128)} %bitcast.16, s32[1,1024]{1,0:T(1,128)} %reshape.71.key), custom_call_target="tpu_custom_call" | custom-call | flops 10000000000 | bytes 2097152 | tf_op jit(solution)/shard_map/invert/pallas_call | solution.py:264
  56.2 4.4 %collective-permute-done.refs_0_.far_right.right = f32[2,64,256]{2,1,0:T(8,128)S(1)} collective-permute-done((f32[2,64,256]{2,1,0:T(8,128)}, f32[2,64,256]{2,1,0:T(8,128)S(1)}, u32[]{:S(2)}, u32[]{:S(2)}) %collective-permute-start) | collective-permute-done | bytes 131104 | tf_op jit(solution)/shard_map/ppermute | solution.py:614
  60.6 8.3 %collective-permute-done.1.refs_1_.far_left.left = f32[2,64,256]{2,1,0:T(8,128)S(1)} collective-permute-done((f32[2,64,256]{2,1,0:T(8,128)}, f32[2,64,256]{2,1,0:T(8,128)S(1)}, u32[]{:S(2)}, u32[]{:S(2)}) %collective-permute-start.1) | collective-permute-done | bytes 131104 | tf_op jit(solution)/shard_map/ppermute | solution.py:614
  69.0 0.6 copy-done.8
  69.6 0.2 copy-done.2
  69.8 0.1 copy-done.4
  69.8 6.4 %stresses.1 = (f32[2,4,64,256]{3,2,1,0:T(8,128)}, f32[64,128]{1,0:T(8,128)}, f32[2,4,8,256]{3,2,1,0:T(8,128)}) custom-call(f32[128,6,8,128]{3,2,1,0:T(8,128)} %all-to-all-done.response_in.current_ref, f32[128,6,8,128]{3,2,1,0:T(8,128)} %send.1.sent_in.response, s32[128,8,128]{2,1,0:T(8,128)} %get-tuple-element.16.inverse_in, ...), custom_call_target="tpu_custom_call" | custom-call | flops 1000000000 | bytes 4194304 | tf_op jit(solution)/shard_map/stresses/pallas_call | solution.py:353
  76.4 7.2 %collective-permute-start.4 = (f32[64,128]{1,0:T(8,128)}, f32[64,128]{1,0:T(8,128)S(1)}, u32[]{:S(2)}, u32[]{:S(2)}) collective-permute-start(f32[64,128]{1,0:T(8,128)} %get-tuple-element.20._), channel_id=1, source_target_pairs={{4,0},{5,1},{6,2},{7,3},{8,4},{9,5},{10,6},{11,7},{12,8},{13,9},{1... | collective-permute-start | bytes 98312 | tf_op jit(solution)/shard_map/ppermute | solution.py:614
  83.6 0.8 copy-done.12
  84.4 3.6 %velocities.1 = (f32[2,128,8,128]{3,2,1,0:T(8,128)}, f32[8,128]{1,0:T(8,128)S(1)}) custom-call(f32[128,6,8,128]{3,2,1,0:T(8,128)S(1)} %copy-done, f32[128,6,8,128]{3,2,1,0:T(8,128)} %all-to-all-done.response_in.current_ref, f32[64,128]{1,0:T(8,128)S(1)} %copy-done.12), custom_call_target="tpu_custom_call" | custom-call | flops 10000000 | bytes 4194304 | tf_op jit(solution)/shard_map/velocities/pallas_call | solution.py:226
  88.0 0.1 widen.1._
  88.1 3.3 %collective-permute-start.7 = (f32[12,8,384]{2,1,0:T(8,128)S(1)}, f32[12,8,384]{2,1,0:T(8,128)S(1)}, u32[]{:S(2)}, u32[]{:S(2)}) collective-permute-start(f32[12,8,384]{2,1,0:T(8,128)S(1)} %widen.1._), channel_id=1, source_target_pairs={{0,1},{1,2},{2,3},{4,5},{5,6},{6,7},{8,9},{9,10},{10,11},{12,13},{... | collective-permute-start | bytes 442376 | tf_op jit(solution)/shard_map/ppermute | solution.py:614
  91.4 1.9 %collective-permute-start.6 = (f32[12,8,384]{2,1,0:T(8,128)S(1)}, f32[12,8,384]{2,1,0:T(8,128)S(1)}, u32[]{:S(2)}, u32[]{:S(2)}) collective-permute-start(f32[12,8,384]{2,1,0:T(8,128)S(1)} %widen.1._), channel_id=1, source_target_pairs={{1,0},{2,1},{3,2},{5,4},{6,5},{7,6},{9,8},{10,9},{11,10},{13,12},{... | collective-permute-start | bytes 442376 | tf_op jit(solution)/shard_map/ppermute | solution.py:614
  93.4 0.9 extend.1.operator
  94.3 3.6 %collective-permute-done.6.below = f32[12,8,384]{2,1,0:T(8,128)S(1)} collective-permute-done((f32[12,8,384]{2,1,0:T(8,128)S(1)}, f32[12,8,384]{2,1,0:T(8,128)S(1)}, u32[]{:S(2)}, u32[]{:S(2)}) %collective-permute-start.6) | collective-permute-done | bytes 147488 | tf_op jit(solution)/shard_map/ppermute | solution.py:614
  97.9 3.4 %sweep.1 = f32[128,512]{1,0:T(8,128)} custom-call(f32[11,4,64,384]{3,2,1,0:T(8,128)S(1)} %extend.1.operator, f32[11,4,8,256]{3,2,1,0:T(8,128)S(1)} %copy-done.5, f32[11,4,8,256]{3,2,1,0:T(8,128)S(1)} %copy-done.3, f32[2,4,64,256]{3,2,1,0:T(8,128)S(1)} %copy-done.10, f32[64,128]{1,0:T(8,128)S(1)} %collective-permute-done.4.right, ...), custom_call_target="tpu_custom_call" | custom-call | flops 100000000 | bytes 6291456 | tf_op jit(solution)/shard_map/sweep/pallas_call | solution.py:583
  (33 shorter events, 0.2 us)
Async XLA Ops:
  8.8 60.2 %all-to-all-start = ((f32[128,6,8,128]{3,2,1,0:T(8,128)}), f32[128,6,8,128]{3,2,1,0:T(8,128)}, u32[]{:S(2)}, u32[]{:S(2)}) async-start(f32[128,6,8,128]{3,2,1,0:T(8,128)} %send.1.sent_in.response), calls=%async_computation | async-start | bytes 6291456 | tf_op jit(solution)/shard_map/all_to_all | solution.py:603
  20.7 22.0 %copy-start.13 = (s32[1,128,8]{1,2,0:T(8,128)S(1)}, s32[1,128,8]{1,2,0:T(8,128)}, u32[]{:S(2)}) copy-start(s32[1,128,8]{1,2,0:T(8,128)} %param.18) | copy-start | bytes 12292
  29.6 39.4 %collective-permute-start.3 = (f32[11,4,8,256]{3,2,1,0:T(8,128)}, f32[11,4,8,256]{3,2,1,0:T(8,128)S(1)}, u32[]{:S(2)}, u32[]{:S(2)}) collective-permute-start(f32[11,4,8,256]{3,2,1,0:T(8,128)} %get-tuple-element.18), channel_id=1, source_target_pairs={{0,1},{1,2},{2,3},{4,5},{5,6},{6,7},{8,9},{9,10},{10,11},{12,13},{... | collective-permute-start | bytes 1081352 | tf_op jit(solution)/shard_map/ppermute | solution.py:614
  33.1 35.8 %collective-permute-start.2 = (f32[11,4,8,256]{3,2,1,0:T(8,128)}, f32[11,4,8,256]{3,2,1,0:T(8,128)S(1)}, u32[]{:S(2)}, u32[]{:S(2)}) collective-permute-start(f32[11,4,8,256]{3,2,1,0:T(8,128)} %get-tuple-element.18), channel_id=1, source_target_pairs={{1,0},{2,1},{3,2},{5,4},{6,5},{7,6},{9,8},{10,9},{11,10},{13,12},{... | collective-permute-start | bytes 1081352 | tf_op jit(solution)/shard_map/ppermute | solution.py:614
  35.0 25.6 %collective-permute-start = (f32[2,64,256]{2,1,0:T(8,128)}, f32[2,64,256]{2,1,0:T(8,128)S(1)}, u32[]{:S(2)}, u32[]{:S(2)}) collective-permute-start(f32[2,64,256]{2,1,0:T(8,128)} %get-tuple-element.14), channel_id=1, source_target_pairs={{4,0},{5,1},{6,2},{7,3},{8,4},{9,5},{10,6},{11,7},{12,8},{13,9},{1... | collective-permute-start | bytes 393224 | tf_op jit(solution)/shard_map/ppermute | solution.py:614
  42.6 26.3 %collective-permute-start.1 = (f32[2,64,256]{2,1,0:T(8,128)}, f32[2,64,256]{2,1,0:T(8,128)S(1)}, u32[]{:S(2)}, u32[]{:S(2)}) collective-permute-start(f32[2,64,256]{2,1,0:T(8,128)} %get-tuple-element.15), channel_id=1, source_target_pairs={{124,0},{125,1},{126,2},{127,3},{0,4},{1,5},{2,6},{3,7},{4,8},{5,9... | collective-permute-start | bytes 393224 | tf_op jit(solution)/shard_map/ppermute | solution.py:614
  60.6 8.4 %copy-start.6 = (f32[2,64,256]{2,1,0:T(8,128)}, f32[2,64,256]{2,1,0:T(8,128)S(1)}, u32[]{:S(2)}) copy-start(f32[2,64,256]{2,1,0:T(8,128)S(1)} %collective-permute-done.refs_0_.far_right.right) | copy-start | bytes 393220
  68.9 0.6 copy-start.8
  68.9 0.8 copy-start.2
  68.9 0.9 copy-start.4
  69.8 13.7 %copy-start = (f32[128,6,8,128]{3,2,1,0:T(8,128)S(1)}, f32[128,6,8,128]{3,2,1,0:T(8,128)}, u32[]{:S(2)}) copy-start(f32[128,6,8,128]{3,2,1,0:T(8,128)} %send.1.sent_in.response) | copy-start | bytes 9437188
  76.3 11.7 %copy-start.7 = (f32[2,64,256]{2,1,0:T(8,128)S(1)}, f32[2,64,256]{2,1,0:T(8,128)}, u32[]{:S(2)}) copy-start(f32[2,64,256]{2,1,0:T(8,128)} %copy-done.6) | copy-start | bytes 393220
  76.3 11.7 %copy-start.9 = (f32[2,64,256]{2,1,0:T(8,128)S(1)}, f32[2,64,256]{2,1,0:T(8,128)}, u32[]{:S(2)}) copy-start(f32[2,64,256]{2,1,0:T(8,128)} %copy-done.8) | copy-start | bytes 393220
  76.3 11.7 %copy-start.11 = (f32[2,4,8,256]{3,2,1,0:T(8,128)S(1)}, f32[2,4,8,256]{3,2,1,0:T(8,128)}, u32[]{:S(2)}) copy-start(f32[2,4,8,256]{3,2,1,0:T(8,128)} %get-tuple-element.19.ends) | copy-start | bytes 196612
  76.3 17.1 %copy-start.1 = (f32[11,4,64,256]{3,2,1,0:T(8,128)S(1)}, f32[11,4,64,256]{3,2,1,0:T(8,128)}, u32[]{:S(2)}) copy-start(f32[11,4,64,256]{3,2,1,0:T(8,128)} %get-tuple-element.13.planes) | copy-start | bytes 8650756
  76.3 11.6 %collective-permute-start.5 = (f32[64,128]{1,0:T(8,128)}, f32[64,128]{1,0:T(8,128)S(1)}, u32[]{:S(2)}, u32[]{:S(2)}) collective-permute-start(f32[64,128]{1,0:T(8,128)} %get-tuple-element.20._), channel_id=1, source_target_pairs={{124,0},{125,1},{126,2},{127,3},{0,4},{1,5},{2,6},{3,7},{4,8},{5,9... | collective-permute-start | bytes 98312 | tf_op jit(solution)/shard_map/ppermute | solution.py:614
  76.4 11.6 %collective-permute-start.4 = (f32[64,128]{1,0:T(8,128)}, f32[64,128]{1,0:T(8,128)S(1)}, u32[]{:S(2)}, u32[]{:S(2)}) collective-permute-start(f32[64,128]{1,0:T(8,128)} %get-tuple-element.20._), channel_id=1, source_target_pairs={{4,0},{5,1},{6,2},{7,3},{8,4},{9,5},{10,6},{11,7},{12,8},{13,9},{1... | collective-permute-start | bytes 98312 | tf_op jit(solution)/shard_map/ppermute | solution.py:614
  83.6 0.8 copy-start.12
  88.1 6.2 %collective-permute-start.7 = (f32[12,8,384]{2,1,0:T(8,128)S(1)}, f32[12,8,384]{2,1,0:T(8,128)S(1)}, u32[]{:S(2)}, u32[]{:S(2)}) collective-permute-start(f32[12,8,384]{2,1,0:T(8,128)S(1)} %widen.1._), channel_id=1, source_target_pairs={{0,1},{1,2},{2,3},{4,5},{5,6},{6,7},{8,9},{9,10},{10,11},{12,13},{... | collective-permute-start | bytes 442376 | tf_op jit(solution)/shard_map/ppermute | solution.py:614
  91.4 6.5 %collective-permute-start.6 = (f32[12,8,384]{2,1,0:T(8,128)S(1)}, f32[12,8,384]{2,1,0:T(8,128)S(1)}, u32[]{:S(2)}, u32[]{:S(2)}) collective-permute-start(f32[12,8,384]{2,1,0:T(8,128)S(1)} %widen.1._), channel_id=1, source_target_pairs={{1,0},{2,1},{3,2},{5,4},{6,5},{7,6},{9,8},{10,9},{11,10},{13,12},{... | collective-permute-start | bytes 442376 | tf_op jit(solution)/shard_map/ppermute | solution.py:614
  93.4 4.5 %copy-start.3 = (f32[11,4,8,256]{3,2,1,0:T(8,128)S(1)}, f32[11,4,8,256]{3,2,1,0:T(8,128)}, u32[]{:S(2)}) copy-start(f32[11,4,8,256]{3,2,1,0:T(8,128)} %copy-done.2) | copy-start | bytes 1081348
  93.4 4.5 %copy-start.5 = (f32[11,4,8,256]{3,2,1,0:T(8,128)S(1)}, f32[11,4,8,256]{3,2,1,0:T(8,128)}, u32[]{:S(2)}) copy-start(f32[11,4,8,256]{3,2,1,0:T(8,128)} %copy-done.4) | copy-start | bytes 1081348
  93.4 4.5 %copy-start.10 = (f32[2,4,64,256]{3,2,1,0:T(8,128)S(1)}, f32[2,4,64,256]{3,2,1,0:T(8,128)}, u32[]{:S(2)}) copy-start(f32[2,4,64,256]{3,2,1,0:T(8,128)} %get-tuple-element.22.stress) | copy-start | bytes 1572868

commit v5 on v4

--- a/solution.py
+++ b/solution.py
@@ -641,7 +641,7 @@
     far_right, far_left = from_neighbour(left_edge, 1, 0), from_neighbour(right_edge, -1, 0)
     far_below, far_above = from_neighbour(ends, 0, 1), from_neighbour(ends, 0, -1)
     inverse, hot = invert(cols, scatter_key)
-    stress, side, ends = stresses(received, sent, inverse, hot, (far_right, far_left, far_below, far_above))
+    stress, side, ends = stresses(received, sent, inverse, hot, (left_edge,))
     right, left = from_neighbour(side, 1, 0), from_neighbour(side, -1, 0)
     velocity, done = velocities(sent, received, side)
     rows = widen(ends, right, left, far_right, far_left, done)

time: 102 us -> 94.8 us (0.929)
  waiting for transfers between devices: 16.4 us -> 9.75 us
    ppermute x8, waiting for transfers between devices: 16.4 us -> 4.12 us  [from_neighbour(): return lax.ppermute(values, AXES, pairs)]
    all_to_all x1, waiting for transfers between devices: 0.01 us -> 5.63 us  [exchange(): return lax.all_to_all(values, AXES, split_axis=0, concat_axis=0, tiled=True)]
  transfers between devices with their start and end apart: 9 -> 9, of which waited for: 3 -> 3; matrix products, arithmetic and copies ran while one was open for 1% -> 1% of each run, Pallas kernels for 26% -> 35%
where the time goes in v5:
time: 94.8 us; the launch traced here: 94.3 us
  Pallas kernels  44.2 us (47%)
  starting transfers between devices  38 us (40%)
  waiting for transfers between devices  9.75 us (10%)
  local copies, waits for them, and re-layouts  1.61 us (2%)
    ppermute x8, starting transfers between devices, from_neighbour(): return lax.ppermute(values, AXES, pairs)  26.1 us
    pallas_call x1, Pallas kernels, invert(): pl.pallas_call(invert_kernel, out_shape=(jax.ShapeDtypeStruct((count, 8,...  12.7 us
    all_to_all x1, starting transfers between devices, exchange(): return lax.all_to_all(values, AXES, split_axis=0, concat_axis=0, tiled=True)  11.9 us
    pallas_call x1, Pallas kernels, prepare(): pl.pallas_call(prepare_kernel, out_shape=(jax.ShapeDtypeStruct((ARRAYS, 4...  8.89 us
    pallas_call x1, Pallas kernels, send(): pl.pallas_call(send_kernel, in_specs=[ORDER, pl.BlockSpec(memory_space=pl...  8.13 us
    pallas_call x1, Pallas kernels, stresses(): pl.pallas_call(stress_kernel, in_specs=[ORDER] * (4 + len(after)), out_sp...  6.44 us
    all_to_all x1, waiting for transfers between devices, exchange(): return lax.all_to_all(values, AXES, split_axis=0, concat_axis=0, tiled=True)  5.63 us
    ppermute x8, waiting for transfers between devices, from_neighbour(): return lax.ppermute(values, AXES, pairs)  4.12 us
  transfers between devices with their start and end apart: 9, of which 3 were waited for; matrix products, arithmetic and copies ran while one was open for 1% of the time, Pallas kernels for 35%

profile of v5, /device:TPU:1, one launch (start us, length us, event | category | flops | bytes accessed | tf_op | source)
XLA Modules:
  0.0 94.3 jit_solution(7510373367450525411)
XLA Ops:
  0.6 8.1 %send.1.sent_in.response = f32[128,6,8,128]{3,2,1,0:T(8,128)} custom-call(f32[2,128,512]{2,1,0:T(8,128)} %current_in.1, s32[8,128]{1,0:T(8,128)} %bitcast.17, s32[128,8,128]{2,1,0:T(8,128)} %bitcast.15, f32[128,8,128]{2,1,0:T(8,128)} %bitcast.13, f32[128,8,128]{2,1,0:T(8,128)} %bitcast.14, f32[2,128,8,128]{3,2,1,0:T(8,128)} %bitcast.11, ...), custom_call_target="tpu_custom_call" | custom-call | flops 1000000000 | bytes 8388608 | tf_op jit(solution)/shard_map/send/pallas_call | solution.py:179
  8.8 11.9 %all-to-all-start = ((f32[128,6,8,128]{3,2,1,0:T(8,128)}), f32[128,6,8,128]{3,2,1,0:T(8,128)}, u32[]{:S(2)}, u32[]{:S(2)}) async-start(f32[128,6,8,128]{3,2,1,0:T(8,128)} %send.1.sent_in.response), calls=%async_computation | async-start | bytes 6291456 | tf_op jit(solution)/shard_map/all_to_all | solution.py:603
  20.7 0.0 copy-start.5
  20.7 8.9 %prepare.1 = (f32[11,4,64,256]{3,2,1,0:T(8,128)}, f32[2,64,256]{2,1,0:T(8,128)}, f32[2,64,256]{2,1,0:T(8,128)}, f32[11,4,8,256]{3,2,1,0:T(8,128)}) custom-call(f32[128,512]{1,0:T(8,128)} %sea.1, f32[128,512]{1,0:T(8,128)} %forcing.1, f32[8,128,512]{2,1,0:T(8,128)} %weights.1, f32[128,512]{1,0:T(8,128)} %excess.1, s32[128,512]{1,0:T(8,128)} %mask.1), custom_call_target="tpu_custom_call" | custom-call | flops 10000000 | bytes 7340032 | tf_op jit(solution)/shard_map/prepare/pallas_call | solution.py:461
  29.6 3.5 %collective-permute-start.5 = (f32[11,4,8,256]{3,2,1,0:T(8,128)}, f32[11,4,8,256]{3,2,1,0:T(8,128)S(1)}, u32[]{:S(2)}, u32[]{:S(2)}) collective-permute-start(f32[11,4,8,256]{3,2,1,0:T(8,128)} %get-tuple-element.21), channel_id=1, source_target_pairs={{0,1},{1,2},{2,3},{4,5},{5,6},{6,7},{8,9},{9,10},{10,11},{12,13},{... | collective-permute-start | bytes 1081352 | tf_op jit(solution)/shard_map/ppermute | solution.py:614
  33.1 1.9 %collective-permute-start.4 = (f32[11,4,8,256]{3,2,1,0:T(8,128)}, f32[11,4,8,256]{3,2,1,0:T(8,128)S(1)}, u32[]{:S(2)}, u32[]{:S(2)}) collective-permute-start(f32[11,4,8,256]{3,2,1,0:T(8,128)} %get-tuple-element.21), channel_id=1, source_target_pairs={{1,0},{2,1},{3,2},{5,4},{6,5},{7,6},{9,8},{10,9},{11,10},{13,12},{... | collective-permute-start | bytes 1081352 | tf_op jit(solution)/shard_map/ppermute | solution.py:614
  35.0 1.3 %collective-permute-start.1 = (f32[2,64,256]{2,1,0:T(8,128)}, f32[2,64,256]{2,1,0:T(8,128)S(1)}, u32[]{:S(2)}, u32[]{:S(2)}) collective-permute-start(f32[2,64,256]{2,1,0:T(8,128)} %get-tuple-element.15), channel_id=1, source_target_pairs={{124,0},{125,1},{126,2},{127,3},{0,4},{1,5},{2,6},{3,7},{4,8},{5,9... | collective-permute-start | bytes 393224 | tf_op jit(solution)/shard_map/ppermute | solution.py:614
  36.3 6.4 %collective-permute-start = (f32[2,64,256]{2,1,0:T(8,128)}, f32[2,64,256]{2,1,0:T(8,128)S(1)}, u32[]{:S(2)}, u32[]{:S(2)}) collective-permute-start(f32[2,64,256]{2,1,0:T(8,128)} %get-tuple-element.14.refs_0_), channel_id=1, source_target_pairs={{4,0},{5,1},{6,2},{7,3},{8,4},{9,5},{10,6},{11,7},{12,8},{13,9},{1... | collective-permute-start | bytes 393224 | tf_op jit(solution)/shard_map/ppermute | solution.py:614
  42.7 0.1 copy.16
  42.8 0.7 reshape.71.key
  43.5 12.7 %invert.1 = (s32[128,8,128]{2,1,0:T(8,128)}, bf16[512,1024]{1,0:T(8,128)(2,1)}) custom-call(s32[128,8,128]{2,1,0:T(8,128)} %bitcast.16, s32[1,1024]{1,0:T(1,128)} %reshape.71.key), custom_call_target="tpu_custom_call" | custom-call | flops 10000000000 | bytes 2097152 | tf_op jit(solution)/shard_map/invert/pallas_call | solution.py:264
  56.3 5.6 %all-to-all-done.response_in.current_ref = f32[128,6,8,128]{3,2,1,0:T(8,128)} async-done(((f32[128,6,8,128]{3,2,1,0:T(8,128)}), f32[128,6,8,128]{3,2,1,0:T(8,128)}, u32[]{:S(2)}, u32[]{:S(2)}) %all-to-all-start) | async-done | bytes 3145760 | tf_op jit(solution)/shard_map/all_to_all | solution.py:603
  61.9 6.4 %stresses.1 = (f32[2,4,64,256]{3,2,1,0:T(8,128)}, f32[64,128]{1,0:T(8,128)}, f32[2,4,8,256]{3,2,1,0:T(8,128)}) custom-call(f32[128,6,8,128]{3,2,1,0:T(8,128)} %all-to-all-done.response_in.current_ref, f32[128,6,8,128]{3,2,1,0:T(8,128)} %send.1.sent_in.response, s32[128,8,128]{2,1,0:T(8,128)} %get-tuple-element.16.inverse_in, ...), custom_call_target="tpu_custom_call" | custom-call | flops 1000000000 | bytes 4194304 | tf_op jit(solution)/shard_map/stresses/pallas_call | solution.py:353
  68.4 0.1 collective-permute-start.3
  68.4 0.5 collective-permute-done.1.far_left.left
  68.9 6.7 %collective-permute-start.2 = (f32[64,128]{1,0:T(8,128)}, f32[64,128]{1,0:T(8,128)S(1)}, u32[]{:S(2)}, u32[]{:S(2)}) collective-permute-start(f32[64,128]{1,0:T(8,128)} %get-tuple-element.19._), channel_id=1, source_target_pairs={{4,0},{5,1},{6,2},{7,3},{8,4},{9,5},{10,6},{11,7},{12,8},{13,9},{1... | collective-permute-start | bytes 98312 | tf_op jit(solution)/shard_map/ppermute | solution.py:614
  75.6 0.8 copy-done.4
  76.4 3.6 %velocities.1 = (f32[2,128,8,128]{3,2,1,0:T(8,128)}, f32[8,128]{1,0:T(8,128)S(1)}) custom-call(f32[128,6,8,128]{3,2,1,0:T(8,128)S(1)} %copy-done, f32[128,6,8,128]{3,2,1,0:T(8,128)} %all-to-all-done.response_in.current_ref, f32[64,128]{1,0:T(8,128)S(1)} %copy-done.4), custom_call_target="tpu_custom_call" | custom-call | flops 10000000 | bytes 4194304 | tf_op jit(solution)/shard_map/velocities/pallas_call | solution.py:226
  80.0 0.1 widen.1._
  80.1 4.3 %collective-permute-start.7 = (f32[12,8,384]{2,1,0:T(8,128)S(1)}, f32[12,8,384]{2,1,0:T(8,128)S(1)}, u32[]{:S(2)}, u32[]{:S(2)}) collective-permute-start(f32[12,8,384]{2,1,0:T(8,128)S(1)} %widen.1._), channel_id=1, source_target_pairs={{0,1},{1,2},{2,3},{4,5},{5,6},{6,7},{8,9},{9,10},{10,11},{12,13},{... | collective-permute-start | bytes 442376 | tf_op jit(solution)/shard_map/ppermute | solution.py:614
  84.4 1.9 %collective-permute-start.6 = (f32[12,8,384]{2,1,0:T(8,128)S(1)}, f32[12,8,384]{2,1,0:T(8,128)S(1)}, u32[]{:S(2)}, u32[]{:S(2)}) collective-permute-start(f32[12,8,384]{2,1,0:T(8,128)S(1)} %widen.1._), channel_id=1, source_target_pairs={{1,0},{2,1},{3,2},{5,4},{6,5},{7,6},{9,8},{10,9},{11,10},{13,12},{... | collective-permute-start | bytes 442376 | tf_op jit(solution)/shard_map/ppermute | solution.py:614
  86.4 0.9 extend.1.operator
  87.3 3.6 %collective-permute-done.6.below = f32[12,8,384]{2,1,0:T(8,128)S(1)} collective-permute-done((f32[12,8,384]{2,1,0:T(8,128)S(1)}, f32[12,8,384]{2,1,0:T(8,128)S(1)}, u32[]{:S(2)}, u32[]{:S(2)}) %collective-permute-start.6) | collective-permute-done | bytes 147488 | tf_op jit(solution)/shard_map/ppermute | solution.py:614
  90.9 3.4 %sweep.1 = f32[128,512]{1,0:T(8,128)} custom-call(f32[11,4,64,384]{3,2,1,0:T(8,128)S(1)} %extend.1.operator, f32[11,4,8,256]{3,2,1,0:T(8,128)S(1)} %collective-permute-done.4.far_below, f32[11,4,8,256]{3,2,1,0:T(8,128)S(1)} %collective-permute-done.5.far_above, f32[2,4,64,256]{3,2,1,0:T(8,128)S(1)} %copy-done.2, f32[64,128]{1,0:T(8,128)S(1)} %collective-permute-done.2.right, ...), custom_call_target="tpu_custom_call" | custom-call | flops 100000000 | bytes 6291456 | tf_op jit(solution)/shard_map/sweep/pallas_call | solution.py:583
  (17 shorter events, 0.0 us)
Async XLA Ops:
  8.8 53.1 %all-to-all-start = ((f32[128,6,8,128]{3,2,1,0:T(8,128)}), f32[128,6,8,128]{3,2,1,0:T(8,128)}, u32[]{:S(2)}, u32[]{:S(2)}) async-start(f32[128,6,8,128]{3,2,1,0:T(8,128)} %send.1.sent_in.response), calls=%async_computation | async-start | bytes 6291456 | tf_op jit(solution)/shard_map/all_to_all | solution.py:603
  20.7 22.0 %copy-start.5 = (s32[1,128,8]{1,2,0:T(8,128)S(1)}, s32[1,128,8]{1,2,0:T(8,128)}, u32[]{:S(2)}) copy-start(s32[1,128,8]{1,2,0:T(8,128)} %param.18) | copy-start | bytes 12292
  29.6 57.7 %collective-permute-start.5 = (f32[11,4,8,256]{3,2,1,0:T(8,128)}, f32[11,4,8,256]{3,2,1,0:T(8,128)S(1)}, u32[]{:S(2)}, u32[]{:S(2)}) collective-permute-start(f32[11,4,8,256]{3,2,1,0:T(8,128)} %get-tuple-element.21), channel_id=1, source_target_pairs={{0,1},{1,2},{2,3},{4,5},{5,6},{6,7},{8,9},{9,10},{10,11},{12,13},{... | collective-permute-start | bytes 1081352 | tf_op jit(solution)/shard_map/ppermute | solution.py:614
  33.1 54.1 %collective-permute-start.4 = (f32[11,4,8,256]{3,2,1,0:T(8,128)}, f32[11,4,8,256]{3,2,1,0:T(8,128)S(1)}, u32[]{:S(2)}, u32[]{:S(2)}) collective-permute-start(f32[11,4,8,256]{3,2,1,0:T(8,128)} %get-tuple-element.21), channel_id=1, source_target_pairs={{1,0},{2,1},{3,2},{5,4},{6,5},{7,6},{9,8},{10,9},{11,10},{13,12},{... | collective-permute-start | bytes 1081352 | tf_op jit(solution)/shard_map/ppermute | solution.py:614
  35.0 33.9 %collective-permute-start.1 = (f32[2,64,256]{2,1,0:T(8,128)}, f32[2,64,256]{2,1,0:T(8,128)S(1)}, u32[]{:S(2)}, u32[]{:S(2)}) collective-permute-start(f32[2,64,256]{2,1,0:T(8,128)} %get-tuple-element.15), channel_id=1, source_target_pairs={{124,0},{125,1},{126,2},{127,3},{0,4},{1,5},{2,6},{3,7},{4,8},{5,9... | collective-permute-start | bytes 393224 | tf_op jit(solution)/shard_map/ppermute | solution.py:614
  36.3 43.7 %collective-permute-start = (f32[2,64,256]{2,1,0:T(8,128)}, f32[2,64,256]{2,1,0:T(8,128)S(1)}, u32[]{:S(2)}, u32[]{:S(2)}) collective-permute-start(f32[2,64,256]{2,1,0:T(8,128)} %get-tuple-element.14.refs_0_), channel_id=1, source_target_pairs={{4,0},{5,1},{6,2},{7,3},{8,4},{9,5},{10,6},{11,7},{12,8},{13,9},{1... | collective-permute-start | bytes 393224 | tf_op jit(solution)/shard_map/ppermute | solution.py:614
  61.9 13.7 %copy-start = (f32[128,6,8,128]{3,2,1,0:T(8,128)S(1)}, f32[128,6,8,128]{3,2,1,0:T(8,128)}, u32[]{:S(2)}) copy-start(f32[128,6,8,128]{3,2,1,0:T(8,128)} %send.1.sent_in.response) | copy-start | bytes 9437188
  68.3 11.7 %copy-start.3 = (f32[2,4,8,256]{3,2,1,0:T(8,128)S(1)}, f32[2,4,8,256]{3,2,1,0:T(8,128)}, u32[]{:S(2)}) copy-start(f32[2,4,8,256]{3,2,1,0:T(8,128)} %get-tuple-element.18.ends) | copy-start | bytes 196612
  68.4 18.0 %copy-start.1 = (f32[11,4,64,256]{3,2,1,0:T(8,128)S(1)}, f32[11,4,64,256]{3,2,1,0:T(8,128)}, u32[]{:S(2)}) copy-start(f32[11,4,64,256]{3,2,1,0:T(8,128)} %get-tuple-element.13.planes) | copy-start | bytes 8650756
  68.4 11.7 %collective-permute-start.3 = (f32[64,128]{1,0:T(8,128)}, f32[64,128]{1,0:T(8,128)S(1)}, u32[]{:S(2)}, u32[]{:S(2)}) collective-permute-start(f32[64,128]{1,0:T(8,128)} %get-tuple-element.19._), channel_id=1, source_target_pairs={{124,0},{125,1},{126,2},{127,3},{0,4},{1,5},{2,6},{3,7},{4,8},{5,9... | collective-permute-start | bytes 98312 | tf_op jit(solution)/shard_map/ppermute | solution.py:614
  68.9 11.1 %collective-permute-start.2 = (f32[64,128]{1,0:T(8,128)}, f32[64,128]{1,0:T(8,128)S(1)}, u32[]{:S(2)}, u32[]{:S(2)}) collective-permute-start(f32[64,128]{1,0:T(8,128)} %get-tuple-element.19._), channel_id=1, source_target_pairs={{4,0},{5,1},{6,2},{7,3},{8,4},{9,5},{10,6},{11,7},{12,8},{13,9},{1... | collective-permute-start | bytes 98312 | tf_op jit(solution)/shard_map/ppermute | solution.py:614
  75.6 0.8 copy-start.4
  80.1 7.1 %collective-permute-start.7 = (f32[12,8,384]{2,1,0:T(8,128)S(1)}, f32[12,8,384]{2,1,0:T(8,128)S(1)}, u32[]{:S(2)}, u32[]{:S(2)}) collective-permute-start(f32[12,8,384]{2,1,0:T(8,128)S(1)} %widen.1._), channel_id=1, source_target_pairs={{0,1},{1,2},{2,3},{4,5},{5,6},{6,7},{8,9},{9,10},{10,11},{12,13},{... | collective-permute-start | bytes 442376 | tf_op jit(solution)/shard_map/ppermute | solution.py:614
  84.4 6.5 %collective-permute-start.6 = (f32[12,8,384]{2,1,0:T(8,128)S(1)}, f32[12,8,384]{2,1,0:T(8,128)S(1)}, u32[]{:S(2)}, u32[]{:S(2)}) collective-permute-start(f32[12,8,384]{2,1,0:T(8,128)S(1)} %widen.1._), channel_id=1, source_target_pairs={{1,0},{2,1},{3,2},{5,4},{6,5},{7,6},{9,8},{10,9},{11,10},{13,12},{... | collective-permute-start | bytes 442376 | tf_op jit(solution)/shard_map/ppermute | solution.py:614
  86.4 4.5 %copy-start.2 = (f32[2,4,64,256]{3,2,1,0:T(8,128)S(1)}, f32[2,4,64,256]{3,2,1,0:T(8,128)}, u32[]{:S(2)}) copy-start(f32[2,4,64,256]{3,2,1,0:T(8,128)} %get-tuple-element.22.stress) | copy-start | bytes 1572868

commit v6 on v5

--- a/solution.py
+++ b/solution.py
@@ -38,6 +38,23 @@
     middle = rest.astype(BF16)
     low = (rest - middle.astype(F32)).astype(BF16)
     return high, middle, low
+
+
+def half_turn(tile):
+    return pltpu.roll(tile, 4, 0)
+
+
+def pack_rows(even_rows, odd_rows, top):
+    return (
+        jnp.where(top, even_rows, half_turn(odd_rows)),
+        jnp.where(top, half_turn(even_rows), odd_rows),
+    )
+
+
+def unpack_rows(py, below, above, top):
+    if py:
+        return jnp.where(top, half_turn(below), above)
+    return jnp.where(top, below, half_turn(above))
 
 
 def dot(a, b):
@@ -370,24 +387,29 @@
     )(received, sent, inverse, hot, *after)
 
 
-def widen_kernel(ends, right, left, far_right, far_left, _, out):
+def widen_kernel(ends, right, left, far_right, far_left, _, up, down):
     lane = iota((8, 128), 1)
     top = iota((8, 128), 0) < 4
+    wide_top = iota((8, COLS), 0) < 4
     from_right = jnp.where(top, right[0:8], right[56:64])
     from_left = jnp.where(top, left[0:8], left[56:64])
+
+    def edges(item):
+        r = pltpu.roll(from_right, (128 - 8 * item) % 128, 1) if item else from_right
+        s = pltpu.roll(from_left, (56 - 8 * item) % 128, 1) if item != 7 else from_left
+        return jnp.where(lane < 64, r, s)
+
     for c in range(2):
-        for p in range(4):
-            item = 4 * c + p
-            r = pltpu.roll(from_right, (128 - 8 * item) % 128, 1) if item else from_right
-            s = pltpu.roll(from_left, (56 - 8 * item) % 128, 1) if item != 7 else from_left
-            out[item, :, 0:COLS] = ends[c, p]
-            out[item, :, COLS:XCOLS] = jnp.where(lane < 64, r, s)
-    for py in range(2):
-        for g in range(2):
-            for n, edge in enumerate((far_right, far_left)):
-                span = slice(128 * g, 128 * g + 128)
-                out[8 + 2 * py + n, :, span] = jnp.where(top, edge[py, 0:8, span], edge[py, 56:64, span])
-            out[8 + 2 * py + g, :, COLS:XCOLS] = jnp.zeros((8, 128), F32)
+        for px in range(2):
+            up[2 * c + px, :, 0:COLS], down[2 * c + px, :, 0:COLS] = pack_rows(ends[c, px], ends[c, 2 + px], wide_top)
+            up[2 * c + px, :, COLS:XCOLS], down[2 * c + px, :, COLS:XCOLS] = pack_rows(
+                edges(4 * c + px), edges(4 * c + 2 + px), top
+            )
+    for n, edge in enumerate((far_right, far_left)):
+        even, odd = (jnp.where(wide_top, edge[py, 0:8], edge[py, 56:64]) for py in range(2))
+        up[4 + n, :, 0:COLS], down[4 + n, :, 0:COLS] = pack_rows(even, odd, wide_top)
+        up[4 + n, :, COLS:XCOLS] = jnp.zeros((8, 128), F32)
+        down[4 + n, :, COLS:XCOLS] = jnp.zeros((8, 128), F32)
 
 
 def widen(ends, right, left, far_right, far_left, after):
@@ -395,7 +417,7 @@
     return pl.pallas_call(
         widen_kernel,
         in_specs=[inside] * 5 + [ORDER],
-        out_shape=jax.ShapeDtypeStruct((12, 8, XCOLS), F32),
+        out_shape=(jax.ShapeDtypeStruct((6, 8, XCOLS), F32),) * 2,
         compiler_params=params(4),
         cost_estimate=cost(10**5, MIB // 4),
         name="widen",
@@ -406,7 +428,7 @@
 
 
 def prepare_kernel(
-    sea, forcing, weights, excess, mask, planes, left, right, ends, halves
+    sea, forcing, weights, excess, mask, planes, left, right, up, down, halves
 ):
     lane = iota((8, 128), 1)
     low = lane < 64
@@ -453,8 +475,9 @@
     lax.fori_loop(0, ROWS // 8, pack, 0)
     top = iota((8, 256), 0) < 4
     for n in range(ARRAYS):
-        for p in range(4):
-            ends[n, p] = jnp.where(top, planes[n, p, 0:8], planes[n, p, 56:64])
+        for px in range(2):
+            even, odd = (jnp.where(top, planes[n, p, 0:8], planes[n, p, 56:64]) for p in (px, 2 + px))
+            up[n, px], down[n, px] = pack_rows(even, odd, top)
 
 
 def prepare(sea, forcing, weights, excess, mask):
@@ -464,7 +487,8 @@
             jax.ShapeDtypeStruct((ARRAYS, 4, ROWS, COLS), F32),
             jax.ShapeDtypeStruct((2, ROWS, 256), F32),
             jax.ShapeDtypeStruct((2, ROWS, 256), F32),
-            jax.ShapeDtypeStruct((ARRAYS, 4, 8, COLS), F32),
+            jax.ShapeDtypeStruct((ARRAYS, 2, 8, COLS), F32),
+            jax.ShapeDtypeStruct((ARRAYS, 2, 8, COLS), F32),
         ),
         scratch_shapes=[pltpu.VMEM((4 * ARRAYS, 2 * ROWS, 128), F32)],
         compiler_params=params(60),
@@ -530,13 +554,13 @@
             s = pltpu.roll(left[...], (56 - 8 * item) % 128, 1) if item != 7 else left[...]
             wide[c, p, 0:ROWS, 0:COLS] = stress[c, p]
             wide[c, p, 0:ROWS, COLS:XCOLS] = jnp.where(lane < 64, r, s)
-            wide[c, p, ROWS:XROWS, :] = jnp.where(top, below[item], above[item])
-    corners = [jnp.where(top, below[8 + n], above[8 + n]) for n in range(4)]
+            wide[c, p, ROWS:XROWS, :] = unpack_rows(p // 2, below[2 * c + p % 2], above[2 * c + p % 2], top)
+    corners = [[unpack_rows(py, below[4 + n], above[4 + n], top) for n in range(2)] for py in range(2)]
     for n in range(ARRAYS):
         for p in range(4):
             span = packed_at(n, p)
-            far_right, far_left = corners[2 * (p // 2)], corners[2 * (p // 2) + 1]
-            rim[n, p, :, 0:COLS] = jnp.where(top[:, :COLS], far_below[n, p], far_above[n, p])
+            far_right, far_left = corners[p // 2]
+            rim[n, p, :, 0:COLS] = unpack_rows(p // 2, far_below[n, p % 2], far_above[n, p % 2], top[:, :COLS])
             rim[n, p, :, COLS:XCOLS] = place_edges(n, p, far_right[:, span], far_left[:, span], lane[:8])
 
     def entry(n, p):
@@ -637,16 +661,16 @@
 
     sent = send(current, by_slot, cols, ice_mass[0], coriolis[0], ice_start[:, 0], wind_stress[:, 0])
     received = exchange(sent)
-    planes, left_edge, right_edge, ends = prepare(sea_level, forcing, link_weights, excess, ocean_mask)
+    planes, left_edge, right_edge, far_up, far_down = prepare(sea_level, forcing, link_weights, excess, ocean_mask)
     far_right, far_left = from_neighbour(left_edge, 1, 0), from_neighbour(right_edge, -1, 0)
-    far_below, far_above = from_neighbour(ends, 0, 1), from_neighbour(ends, 0, -1)
+    far_below, far_above = from_neighbour(far_up, 0, 1), from_neighbour(far_down, 0, -1)
     inverse, hot = invert(cols, scatter_key)
     stress, side, ends = stresses(received, sent, inverse, hot, (left_edge,))
     right, left = from_neighbour(side, 1, 0), from_neighbour(side, -1, 0)
-    velocity, done = velocities(sent, received, side)
-    rows = widen(ends, right, left, far_right, far_left, done)
-    operator = extend(planes, far_right, far_left, rows)
-    below, above = from_neighbour(rows, 0, 1), from_neighbour(rows, 0, -1)
+    velocity, done = velocities(sent, received, stress)
+    up, down = widen(ends, right, left, far_right, far_left, done)
+    operator = extend(planes, far_right, far_left, up)
+    below, above = from_neighbour(up, 0, 1), from_neighbour(down, 0, -1)
     surface = sweep(operator, far_below, far_above, stress, right, left, below, above)
     return surface, velocity[:, None]
 

time: 94.8 us -> 94.2 us (level)
  waiting for transfers between devices: 9.75 us -> 8.04 us
    ppermute x8, waiting for transfers between devices: 4.12 us -> 2.85 us  [from_neighbour(): return lax.ppermute(values, AXES, pairs)]
  transfers between devices with their start and end apart: 9 -> 9, of which waited for: 3 -> 2; matrix products, arithmetic and copies ran while one was open for 1% -> 1% of each run, Pallas kernels for 35% -> 35%
where the time goes in v6:
time: 94.2 us; the launch traced here: 93.9 us
  Pallas kernels  44.3 us (47%)
  starting transfers between devices  38.9 us (41%)
  waiting for transfers between devices  8.04 us (9%)
  local copies, waits for them, and re-layouts  1.85 us (2%)
    ppermute x8, starting transfers between devices, from_neighbour(): return lax.ppermute(values, AXES, pairs)  27 us
    pallas_call x1, Pallas kernels, invert(): pl.pallas_call(invert_kernel, out_shape=(jax.ShapeDtypeStruct((count, 8,...  12.7 us
    all_to_all x1, starting transfers between devices, exchange(): return lax.all_to_all(values, AXES, split_axis=0, concat_axis=0, tiled=True)  11.9 us
    pallas_call x1, Pallas kernels, prepare(): pl.pallas_call(prepare_kernel, out_shape=(jax.ShapeDtypeStruct((ARRAYS, 4...  8.89 us
    pallas_call x1, Pallas kernels, send(): pl.pallas_call(send_kernel, in_specs=[ORDER, pl.BlockSpec(memory_space=pl...  8.13 us
    pallas_call x1, Pallas kernels, stresses(): pl.pallas_call(stress_kernel, in_specs=[ORDER] * (4 + len(after)), out_sp...  6.4 us
    all_to_all x1, waiting for transfers between devices, exchange(): return lax.all_to_all(values, AXES, split_axis=0, concat_axis=0, tiled=True)  5.19 us
    pallas_call x1, Pallas kernels, velocities(): pl.pallas_call(velocity_kernel, grid=(grid,), in_specs=[response, current...  3.74 us
  transfers between devices with their start and end apart: 9, of which 2 were waited for; matrix products, arithmetic and copies ran while one was open for 1% of the time, Pallas kernels for 35%

profile of v6, /device:TPU:1, one launch (start us, length us, event | category | flops | bytes accessed | tf_op | source)
XLA Modules:
  0.0 93.9 jit_solution(12198509817818722433)
XLA Ops:
  0.6 8.1 %send.1.sent_in.response = f32[128,6,8,128]{3,2,1,0:T(8,128)} custom-call(f32[2,128,512]{2,1,0:T(8,128)} %current_in.1, s32[8,128]{1,0:T(8,128)} %bitcast.17, s32[128,8,128]{2,1,0:T(8,128)} %bitcast.15, f32[128,8,128]{2,1,0:T(8,128)} %bitcast.13, f32[128,8,128]{2,1,0:T(8,128)} %bitcast.14, f32[2,128,8,128]{3,2,1,0:T(8,128)} %bitcast.11, ...), custom_call_target="tpu_custom_call" | custom-call | flops 1000000000 | bytes 8388608 | tf_op jit(solution)/shard_map/send/pallas_call | solution.py:196
  8.8 11.9 %all-to-all-start = ((f32[128,6,8,128]{3,2,1,0:T(8,128)}), f32[128,6,8,128]{3,2,1,0:T(8,128)}, u32[]{:S(2)}, u32[]{:S(2)}) async-start(f32[128,6,8,128]{3,2,1,0:T(8,128)} %send.1.sent_in.response), calls=%async_computation | async-start | bytes 6291456 | tf_op jit(solution)/shard_map/all_to_all | solution.py:627
  20.7 0.0 copy-start.4
  20.7 8.9 %prepare.1 = (f32[11,4,64,256]{3,2,1,0:T(8,128)}, f32[2,64,256]{2,1,0:T(8,128)}, f32[2,64,256]{2,1,0:T(8,128)}, f32[11,2,8,256]{3,2,1,0:T(8,128)}, f32[11,2,8,256]{3,2,1,0:T(8,128)}) custom-call(f32[128,512]{1,0:T(8,128)} %sea.1, f32[128,512]{1,0:T(8,128)} %forcing.1, f32[8,128,512]{2,1,0:T(8,128)} %weights.1, f32[128,512]{1,0:T(8,128)} %excess.1, ...), custom_call_target="tpu_custom_call" | custom-call | flops 10000000 | bytes 7340032 | tf_op jit(solution)/shard_map/prepare/pallas_call | solution.py:484
  29.6 1.4 %collective-permute-start.1 = (f32[2,64,256]{2,1,0:T(8,128)}, f32[2,64,256]{2,1,0:T(8,128)S(1)}, u32[]{:S(2)}, u32[]{:S(2)}) collective-permute-start(f32[2,64,256]{2,1,0:T(8,128)} %get-tuple-element.18), channel_id=1, source_target_pairs={{124,0},{125,1},{126,2},{127,3},{0,4},{1,5},{2,6},{3,7},{4,8},{5,9... | collective-permute-start | bytes 393224 | tf_op jit(solution)/shard_map/ppermute | solution.py:638
  31.0 6.6 %collective-permute-start = (f32[2,64,256]{2,1,0:T(8,128)}, f32[2,64,256]{2,1,0:T(8,128)S(1)}, u32[]{:S(2)}, u32[]{:S(2)}) collective-permute-start(f32[2,64,256]{2,1,0:T(8,128)} %get-tuple-element.17.refs_0_), channel_id=1, source_target_pairs={{4,0},{5,1},{6,2},{7,3},{8,4},{9,5},{10,6},{11,7},{12,8},{13,9},{1... | collective-permute-start | bytes 393224 | tf_op jit(solution)/shard_map/ppermute | solution.py:638
  37.6 2.8 %collective-permute-start.4 = (f32[11,2,8,256]{3,2,1,0:T(8,128)}, f32[11,2,8,256]{3,2,1,0:T(8,128)S(1)}, u32[]{:S(2)}, u32[]{:S(2)}) collective-permute-start(f32[11,2,8,256]{3,2,1,0:T(8,128)} %get-tuple-element.26), channel_id=1, source_target_pairs={{1,0},{2,1},{3,2},{5,4},{6,5},{7,6},{9,8},{10,9},{11,10},{13,12},{... | collective-permute-start | bytes 540680 | tf_op jit(solution)/shard_map/ppermute | solution.py:638
  40.4 2.8 %collective-permute-start.5 = (f32[11,2,8,256]{3,2,1,0:T(8,128)}, f32[11,2,8,256]{3,2,1,0:T(8,128)S(1)}, u32[]{:S(2)}, u32[]{:S(2)}) collective-permute-start(f32[11,2,8,256]{3,2,1,0:T(8,128)} %get-tuple-element.27), channel_id=1, source_target_pairs={{0,1},{1,2},{2,3},{4,5},{5,6},{6,7},{8,9},{9,10},{10,11},{12,13},{... | collective-permute-start | bytes 540680 | tf_op jit(solution)/shard_map/ppermute | solution.py:638
  43.2 0.1 copy.16
  43.3 0.7 reshape.71.key
  44.0 12.7 %invert.1 = (s32[128,8,128]{2,1,0:T(8,128)}, bf16[512,1024]{1,0:T(8,128)(2,1)}) custom-call(s32[128,8,128]{2,1,0:T(8,128)} %bitcast.16, s32[1,1024]{1,0:T(1,128)} %reshape.71.key), custom_call_target="tpu_custom_call" | custom-call | flops 10000000000 | bytes 2097152 | tf_op jit(solution)/shard_map/invert/pallas_call | solution.py:281
  56.7 5.2 %all-to-all-done.response_in.current_ref = f32[128,6,8,128]{3,2,1,0:T(8,128)} async-done(((f32[128,6,8,128]{3,2,1,0:T(8,128)}), f32[128,6,8,128]{3,2,1,0:T(8,128)}, u32[]{:S(2)}, u32[]{:S(2)}) %all-to-all-start) | async-done | bytes 3145760 | tf_op jit(solution)/shard_map/all_to_all | solution.py:627
  61.9 6.4 %stresses.1 = (f32[2,4,64,256]{3,2,1,0:T(8,128)}, f32[64,128]{1,0:T(8,128)}, f32[2,4,8,256]{3,2,1,0:T(8,128)}) custom-call(f32[128,6,8,128]{3,2,1,0:T(8,128)} %all-to-all-done.response_in.current_ref, f32[128,6,8,128]{3,2,1,0:T(8,128)} %send.1.sent_in.response, s32[128,8,128]{2,1,0:T(8,128)} %get-tuple-element.19.inverse_in, ...), custom_call_target="tpu_custom_call" | custom-call | flops 1000000000 | bytes 4194304 | tf_op jit(solution)/shard_map/stresses/pallas_call | solution.py:370
  68.3 0.1 collective-permute-start.3
  68.4 7.2 %collective-permute-start.2 = (f32[64,128]{1,0:T(8,128)}, f32[64,128]{1,0:T(8,128)S(1)}, u32[]{:S(2)}, u32[]{:S(2)}) collective-permute-start(f32[64,128]{1,0:T(8,128)} %get-tuple-element.22), channel_id=1, source_target_pairs={{4,0},{5,1},{6,2},{7,3},{8,4},{9,5},{10,6},{11,7},{12,8},{13,9},{1... | collective-permute-start | bytes 98312 | tf_op jit(solution)/shard_map/ppermute | solution.py:638
  75.6 1.0 %copy-done.2 = f32[2,4,64,256]{3,2,1,0:T(8,128)S(1)} copy-done((f32[2,4,64,256]{3,2,1,0:T(8,128)S(1)}, f32[2,4,64,256]{3,2,1,0:T(8,128)}, u32[]{:S(2)}) %copy-start.2) | copy-done | bytes 524312
  76.6 3.7 %velocities.1 = (f32[2,128,8,128]{3,2,1,0:T(8,128)}, f32[8,128]{1,0:T(8,128)S(1)}) custom-call(f32[128,6,8,128]{3,2,1,0:T(8,128)S(1)} %copy-done, f32[128,6,8,128]{3,2,1,0:T(8,128)} %all-to-all-done.response_in.current_ref, f32[2,4,64,256]{3,2,1,0:T(8,128)S(1)} %copy-done.2), custom_call_target="tpu_custom_call" | custom-call | flops 10000000 | bytes 4194304 | tf_op jit(solution)/shard_map/velocities/pallas_call | solution.py:243
  80.4 0.1 widen.1
  80.5 4.3 %collective-permute-start.7 = (f32[6,8,384]{2,1,0:T(8,128)S(1)}, f32[6,8,384]{2,1,0:T(8,128)S(1)}, u32[]{:S(2)}, u32[]{:S(2)}) collective-permute-start(f32[6,8,384]{2,1,0:T(8,128)S(1)} %get-tuple-element.28), channel_id=1, source_target_pairs={{0,1},{1,2},{2,3},{4,5},{5,6},{6,7},{8,9},{9,10},{10,11},{12,13},{... | collective-permute-start | bytes 221192 | tf_op jit(solution)/shard_map/ppermute | solution.py:638
  84.8 1.9 %collective-permute-start.6 = (f32[6,8,384]{2,1,0:T(8,128)S(1)}, f32[6,8,384]{2,1,0:T(8,128)S(1)}, u32[]{:S(2)}, u32[]{:S(2)}) collective-permute-start(f32[6,8,384]{2,1,0:T(8,128)S(1)} %get-tuple-element.25._), channel_id=1, source_target_pairs={{1,0},{2,1},{3,2},{5,4},{6,5},{7,6},{9,8},{10,9},{11,10},{13,12},{... | collective-permute-start | bytes 221192 | tf_op jit(solution)/shard_map/ppermute | solution.py:638
  86.7 0.9 extend.1.operator
  87.6 0.0 collective-permute-done.4.far_below
  87.6 2.8 %collective-permute-done.6.below = f32[6,8,384]{2,1,0:T(8,128)S(1)} collective-permute-done((f32[6,8,384]{2,1,0:T(8,128)S(1)}, f32[6,8,384]{2,1,0:T(8,128)S(1)}, u32[]{:S(2)}, u32[]{:S(2)}) %collective-permute-start.6) | collective-permute-done | bytes 73760 | tf_op jit(solution)/shard_map/ppermute | solution.py:638
  90.5 3.4 %sweep.1 = f32[128,512]{1,0:T(8,128)} custom-call(f32[11,4,64,384]{3,2,1,0:T(8,128)S(1)} %extend.1.operator, f32[11,2,8,256]{3,2,1,0:T(8,128)S(1)} %collective-permute-done.4.far_below, f32[11,2,8,256]{3,2,1,0:T(8,128)S(1)} %collective-permute-done.5.far_above, f32[2,4,64,256]{3,2,1,0:T(8,128)S(1)} %copy-done.2, f32[64,128]{1,0:T(8,128)S(1)} %collective-permute-done.2.right, ...), custom_call_target="tpu_custom_call" | custom-call | flops 100000000 | bytes 6291456 | tf_op jit(solution)/shard_map/sweep/pallas_call | solution.py:607
  (15 shorter events, 0.0 us)
Async XLA Ops:
  8.8 53.1 %all-to-all-start = ((f32[128,6,8,128]{3,2,1,0:T(8,128)}), f32[128,6,8,128]{3,2,1,0:T(8,128)}, u32[]{:S(2)}, u32[]{:S(2)}) async-start(f32[128,6,8,128]{3,2,1,0:T(8,128)} %send.1.sent_in.response), calls=%async_computation | async-start | bytes 6291456 | tf_op jit(solution)/shard_map/all_to_all | solution.py:627
  20.7 22.5 %copy-start.4 = (s32[1,128,8]{1,2,0:T(8,128)S(1)}, s32[1,128,8]{1,2,0:T(8,128)}, u32[]{:S(2)}) copy-start(s32[1,128,8]{1,2,0:T(8,128)} %param.18) | copy-start | bytes 12292
  29.6 38.8 %collective-permute-start.1 = (f32[2,64,256]{2,1,0:T(8,128)}, f32[2,64,256]{2,1,0:T(8,128)S(1)}, u32[]{:S(2)}, u32[]{:S(2)}) collective-permute-start(f32[2,64,256]{2,1,0:T(8,128)} %get-tuple-element.18), channel_id=1, source_target_pairs={{124,0},{125,1},{126,2},{127,3},{0,4},{1,5},{2,6},{3,7},{4,8},{5,9... | collective-permute-start | bytes 393224 | tf_op jit(solution)/shard_map/ppermute | solution.py:638
  31.0 49.4 %collective-permute-start = (f32[2,64,256]{2,1,0:T(8,128)}, f32[2,64,256]{2,1,0:T(8,128)S(1)}, u32[]{:S(2)}, u32[]{:S(2)}) collective-permute-start(f32[2,64,256]{2,1,0:T(8,128)} %get-tuple-element.17.refs_0_), channel_id=1, source_target_pairs={{4,0},{5,1},{6,2},{7,3},{8,4},{9,5},{10,6},{11,7},{12,8},{13,9},{1... | collective-permute-start | bytes 393224 | tf_op jit(solution)/shard_map/ppermute | solution.py:638
  37.6 50.0 %collective-permute-start.4 = (f32[11,2,8,256]{3,2,1,0:T(8,128)}, f32[11,2,8,256]{3,2,1,0:T(8,128)S(1)}, u32[]{:S(2)}, u32[]{:S(2)}) collective-permute-start(f32[11,2,8,256]{3,2,1,0:T(8,128)} %get-tuple-element.26), channel_id=1, source_target_pairs={{1,0},{2,1},{3,2},{5,4},{6,5},{7,6},{9,8},{10,9},{11,10},{13,12},{... | collective-permute-start | bytes 540680 | tf_op jit(solution)/shard_map/ppermute | solution.py:638
  40.4 47.2 %collective-permute-start.5 = (f32[11,2,8,256]{3,2,1,0:T(8,128)}, f32[11,2,8,256]{3,2,1,0:T(8,128)S(1)}, u32[]{:S(2)}, u32[]{:S(2)}) collective-permute-start(f32[11,2,8,256]{3,2,1,0:T(8,128)} %get-tuple-element.27), channel_id=1, source_target_pairs={{0,1},{1,2},{2,3},{4,5},{5,6},{6,7},{8,9},{9,10},{10,11},{12,13},{... | collective-permute-start | bytes 540680 | tf_op jit(solution)/shard_map/ppermute | solution.py:638
  61.9 13.7 %copy-start = (f32[128,6,8,128]{3,2,1,0:T(8,128)S(1)}, f32[128,6,8,128]{3,2,1,0:T(8,128)}, u32[]{:S(2)}) copy-start(f32[128,6,8,128]{3,2,1,0:T(8,128)} %send.1.sent_in.response) | copy-start | bytes 9437188
  68.3 12.1 %collective-permute-start.3 = (f32[64,128]{1,0:T(8,128)}, f32[64,128]{1,0:T(8,128)S(1)}, u32[]{:S(2)}, u32[]{:S(2)}) collective-permute-start(f32[64,128]{1,0:T(8,128)} %get-tuple-element.22), channel_id=1, source_target_pairs={{124,0},{125,1},{126,2},{127,3},{0,4},{1,5},{2,6},{3,7},{4,8},{5,9... | collective-permute-start | bytes 98312 | tf_op jit(solution)/shard_map/ppermute | solution.py:638
  68.4 12.0 %collective-permute-start.2 = (f32[64,128]{1,0:T(8,128)}, f32[64,128]{1,0:T(8,128)S(1)}, u32[]{:S(2)}, u32[]{:S(2)}) collective-permute-start(f32[64,128]{1,0:T(8,128)} %get-tuple-element.22), channel_id=1, source_target_pairs={{4,0},{5,1},{6,2},{7,3},{8,4},{9,5},{10,6},{11,7},{12,8},{13,9},{1... | collective-permute-start | bytes 98312 | tf_op jit(solution)/shard_map/ppermute | solution.py:638
  75.6 1.0 %copy-start.2 = (f32[2,4,64,256]{3,2,1,0:T(8,128)S(1)}, f32[2,4,64,256]{3,2,1,0:T(8,128)}, u32[]{:S(2)}) copy-start(f32[2,4,64,256]{3,2,1,0:T(8,128)} %get-tuple-element.23._.stress) | copy-start | bytes 1572868
  76.6 3.8 %copy-start.3 = (f32[2,4,8,256]{3,2,1,0:T(8,128)S(1)}, f32[2,4,8,256]{3,2,1,0:T(8,128)}, u32[]{:S(2)}) copy-start(f32[2,4,8,256]{3,2,1,0:T(8,128)} %get-tuple-element.21.ends) | copy-start | bytes 196612
  76.6 10.1 %copy-start.1 = (f32[11,4,64,256]{3,2,1,0:T(8,128)S(1)}, f32[11,4,64,256]{3,2,1,0:T(8,128)}, u32[]{:S(2)}) copy-start(f32[11,4,64,256]{3,2,1,0:T(8,128)} %get-tuple-element.16.planes) | copy-start | bytes 8650756
  80.5 7.1 %collective-permute-start.7 = (f32[6,8,384]{2,1,0:T(8,128)S(1)}, f32[6,8,384]{2,1,0:T(8,128)S(1)}, u32[]{:S(2)}, u32[]{:S(2)}) collective-permute-start(f32[6,8,384]{2,1,0:T(8,128)S(1)} %get-tuple-element.28), channel_id=1, source_target_pairs={{0,1},{1,2},{2,3},{4,5},{5,6},{6,7},{8,9},{9,10},{10,11},{12,13},{... | collective-permute-start | bytes 221192 | tf_op jit(solution)/shard_map/ppermute | solution.py:638
  84.8 5.7 %collective-permute-start.6 = (f32[6,8,384]{2,1,0:T(8,128)S(1)}, f32[6,8,384]{2,1,0:T(8,128)S(1)}, u32[]{:S(2)}, u32[]{:S(2)}) collective-permute-start(f32[6,8,384]{2,1,0:T(8,128)S(1)} %get-tuple-element.25._), channel_id=1, source_target_pairs={{1,0},{2,1},{3,2},{5,4},{6,5},{7,6},{9,8},{10,9},{11,10},{13,12},{... | collective-permute-start | bytes 221192 | tf_op jit(solution)/shard_map/ppermute | solution.py:638

commit v7 on v6

--- a/solution.py
+++ b/solution.py
@@ -76,9 +76,10 @@
 
 
 def respond(a, t, current_east, current_north, lane):
-    east, north = turn(a, t, current_east, current_north)
+    first_east, first_north = east, north = turn(a, t, current_east, current_north)
     for _ in range(ICE_SWEEPS - 1):
-        east, north = sweep_ice(a, t, east, north, current_east, current_north, lane)
+        more_east, more_north = turn(a, t, beside(east, lane), beside(north, lane))
+        east, north = first_east + more_east, first_north + more_north
     return east, north
 
 
@@ -126,10 +127,11 @@
         for k in range(4):
             parts = split3(current[c, :, 128 * k : 128 * k + 128])
             for part in range(3):
-                table[part, 128 * k : 128 * k + 128, 128 * c : 128 * c + 128] = parts[part]
+                first = 512 * part + 128 * k
+                table[first : first + 128, 128 * c : 128 * c + 128] = parts[part]
     for q in range(4):
         span = slice(256 * q, 256 * q + 256)
-        got = dot(hot[span], table[0]) + dot(hot[span], table[1]) + dot(hot[span], table[2])
+        got = dot(jnp.concatenate([hot[span]] * 3, axis=1), table[...])
         rows[0, span] = got[:, :128]
         rows[1, span] = got[:, 128:]
 
@@ -200,7 +202,7 @@
         out_shape=jax.ShapeDtypeStruct((count, 6, 8, 128), F32),
         scratch_shapes=[
             pltpu.VMEM((2, 128, 512), F32),
-            pltpu.VMEM((3, 512, 256), BF16),
+            pltpu.VMEM((1536, 256), BF16),
             pltpu.VMEM((2, 1024, 128), F32),
             pltpu.VMEM((1024, 512), BF16),
             pltpu.VMEM(one, I32),
@@ -219,8 +221,7 @@
     )(current, blocks, cols, mass, coriolis, start, wind)
 
 
-def velocity_kernel(response, current_ref, _, out, done):
-    done[...] = jnp.zeros((8, 128), F32)
+def velocity_kernel(response, current_ref, _, out):
     piece = min(response.shape[0], PIECE)
     tall = 8 * piece
     lane = iota((tall, 128), 1)
@@ -244,8 +245,8 @@
         velocity_kernel,
         grid=(grid,),
         in_specs=[response, current, ORDER],
-        out_specs=(two, pl.BlockSpec((8, 128), lambda i: (0, 0))),
-        out_shape=(jax.ShapeDtypeStruct((2, count, 8, 128), F32), jax.ShapeDtypeStruct((8, 128), F32)),
+        out_specs=two,
+        out_shape=jax.ShapeDtypeStruct((2, count, 8, 128), F32),
         compiler_params=params(50),
         cost_estimate=cost(10**7, 4 * MIB),
         name="velocities",
@@ -288,7 +289,7 @@
 
 
 def stress_kernel(response_in, sent_in, inverse_in, hot_in, *refs):
-    planes, side, ends, parts, response, current_ref, inverse, hot, arrived, listed = refs[-10:]
+    planes, side, up, down, parts, response, current_ref, inverse, hot, arrived, listed = refs[-11:]
     count = inverse.shape[0]
     piece = min(count, PIECE)
 
@@ -313,7 +314,6 @@
 
     def body(g):
         group = pl.ds(piece * g, piece)
-        rows = pl.ds(pl.multiple_of(tall * g, tall), tall)
         base_east, base_north, a, t = (response[group, n].reshape(tall, 128) for n in range(4))
         current = [current_ref[group, c].reshape(tall, 128) for c in range(2)]
         east, north = respond(a, t, *current, lane)
@@ -326,7 +326,8 @@
             )
             pieces = split3(jnp.where(index >= 0, got, 0.0))
             for part in range(3):
-                parts[part, rows, 128 * c : 128 * c + 128] = pieces[part]
+                rows = pl.ds(pl.multiple_of(8 * count * part + tall * g, tall), tall)
+                parts[rows, 128 * c : 128 * c + 128] = pieces[part]
 
     def move(p, carry):
         for copy in transfer(p):
@@ -336,12 +337,13 @@
 
     lax.fori_loop(0, count // piece, move, 0)
     hot_copy.wait()
-    total = dot(hot[...], parts[0]) + dot(hot[...], parts[1]) + dot(hot[...], parts[2])
+    total = dot(jnp.concatenate([hot[...]] * 3, axis=1), parts[...])
     lane = iota((ROWS, 128), 1)
     low = lane < 64
     top = iota((8, 128), 0) < 4
     edge = jnp.zeros((ROWS, 128), F32)
     for c in range(2):
+        ends = {}
         for py in range(2):
             for h in range(2):
                 first = 256 * h + 64 * py
@@ -352,7 +354,7 @@
                 for px, value in ((0, even), (1, odd)):
                     plane = 2 * py + px
                     planes[c, plane, :, 128 * h : 128 * h + 128] = value
-                    ends[c, plane, :, 128 * h : 128 * h + 128] = jnp.where(top, value[:8], value[56:])
+                    ends[plane, h] = jnp.where(top, value[:8], value[56:])
                     item = 4 * c + plane
                     if h == 0:
                         moved = pltpu.roll(value, 8 * item, 1) if item else value
@@ -360,20 +362,24 @@
                     else:
                         moved = pltpu.roll(value, (64 + 8 * item + 8) % 128, 1) if item != 7 else value
                         edge = jnp.where(lane // 8 == 8 + item, moved, edge)
+        for px in range(2):
+            for h in range(2):
+                span = slice(128 * h, 128 * h + 128)
+                up[2 * c + px, :, span], down[2 * c + px, :, span] = pack_rows(ends[px, h], ends[2 + px, h], top)
     side[...] = edge
 
 
 def stresses(received, sent, inverse, hot, after):
     count = inverse.shape[0]
     inside = pl.BlockSpec(memory_space=pltpu.VMEM)
-    shapes = ((2, 4, ROWS, COLS), (ROWS, 128), (2, 4, 8, COLS))
+    shapes = ((2, 4, ROWS, COLS), (ROWS, 128), (4, 8, COLS), (4, 8, COLS))
     return pl.pallas_call(
         stress_kernel,
         in_specs=[ORDER] * (4 + len(after)),
-        out_specs=(inside,) * 3,
+        out_specs=(inside,) * 4,
         out_shape=tuple(jax.ShapeDtypeStruct(shape, F32) for shape in shapes),
         scratch_shapes=[
-            pltpu.VMEM((3, 8 * count, 256), BF16),
+            pltpu.VMEM((24 * count, 256), BF16),
             pltpu.VMEM((count, 4, 8, 128), F32),
             pltpu.VMEM((count, 2, 8, 128), F32),
             pltpu.VMEM((count, 8, 128), I32),
@@ -387,41 +393,45 @@
     )(received, sent, inverse, hot, *after)
 
 
-def widen_kernel(ends, right, left, far_right, far_left, _, up, down):
+MESSAGE = XROWS + 32
+
+
+def widen_kernel(side, below, above, far_below, far_above, to_left, to_right):
     lane = iota((8, 128), 1)
-    top = iota((8, 128), 0) < 4
-    wide_top = iota((8, COLS), 0) < 4
-    from_right = jnp.where(top, right[0:8], right[56:64])
-    from_left = jnp.where(top, left[0:8], left[56:64])
-
-    def edges(item):
-        r = pltpu.roll(from_right, (128 - 8 * item) % 128, 1) if item else from_right
-        s = pltpu.roll(from_left, (56 - 8 * item) % 128, 1) if item != 7 else from_left
-        return jnp.where(lane < 64, r, s)
-
+    top = iota((8, COLS), 0) < 4
+    edge = jnp.zeros((8, 128), F32)
     for c in range(2):
-        for px in range(2):
-            up[2 * c + px, :, 0:COLS], down[2 * c + px, :, 0:COLS] = pack_rows(ends[c, px], ends[c, 2 + px], wide_top)
-            up[2 * c + px, :, COLS:XCOLS], down[2 * c + px, :, COLS:XCOLS] = pack_rows(
-                edges(4 * c + px), edges(4 * c + 2 + px), top
-            )
-    for n, edge in enumerate((far_right, far_left)):
-        even, odd = (jnp.where(wide_top, edge[py, 0:8], edge[py, 56:64]) for py in range(2))
-        up[4 + n, :, 0:COLS], down[4 + n, :, 0:COLS] = pack_rows(even, odd, wide_top)
-        up[4 + n, :, COLS:XCOLS] = jnp.zeros((8, 128), F32)
-        down[4 + n, :, COLS:XCOLS] = jnp.zeros((8, 128), F32)
-
-
-def widen(ends, right, left, far_right, far_left, after):
-    inside = pl.BlockSpec(memory_space=pltpu.VMEM)
+        for p in range(4):
+            item = 4 * c + p
+            rows = unpack_rows(p // 2, below[2 * c + p % 2], above[2 * c + p % 2], top)
+            first = pltpu.roll(rows[:, :128], 8 * item, 1) if item else rows[:, :128]
+            last = pltpu.roll(rows[:, 128:], (72 + 8 * item) % 128, 1) if item != 7 else rows[:, 128:]
+            edge = jnp.where(lane // 8 == item, first, jnp.where(lane // 8 == 8 + item, last, edge))
+    corners = [jnp.zeros((8, 128), F32)] * 8
+    for n in range(ARRAYS):
+        for p in range(4):
+            group, slot = divmod(2 * n + p % 2, 16)
+            rows = unpack_rows(p // 2, far_below[n, p % 2], far_above[n, p % 2], top)
+            first = pltpu.roll(rows[:, :128], 8 * slot, 1) if slot else rows[:, :128]
+            last = pltpu.roll(rows[:, 128:], (8 * slot + 8) % 128, 1) if slot != 15 else rows[:, 128:]
+            at = 2 * (p // 2) + group
+            corners[at] = jnp.where(lane // 8 == slot, first, corners[at])
+            corners[4 + at] = jnp.where(lane // 8 == slot, last, corners[4 + at])
+    for n, out in enumerate((to_left, to_right)):
+        out[0:ROWS] = side[...]
+        out[ROWS:XROWS] = edge
+        for at in range(4):
+            out[XROWS + 8 * at : XROWS + 8 * at + 8] = corners[4 * n + at]
+
+
+def widen(*arrays):
     return pl.pallas_call(
         widen_kernel,
-        in_specs=[inside] * 5 + [ORDER],
-        out_shape=(jax.ShapeDtypeStruct((6, 8, XCOLS), F32),) * 2,
+        out_shape=(jax.ShapeDtypeStruct((MESSAGE, 128), F32),) * 2,
         compiler_params=params(4),
-        cost_estimate=cost(10**5, MIB // 4),
+        cost_estimate=cost(10**5, MIB // 2),
         name="widen",
-    )(ends, right, left, far_right, far_left, after)
+    )(*arrays)
 
 
 ARRAYS = 11
@@ -545,23 +555,22 @@
 def sweep_kernel(
     operator, far_below, far_above, stress, right, left, below, above, out, wide, source, field, natural, rim
 ):
-    lane = iota((ROWS, 128), 1)
-    top = iota((8, XCOLS), 0) < 4
+    lane = iota((XROWS, 128), 1)
+    top = iota((8, COLS), 0) < 4
+    from_right, from_left = right[0:XROWS], left[0:XROWS]
     for c in range(2):
         for p in range(4):
             item = 4 * c + p
-            r = pltpu.roll(right[...], (128 - 8 * item) % 128, 1) if item else right[...]
-            s = pltpu.roll(left[...], (56 - 8 * item) % 128, 1) if item != 7 else left[...]
+            r = pltpu.roll(from_right, (128 - 8 * item) % 128, 1) if item else from_right
+            s = pltpu.roll(from_left, (56 - 8 * item) % 128, 1) if item != 7 else from_left
             wide[c, p, 0:ROWS, 0:COLS] = stress[c, p]
-            wide[c, p, 0:ROWS, COLS:XCOLS] = jnp.where(lane < 64, r, s)
-            wide[c, p, ROWS:XROWS, :] = unpack_rows(p // 2, below[2 * c + p % 2], above[2 * c + p % 2], top)
-    corners = [[unpack_rows(py, below[4 + n], above[4 + n], top) for n in range(2)] for py in range(2)]
+            wide[c, p, ROWS:XROWS, 0:COLS] = unpack_rows(p // 2, below[2 * c + p % 2], above[2 * c + p % 2], top)
+            wide[c, p, :, COLS:XCOLS] = jnp.where(lane < 64, r, s)
     for n in range(ARRAYS):
         for p in range(4):
-            span = packed_at(n, p)
-            far_right, far_left = corners[p // 2]
-            rim[n, p, :, 0:COLS] = unpack_rows(p // 2, far_below[n, p % 2], far_above[n, p % 2], top[:, :COLS])
-            rim[n, p, :, COLS:XCOLS] = place_edges(n, p, far_right[:, span], far_left[:, span], lane[:8])
+            first = XROWS + 8 * (2 * (p // 2) + (2 * n + p % 2) // 16)
+            rim[n, p, :, 0:COLS] = unpack_rows(p // 2, far_below[n, p % 2], far_above[n, p % 2], top)
+            rim[n, p, :, COLS:XCOLS] = place_edges(n, p, right[first : first + 8], left[first : first + 8], lane[:8])
 
     def entry(n, p):
         return jnp.concatenate([operator[n, p], rim[n, p]], axis=0)
@@ -665,12 +674,12 @@
     far_right, far_left = from_neighbour(left_edge, 1, 0), from_neighbour(right_edge, -1, 0)
     far_below, far_above = from_neighbour(far_up, 0, 1), from_neighbour(far_down, 0, -1)
     inverse, hot = invert(cols, scatter_key)
-    stress, side, ends = stresses(received, sent, inverse, hot, (left_edge,))
-    right, left = from_neighbour(side, 1, 0), from_neighbour(side, -1, 0)
-    velocity, done = velocities(sent, received, stress)
-    up, down = widen(ends, right, left, far_right, far_left, done)
-    operator = extend(planes, far_right, far_left, up)
+    stress, side, up, down = stresses(received, sent, inverse, hot, (left_edge,))
     below, above = from_neighbour(up, 0, 1), from_neighbour(down, 0, -1)
+    to_left, to_right = widen(side, below, above, far_below, far_above)
+    right, left = from_neighbour(to_left, 1, 0), from_neighbour(to_right, -1, 0)
+    velocity = velocities(sent, received, to_left)
+    operator = extend(planes, far_right, far_left, to_left)
     surface = sweep(operator, far_below, far_above, stress, right, left, below, above)
     return surface, velocity[:, None]
 

time: 94.2 us -> 92.3 us (0.980)
  waiting for transfers between devices: 8.04 us -> 6.5 us
    ppermute x8, waiting for transfers between devices: 2.85 us -> 1.32 us  [from_neighbour(): return lax.ppermute(values, AXES, pairs)]
  transfers between devices with their start and end apart: 9 -> 9, of which waited for: 2 -> 2; matrix products, arithmetic and copies ran while one was open for 1% -> 1% of each run, Pallas kernels for 35% -> 36%
where the time goes in v7:
time: 92.3 us; the launch traced here: 91.7 us
  Pallas kernels  44.3 us (48%)
  starting transfers between devices  38.4 us (42%)
  waiting for transfers between devices  6.5 us (7%)
  local copies, waits for them, and re-layouts  1.7 us (2%)
    ppermute x8, starting transfers between devices, from_neighbour(): return lax.ppermute(values, AXES, pairs)  26.5 us
    pallas_call x1, Pallas kernels, invert(): pl.pallas_call(invert_kernel, out_shape=(jax.ShapeDtypeStruct((count, 8,...  12.7 us
    all_to_all x1, starting transfers between devices, exchange(): return lax.all_to_all(values, AXES, split_axis=0, concat_axis=0, tiled=True)  11.9 us
    pallas_call x1, Pallas kernels, prepare(): pl.pallas_call(prepare_kernel, out_shape=(jax.ShapeDtypeStruct((ARRAYS, 4...  8.91 us
    pallas_call x1, Pallas kernels, send(): pl.pallas_call(send_kernel, in_specs=[ORDER, pl.BlockSpec(memory_space=pl...  8.1 us
    pallas_call x1, Pallas kernels, stresses(): pl.pallas_call(stress_kernel, in_specs=[ORDER] * (4 + len(after)), out_sp...  6.55 us
    all_to_all x1, waiting for transfers between devices, exchange(): return lax.all_to_all(values, AXES, split_axis=0, concat_axis=0, tiled=True)  5.19 us
    pallas_call x1, Pallas kernels, velocities(): pl.pallas_call(velocity_kernel, grid=(grid,), in_specs=[response, current...  3.59 us
  transfers between devices with their start and end apart: 9, of which 2 were waited for; matrix products, arithmetic and copies ran while one was open for 1% of the time, Pallas kernels for 36%

profile of v7, /device:TPU:1, one launch (start us, length us, event | category | flops | bytes accessed | tf_op | source)
XLA Modules:
  0.0 91.7 jit_solution(7229657474561155917)
XLA Ops:
  0.6 8.1 %send.1.sent_in.response = f32[128,6,8,128]{3,2,1,0:T(8,128)} custom-call(f32[2,128,512]{2,1,0:T(8,128)} %current_in.1, s32[8,128]{1,0:T(8,128)} %bitcast.18, s32[128,8,128]{2,1,0:T(8,128)} %bitcast.16, f32[128,8,128]{2,1,0:T(8,128)} %bitcast.14, f32[128,8,128]{2,1,0:T(8,128)} %bitcast.15, f32[2,128,8,128]{3,2,1,0:T(8,128)} %bitcast.11, ...), custom_call_target="tpu_custom_call" | custom-call | flops 1000000000 | bytes 8388608 | tf_op jit(solution)/shard_map/send/pallas_call | solution.py:198
  8.7 11.9 %all-to-all-start = ((f32[128,6,8,128]{3,2,1,0:T(8,128)}), f32[128,6,8,128]{3,2,1,0:T(8,128)}, u32[]{:S(2)}, u32[]{:S(2)}) async-start(f32[128,6,8,128]{3,2,1,0:T(8,128)} %send.1.sent_in.response), calls=%async_computation | async-start | bytes 6291456 | tf_op jit(solution)/shard_map/all_to_all | solution.py:636
  20.7 0.0 copy-start.4
  20.7 8.9 %prepare.1 = (f32[11,4,64,256]{3,2,1,0:T(8,128)}, f32[2,64,256]{2,1,0:T(8,128)}, f32[2,64,256]{2,1,0:T(8,128)}, f32[11,2,8,256]{3,2,1,0:T(8,128)}, f32[11,2,8,256]{3,2,1,0:T(8,128)}) custom-call(f32[128,512]{1,0:T(8,128)} %sea.1, f32[128,512]{1,0:T(8,128)} %forcing.1, f32[8,128,512]{2,1,0:T(8,128)} %weights.1, f32[128,512]{1,0:T(8,128)} %excess.1, ...), custom_call_target="tpu_custom_call" | custom-call | flops 10000000 | bytes 7340032 | tf_op jit(solution)/shard_map/prepare/pallas_call | solution.py:494
  29.6 1.4 %collective-permute-start.1 = (f32[2,64,256]{2,1,0:T(8,128)}, f32[2,64,256]{2,1,0:T(8,128)S(1)}, u32[]{:S(2)}, u32[]{:S(2)}) collective-permute-start(f32[2,64,256]{2,1,0:T(8,128)} %get-tuple-element.17), channel_id=1, source_target_pairs={{124,0},{125,1},{126,2},{127,3},{0,4},{1,5},{2,6},{3,7},{4,8},{5,9... | collective-permute-start | bytes 393224 | tf_op jit(solution)/shard_map/ppermute | solution.py:647
  31.0 6.6 %collective-permute-start = (f32[2,64,256]{2,1,0:T(8,128)}, f32[2,64,256]{2,1,0:T(8,128)S(1)}, u32[]{:S(2)}, u32[]{:S(2)}) collective-permute-start(f32[2,64,256]{2,1,0:T(8,128)} %get-tuple-element.16.refs_0_), channel_id=1, source_target_pairs={{4,0},{5,1},{6,2},{7,3},{8,4},{9,5},{10,6},{11,7},{12,8},{13,9},{1... | collective-permute-start | bytes 393224 | tf_op jit(solution)/shard_map/ppermute | solution.py:647
  37.6 2.8 %collective-permute-start.4 = (f32[11,2,8,256]{3,2,1,0:T(8,128)}, f32[11,2,8,256]{3,2,1,0:T(8,128)S(1)}, u32[]{:S(2)}, u32[]{:S(2)}) collective-permute-start(f32[11,2,8,256]{3,2,1,0:T(8,128)} %get-tuple-element.23), channel_id=1, source_target_pairs={{1,0},{2,1},{3,2},{5,4},{6,5},{7,6},{9,8},{10,9},{11,10},{13,12},{... | collective-permute-start | bytes 540680 | tf_op jit(solution)/shard_map/ppermute | solution.py:647
  40.4 2.8 %collective-permute-start.5 = (f32[11,2,8,256]{3,2,1,0:T(8,128)}, f32[11,2,8,256]{3,2,1,0:T(8,128)S(1)}, u32[]{:S(2)}, u32[]{:S(2)}) collective-permute-start(f32[11,2,8,256]{3,2,1,0:T(8,128)} %get-tuple-element.24), channel_id=1, source_target_pairs={{0,1},{1,2},{2,3},{4,5},{5,6},{6,7},{8,9},{9,10},{10,11},{12,13},{... | collective-permute-start | bytes 540680 | tf_op jit(solution)/shard_map/ppermute | solution.py:647
  43.2 0.1 copy.16
  43.3 0.7 reshape.71.key
  44.0 12.7 %invert.1 = (s32[128,8,128]{2,1,0:T(8,128)}, bf16[512,1024]{1,0:T(8,128)(2,1)}) custom-call(s32[128,8,128]{2,1,0:T(8,128)} %bitcast.17, s32[1,1024]{1,0:T(1,128)} %reshape.71.key), custom_call_target="tpu_custom_call" | custom-call | flops 10000000000 | bytes 2097152 | tf_op jit(solution)/shard_map/invert/pallas_call | solution.py:282
  56.7 5.2 %all-to-all-done.response_in.current_ref = f32[128,6,8,128]{3,2,1,0:T(8,128)} async-done(((f32[128,6,8,128]{3,2,1,0:T(8,128)}), f32[128,6,8,128]{3,2,1,0:T(8,128)}, u32[]{:S(2)}, u32[]{:S(2)}) %all-to-all-start) | async-done | bytes 3145760 | tf_op jit(solution)/shard_map/all_to_all | solution.py:636
  61.9 6.6 %stresses.1 = (f32[2,4,64,256]{3,2,1,0:T(8,128)}, f32[64,128]{1,0:T(8,128)}, f32[4,8,256]{2,1,0:T(8,128)}, f32[4,8,256]{2,1,0:T(8,128)}) custom-call(f32[128,6,8,128]{3,2,1,0:T(8,128)} %all-to-all-done.response_in.current_ref, f32[128,6,8,128]{3,2,1,0:T(8,128)} %send.1.sent_in.response, s32[128,8,128]{2,1,0:T(8,128)} %get-tuple-element.18.inverse_in, ...), custom_call_target="tpu_custom_call" | custom-call | flops 1000000000 | bytes 4194304 | tf_op jit(solution)/shard_map/stresses/pallas_call | solution.py:376
  68.4 3.5 %collective-permute-start.2 = (f32[4,8,256]{2,1,0:T(8,128)}, f32[4,8,256]{2,1,0:T(8,128)S(1)}, u32[]{:S(2)}, u32[]{:S(2)}) collective-permute-start(f32[4,8,256]{2,1,0:T(8,128)} %get-tuple-element.21), channel_id=1, source_target_pairs={{1,0},{2,1},{3,2},{5,4},{6,5},{7,6},{9,8},{10,9},{11,10},{13,12},{... | collective-permute-start | bytes 98312 | tf_op jit(solution)/shard_map/ppermute | solution.py:647
  72.0 2.1 %collective-permute-start.3 = (f32[4,8,256]{2,1,0:T(8,128)}, f32[4,8,256]{2,1,0:T(8,128)S(1)}, u32[]{:S(2)}, u32[]{:S(2)}) collective-permute-start(f32[4,8,256]{2,1,0:T(8,128)} %get-tuple-element.22), channel_id=1, source_target_pairs={{0,1},{1,2},{2,3},{4,5},{5,6},{6,7},{8,9},{9,10},{10,11},{12,13},{... | collective-permute-start | bytes 98312 | tf_op jit(solution)/shard_map/ppermute | solution.py:647
  74.1 1.3 %collective-permute-done.3.above = f32[4,8,256]{2,1,0:T(8,128)S(1)} collective-permute-done((f32[4,8,256]{2,1,0:T(8,128)}, f32[4,8,256]{2,1,0:T(8,128)S(1)}, u32[]{:S(2)}, u32[]{:S(2)}) %collective-permute-start.3) | collective-permute-done | bytes 32800 | tf_op jit(solution)/shard_map/ppermute | solution.py:647
  75.4 0.8 copy-done.3
  76.2 0.2 widen.1
  76.4 0.1 collective-permute-start.7
  76.5 7.2 %collective-permute-start.6 = (f32[104,128]{1,0:T(8,128)S(1)}, f32[104,128]{1,0:T(8,128)S(1)}, u32[]{:S(2)}, u32[]{:S(2)}) collective-permute-start(f32[104,128]{1,0:T(8,128)S(1)} %get-tuple-element.25._), channel_id=1, source_target_pairs={{4,0},{5,1},{6,2},{7,3},{8,4},{9,5},{10,6},{11,7},{12,8},{13,9},{1... | collective-permute-start | bytes 159752 | tf_op jit(solution)/shard_map/ppermute | solution.py:647
  83.6 3.6 %velocities.1 = f32[2,128,8,128]{3,2,1,0:T(8,128)} custom-call(f32[128,6,8,128]{3,2,1,0:T(8,128)S(1)} %copy-done, f32[128,6,8,128]{3,2,1,0:T(8,128)} %all-to-all-done.response_in.current_ref, f32[104,128]{1,0:T(8,128)S(1)} %get-tuple-element.25._), custom_call_target="tpu_custom_call" | custom-call | flops 10000000 | bytes 4194304 | tf_op jit(solution)/shard_map/velocities/pallas_call | solution.py:244
  87.2 0.9 extend.1.operator
  88.1 0.1 copy-done.2
  88.3 3.4 %sweep.1 = f32[128,512]{1,0:T(8,128)} custom-call(f32[11,4,64,384]{3,2,1,0:T(8,128)S(1)} %extend.1.operator, f32[11,2,8,256]{3,2,1,0:T(8,128)S(1)} %collective-permute-done.4.far_below, f32[11,2,8,256]{3,2,1,0:T(8,128)S(1)} %collective-permute-done.5.far_above, f32[2,4,64,256]{3,2,1,0:T(8,128)S(1)} %copy-done.2, ...), custom_call_target="tpu_custom_call" | custom-call | flops 100000000 | bytes 6291456 | tf_op jit(solution)/shard_map/sweep/pallas_call | solution.py:616
  (15 shorter events, 0.0 us)
Async XLA Ops:
  8.7 53.1 %all-to-all-start = ((f32[128,6,8,128]{3,2,1,0:T(8,128)}), f32[128,6,8,128]{3,2,1,0:T(8,128)}, u32[]{:S(2)}, u32[]{:S(2)}) async-start(f32[128,6,8,128]{3,2,1,0:T(8,128)} %send.1.sent_in.response), calls=%async_computation | async-start | bytes 6291456 | tf_op jit(solution)/shard_map/all_to_all | solution.py:636
  20.7 22.5 %copy-start.4 = (s32[1,128,8]{1,2,0:T(8,128)S(1)}, s32[1,128,8]{1,2,0:T(8,128)}, u32[]{:S(2)}) copy-start(s32[1,128,8]{1,2,0:T(8,128)} %param.18) | copy-start | bytes 12292
  29.6 57.6 %collective-permute-start.1 = (f32[2,64,256]{2,1,0:T(8,128)}, f32[2,64,256]{2,1,0:T(8,128)S(1)}, u32[]{:S(2)}, u32[]{:S(2)}) collective-permute-start(f32[2,64,256]{2,1,0:T(8,128)} %get-tuple-element.17), channel_id=1, source_target_pairs={{124,0},{125,1},{126,2},{127,3},{0,4},{1,5},{2,6},{3,7},{4,8},{5,9... | collective-permute-start | bytes 393224 | tf_op jit(solution)/shard_map/ppermute | solution.py:647
  31.0 56.3 %collective-permute-start = (f32[2,64,256]{2,1,0:T(8,128)}, f32[2,64,256]{2,1,0:T(8,128)S(1)}, u32[]{:S(2)}, u32[]{:S(2)}) collective-permute-start(f32[2,64,256]{2,1,0:T(8,128)} %get-tuple-element.16.refs_0_), channel_id=1, source_target_pairs={{4,0},{5,1},{6,2},{7,3},{8,4},{9,5},{10,6},{11,7},{12,8},{13,9},{1... | collective-permute-start | bytes 393224 | tf_op jit(solution)/shard_map/ppermute | solution.py:647
  37.6 34.4 %collective-permute-start.4 = (f32[11,2,8,256]{3,2,1,0:T(8,128)}, f32[11,2,8,256]{3,2,1,0:T(8,128)S(1)}, u32[]{:S(2)}, u32[]{:S(2)}) collective-permute-start(f32[11,2,8,256]{3,2,1,0:T(8,128)} %get-tuple-element.23), channel_id=1, source_target_pairs={{1,0},{2,1},{3,2},{5,4},{6,5},{7,6},{9,8},{10,9},{11,10},{13,12},{... | collective-permute-start | bytes 540680 | tf_op jit(solution)/shard_map/ppermute | solution.py:647
  40.4 33.8 %collective-permute-start.5 = (f32[11,2,8,256]{3,2,1,0:T(8,128)}, f32[11,2,8,256]{3,2,1,0:T(8,128)S(1)}, u32[]{:S(2)}, u32[]{:S(2)}) collective-permute-start(f32[11,2,8,256]{3,2,1,0:T(8,128)} %get-tuple-element.24), channel_id=1, source_target_pairs={{0,1},{1,2},{2,3},{4,5},{5,6},{6,7},{8,9},{9,10},{10,11},{12,13},{... | collective-permute-start | bytes 540680 | tf_op jit(solution)/shard_map/ppermute | solution.py:647
  61.9 21.8 %copy-start = (f32[128,6,8,128]{3,2,1,0:T(8,128)S(1)}, f32[128,6,8,128]{3,2,1,0:T(8,128)}, u32[]{:S(2)}) copy-start(f32[128,6,8,128]{3,2,1,0:T(8,128)} %send.1.sent_in.response) | copy-start | bytes 9437188
  68.4 5.7 %collective-permute-start.2 = (f32[4,8,256]{2,1,0:T(8,128)}, f32[4,8,256]{2,1,0:T(8,128)S(1)}, u32[]{:S(2)}, u32[]{:S(2)}) collective-permute-start(f32[4,8,256]{2,1,0:T(8,128)} %get-tuple-element.21), channel_id=1, source_target_pairs={{1,0},{2,1},{3,2},{5,4},{6,5},{7,6},{9,8},{10,9},{11,10},{13,12},{... | collective-permute-start | bytes 98312 | tf_op jit(solution)/shard_map/ppermute | solution.py:647
  72.0 3.4 %collective-permute-start.3 = (f32[4,8,256]{2,1,0:T(8,128)}, f32[4,8,256]{2,1,0:T(8,128)S(1)}, u32[]{:S(2)}, u32[]{:S(2)}) collective-permute-start(f32[4,8,256]{2,1,0:T(8,128)} %get-tuple-element.22), channel_id=1, source_target_pairs={{0,1},{1,2},{2,3},{4,5},{5,6},{6,7},{8,9},{9,10},{10,11},{12,13},{... | collective-permute-start | bytes 98312 | tf_op jit(solution)/shard_map/ppermute | solution.py:647
  75.4 0.8 copy-start.3
  76.4 11.7 %collective-permute-start.7 = (f32[104,128]{1,0:T(8,128)S(1)}, f32[104,128]{1,0:T(8,128)S(1)}, u32[]{:S(2)}, u32[]{:S(2)}) collective-permute-start(f32[104,128]{1,0:T(8,128)S(1)} %get-tuple-element.27), channel_id=1, source_target_pairs={{124,0},{125,1},{126,2},{127,3},{0,4},{1,5},{2,6},{3,7},{4,8},{5,9... | collective-permute-start | bytes 159752 | tf_op jit(solution)/shard_map/ppermute | solution.py:647
  76.4 10.8 %copy-start.1 = (f32[11,4,64,256]{3,2,1,0:T(8,128)S(1)}, f32[11,4,64,256]{3,2,1,0:T(8,128)}, u32[]{:S(2)}) copy-start(f32[11,4,64,256]{3,2,1,0:T(8,128)} %get-tuple-element.15.planes) | copy-start | bytes 8650756
  76.5 11.7 %collective-permute-start.6 = (f32[104,128]{1,0:T(8,128)S(1)}, f32[104,128]{1,0:T(8,128)S(1)}, u32[]{:S(2)}, u32[]{:S(2)}) collective-permute-start(f32[104,128]{1,0:T(8,128)S(1)} %get-tuple-element.25._), channel_id=1, source_target_pairs={{4,0},{5,1},{6,2},{7,3},{8,4},{9,5},{10,6},{11,7},{12,8},{13,9},{1... | collective-permute-start | bytes 159752 | tf_op jit(solution)/shard_map/ppermute | solution.py:647
  87.2 1.0 %copy-start.2 = (f32[2,4,64,256]{3,2,1,0:T(8,128)S(1)}, f32[2,4,64,256]{3,2,1,0:T(8,128)}, u32[]{:S(2)}) copy-start(f32[2,4,64,256]{3,2,1,0:T(8,128)} %get-tuple-element.26.stress) | copy-start | bytes 1572868

commit v8 on v7

--- a/solution.py
+++ b/solution.py
@@ -396,17 +396,9 @@
 MESSAGE = XROWS + 32
 
 
-def widen_kernel(side, below, above, far_below, far_above, to_left, to_right):
+def pack_kernel(side, far_below, far_above, to_left, to_right):
     lane = iota((8, 128), 1)
     top = iota((8, COLS), 0) < 4
-    edge = jnp.zeros((8, 128), F32)
-    for c in range(2):
-        for p in range(4):
-            item = 4 * c + p
-            rows = unpack_rows(p // 2, below[2 * c + p % 2], above[2 * c + p % 2], top)
-            first = pltpu.roll(rows[:, :128], 8 * item, 1) if item else rows[:, :128]
-            last = pltpu.roll(rows[:, 128:], (72 + 8 * item) % 128, 1) if item != 7 else rows[:, 128:]
-            edge = jnp.where(lane // 8 == item, first, jnp.where(lane // 8 == 8 + item, last, edge))
     corners = [jnp.zeros((8, 128), F32)] * 8
     for n in range(ARRAYS):
         for p in range(4):
@@ -419,18 +411,38 @@
             corners[4 + at] = jnp.where(lane // 8 == slot, last, corners[4 + at])
     for n, out in enumerate((to_left, to_right)):
         out[0:ROWS] = side[...]
-        out[ROWS:XROWS] = edge
+        out[ROWS:XROWS] = jnp.zeros((8, 128), F32)
         for at in range(4):
             out[XROWS + 8 * at : XROWS + 8 * at + 8] = corners[4 * n + at]
 
 
-def widen(*arrays):
+def widen_kernel(packed_left, packed_right, below, above, to_left, to_right):
+    lane = iota((8, 128), 1)
+    top = iota((8, COLS), 0) < 4
+    edge = jnp.zeros((8, 128), F32)
+    for c in range(2):
+        for p in range(4):
+            item = 4 * c + p
+            rows = unpack_rows(p // 2, below[2 * c + p % 2], above[2 * c + p % 2], top)
+            first = pltpu.roll(rows[:, :128], 8 * item, 1) if item else rows[:, :128]
+            last = pltpu.roll(rows[:, 128:], (72 + 8 * item) % 128, 1) if item != 7 else rows[:, 128:]
+            edge = jnp.where(lane // 8 == item, first, jnp.where(lane // 8 == 8 + item, last, edge))
+    for packed, out in ((packed_left, to_left), (packed_right, to_right)):
+        out[0:ROWS] = packed[0:ROWS]
+        out[ROWS:XROWS] = edge
+        out[XROWS:MESSAGE] = packed[XROWS:MESSAGE]
+
+
+MESSAGE = XROWS + 32
+
+
+def messages(kernel, name, *arrays):
     return pl.pallas_call(
-        widen_kernel,
+        kernel,
         out_shape=(jax.ShapeDtypeStruct((MESSAGE, 128), F32),) * 2,
         compiler_params=params(4),
         cost_estimate=cost(10**5, MIB // 2),
-        name="widen",
+        name=name,
     )(*arrays)
 
 
@@ -550,6 +562,16 @@
 
 def neighbour(step, parity):
     return (step + parity) // 2
+
+
+def versions_read(plane, start):
+    versions = set()
+    for colour in COLOURS[start:]:
+        if colour == plane:
+            break
+        across, along = colour // 2 != plane // 2, colour % 2 != plane % 2
+        versions |= {1, 2, 3} if across and along else {2} if across else {1}
+    return versions
 
 
 def sweep_kernel(
@@ -575,6 +597,17 @@
     def entry(n, p):
         return jnp.concatenate([operator[n, p], rim[n, p]], axis=0)
 
+    def publish(p, value, versions):
+        field[p, 0] = value
+        across, along = (-1 if p // 2 else 1), (-1 if p % 2 else 1)
+        if 1 in versions:
+            field[p, 1] = col_shift(value, along)
+        if 2 in versions:
+            moved = row_shift(value, across)
+            field[p, 2] = moved
+            if 3 in versions:
+                field[p, 3] = col_shift(moved, along)
+
     for p in range(4):
         py, px = p // 2, p % 2
         north = wide[1, 2 * py + 1 - px]
@@ -582,26 +615,22 @@
         zonal = col_shift(north, neighbour(1, px)) - col_shift(north, neighbour(-1, px))
         meridional = row_shift(east, neighbour(1, py)) - row_shift(east, neighbour(-1, py))
         source[p] = (entry(9, p) + zonal - meridional) * entry(8, p)
-        field[p] = entry(10, p)
-    for colour in COLOURS:
+        publish(p, entry(10, p), versions_read(p, 0))
+    for turn_at, colour in enumerate(COLOURS):
         py, px = colour // 2, colour % 2
         value = source[colour]
         for k, (dy, dx) in enumerate(STEPS):
             plane = 2 * (py ^ (dy & 1)) + (px ^ (dx & 1))
-            v = field[plane]
-            if dy:
-                v = row_shift(v, neighbour(dy, py))
-            if dx:
-                v = col_shift(v, neighbour(dx, px))
-            value = value + entry(k, colour) * v
-        field[colour] = value
+            moved = (2 if dy and neighbour(dy, py) else 0) + (1 if dx and neighbour(dx, px) else 0)
+            value = value + entry(k, colour) * field[plane, moved]
+        publish(colour, value, versions_read(colour, turn_at + 1))
     lane = iota((ROWS, 128), 1)
     even_lane = lane % 2 == 0
     first = lane // 2
     for py in range(2):
         for h in range(2):
-            even = field[2 * py, 0:ROWS, 128 * h : 128 * h + 128]
-            odd = field[2 * py + 1, 0:ROWS, 128 * h : 128 * h + 128]
+            even = field[2 * py, 0, 0:ROWS, 128 * h : 128 * h + 128]
+            odd = field[2 * py + 1, 0, 0:ROWS, 128 * h : 128 * h + 128]
             for b in range(2):
                 for t in range(ROWS // 8):
                     index = first[:8] + 64 * b
@@ -619,7 +648,7 @@
         scratch_shapes=[
             pltpu.VMEM((2, 4, XROWS, XCOLS), F32),
             pltpu.VMEM((4, XROWS, XCOLS), F32),
-            pltpu.VMEM((4, XROWS, XCOLS), F32),
+            pltpu.VMEM((4, 4, XROWS, XCOLS), F32),
             pltpu.VMEM((4, 128, 128), F32),
             pltpu.VMEM((ARRAYS, 4, 8, XCOLS), F32),
         ],
@@ -676,7 +705,8 @@
     inverse, hot = invert(cols, scatter_key)
     stress, side, up, down = stresses(received, sent, inverse, hot, (left_edge,))
     below, above = from_neighbour(up, 0, 1), from_neighbour(down, 0, -1)
-    to_left, to_right = widen(side, below, above, far_below, far_above)
+    packed = messages(pack_kernel, "pack", side, far_below, far_above)
+    to_left, to_right = messages(widen_kernel, "widen", *packed, below, above)
     right, left = from_neighbour(to_left, 1, 0), from_neighbour(to_right, -1, 0)
     velocity = velocities(sent, received, to_left)
     operator = extend(planes, far_right, far_left, to_left)

time: 92.3 us -> 91.1 us (0.987)
  no operation moved by 1% of the time
where the time goes in v8:
time: 91.1 us; the launch traced here: 90.4 us
  Pallas kernels  44 us (48%)
  starting transfers between devices  38.4 us (42%)
  waiting for transfers between devices  5.59 us (6%)
  local copies, waits for them, and re-layouts  1.7 us (2%)
    ppermute x8, starting transfers between devices, from_neighbour(): return lax.ppermute(values, AXES, pairs)  26.5 us
    pallas_call x1, Pallas kernels, invert(): pl.pallas_call(invert_kernel, out_shape=(jax.ShapeDtypeStruct((count, 8,...  12.7 us
    all_to_all x1, starting transfers between devices, exchange(): return lax.all_to_all(values, AXES, split_axis=0, concat_axis=0, tiled=True)  11.9 us
    pallas_call x1, Pallas kernels, prepare(): pl.pallas_call(prepare_kernel, out_shape=(jax.ShapeDtypeStruct((ARRAYS, 4...  8.89 us
    pallas_call x1, Pallas kernels, send(): pl.pallas_call(send_kernel, in_specs=[ORDER, pl.BlockSpec(memory_space=pl...  8.1 us
    pallas_call x1, Pallas kernels, stresses(): pl.pallas_call(stress_kernel, in_specs=[ORDER] * (4 + len(after)), out_sp...  6.53 us
    all_to_all x1, waiting for transfers between devices, exchange(): return lax.all_to_all(values, AXES, split_axis=0, concat_axis=0, tiled=True)  5.19 us
    pallas_call x1, Pallas kernels, velocities(): pl.pallas_call(velocity_kernel, grid=(grid,), in_specs=[response, current...  3.59 us
  transfers between devices with their start and end apart: 9, of which 2 were waited for; matrix products, arithmetic and copies ran while one was open for 1% of the time, Pallas kernels for 36%

profile of v8, /device:TPU:1, one launch (start us, length us, event | category | flops | bytes accessed | tf_op | source)
XLA Modules:
  0.0 90.4 jit_solution(11117225581589652755)
XLA Ops:
  0.6 8.1 %send.1.sent_in.response = f32[128,6,8,128]{3,2,1,0:T(8,128)} custom-call(f32[2,128,512]{2,1,0:T(8,128)} %current_in.1, s32[8,128]{1,0:T(8,128)} %bitcast.18, s32[128,8,128]{2,1,0:T(8,128)} %bitcast.16, f32[128,8,128]{2,1,0:T(8,128)} %bitcast.14, f32[128,8,128]{2,1,0:T(8,128)} %bitcast.15, f32[2,128,8,128]{3,2,1,0:T(8,128)} %bitcast.11, ...), custom_call_target="tpu_custom_call" | custom-call | flops 1000000000 | bytes 8388608 | tf_op jit(solution)/shard_map/send/pallas_call | solution.py:198
  8.7 11.9 %all-to-all-start = ((f32[128,6,8,128]{3,2,1,0:T(8,128)}), f32[128,6,8,128]{3,2,1,0:T(8,128)}, u32[]{:S(2)}, u32[]{:S(2)}) async-start(f32[128,6,8,128]{3,2,1,0:T(8,128)} %send.1.sent_in.response), calls=%async_computation | async-start | bytes 6291456 | tf_op jit(solution)/shard_map/all_to_all | solution.py:665
  20.7 8.9 %prepare.1 = (f32[11,4,64,256]{3,2,1,0:T(8,128)}, f32[2,64,256]{2,1,0:T(8,128)}, f32[2,64,256]{2,1,0:T(8,128)}, f32[11,2,8,256]{3,2,1,0:T(8,128)}, f32[11,2,8,256]{3,2,1,0:T(8,128)}) custom-call(f32[128,512]{1,0:T(8,128)} %sea.1, f32[128,512]{1,0:T(8,128)} %forcing.1, f32[8,128,512]{2,1,0:T(8,128)} %weights.1, f32[128,512]{1,0:T(8,128)} %excess.1, ...), custom_call_target="tpu_custom_call" | custom-call | flops 10000000 | bytes 7340032 | tf_op jit(solution)/shard_map/prepare/pallas_call | solution.py:506
  29.6 1.4 %collective-permute-start.1 = (f32[2,64,256]{2,1,0:T(8,128)}, f32[2,64,256]{2,1,0:T(8,128)S(1)}, u32[]{:S(2)}, u32[]{:S(2)}) collective-permute-start(f32[2,64,256]{2,1,0:T(8,128)} %get-tuple-element.19), channel_id=1, source_target_pairs={{124,0},{125,1},{126,2},{127,3},{0,4},{1,5},{2,6},{3,7},{4,8},{5,9... | collective-permute-start | bytes 393224 | tf_op jit(solution)/shard_map/ppermute | solution.py:676
  30.9 6.6 %collective-permute-start = (f32[2,64,256]{2,1,0:T(8,128)}, f32[2,64,256]{2,1,0:T(8,128)S(1)}, u32[]{:S(2)}, u32[]{:S(2)}) collective-permute-start(f32[2,64,256]{2,1,0:T(8,128)} %get-tuple-element.18.refs_0_), channel_id=1, source_target_pairs={{4,0},{5,1},{6,2},{7,3},{8,4},{9,5},{10,6},{11,7},{12,8},{13,9},{1... | collective-permute-start | bytes 393224 | tf_op jit(solution)/shard_map/ppermute | solution.py:676
  37.6 2.8 %collective-permute-start.2 = (f32[11,2,8,256]{3,2,1,0:T(8,128)}, f32[11,2,8,256]{3,2,1,0:T(8,128)S(1)}, u32[]{:S(2)}, u32[]{:S(2)}) collective-permute-start(f32[11,2,8,256]{3,2,1,0:T(8,128)} %get-tuple-element.23), channel_id=1, source_target_pairs={{1,0},{2,1},{3,2},{5,4},{6,5},{7,6},{9,8},{10,9},{11,10},{13,12},{... | collective-permute-start | bytes 540680 | tf_op jit(solution)/shard_map/ppermute | solution.py:676
  40.3 2.8 %collective-permute-start.3 = (f32[11,2,8,256]{3,2,1,0:T(8,128)}, f32[11,2,8,256]{3,2,1,0:T(8,128)S(1)}, u32[]{:S(2)}, u32[]{:S(2)}) collective-permute-start(f32[11,2,8,256]{3,2,1,0:T(8,128)} %get-tuple-element.24), channel_id=1, source_target_pairs={{0,1},{1,2},{2,3},{4,5},{5,6},{6,7},{8,9},{9,10},{10,11},{12,13},{... | collective-permute-start | bytes 540680 | tf_op jit(solution)/shard_map/ppermute | solution.py:676
  43.2 0.1 copy.16
  43.3 0.7 reshape.71.key
  43.9 12.7 %invert.1 = (s32[128,8,128]{2,1,0:T(8,128)}, bf16[512,1024]{1,0:T(8,128)(2,1)}) custom-call(s32[128,8,128]{2,1,0:T(8,128)} %bitcast.17, s32[1,1024]{1,0:T(1,128)} %reshape.71.key), custom_call_target="tpu_custom_call" | custom-call | flops 10000000000 | bytes 2097152 | tf_op jit(solution)/shard_map/invert/pallas_call | solution.py:282
  56.7 5.2 %all-to-all-done.response_in.current_ref = f32[128,6,8,128]{3,2,1,0:T(8,128)} async-done(((f32[128,6,8,128]{3,2,1,0:T(8,128)}), f32[128,6,8,128]{3,2,1,0:T(8,128)}, u32[]{:S(2)}, u32[]{:S(2)}) %all-to-all-start) | async-done | bytes 3145760 | tf_op jit(solution)/shard_map/all_to_all | solution.py:665
  61.9 6.5 %stresses.1 = (f32[2,4,64,256]{3,2,1,0:T(8,128)}, f32[64,128]{1,0:T(8,128)}, f32[4,8,256]{2,1,0:T(8,128)}, f32[4,8,256]{2,1,0:T(8,128)}) custom-call(f32[128,6,8,128]{3,2,1,0:T(8,128)} %all-to-all-done.response_in.current_ref, f32[128,6,8,128]{3,2,1,0:T(8,128)} %send.1.sent_in.response, s32[128,8,128]{2,1,0:T(8,128)} %get-tuple-element.20.inverse_in, ...), custom_call_target="tpu_custom_call" | custom-call | flops 1000000000 | bytes 4194304 | tf_op jit(solution)/shard_map/stresses/pallas_call | solution.py:376
  68.4 3.5 %collective-permute-start.4 = (f32[4,8,256]{2,1,0:T(8,128)}, f32[4,8,256]{2,1,0:T(8,128)S(1)}, u32[]{:S(2)}, u32[]{:S(2)}) collective-permute-start(f32[4,8,256]{2,1,0:T(8,128)} %get-tuple-element.27), channel_id=1, source_target_pairs={{1,0},{2,1},{3,2},{5,4},{6,5},{7,6},{9,8},{10,9},{11,10},{13,12},{... | collective-permute-start | bytes 98312 | tf_op jit(solution)/shard_map/ppermute | solution.py:676
  72.0 2.1 %collective-permute-start.5 = (f32[4,8,256]{2,1,0:T(8,128)}, f32[4,8,256]{2,1,0:T(8,128)S(1)}, u32[]{:S(2)}, u32[]{:S(2)}) collective-permute-start(f32[4,8,256]{2,1,0:T(8,128)} %get-tuple-element.28), channel_id=1, source_target_pairs={{0,1},{1,2},{2,3},{4,5},{5,6},{6,7},{8,9},{9,10},{10,11},{12,13},{... | collective-permute-start | bytes 98312 | tf_op jit(solution)/shard_map/ppermute | solution.py:676
  74.1 0.7 copy-done.3
  74.9 0.1 pack.1
  75.0 0.4 collective-permute-done.5.above
  75.4 0.1 widen.1
  75.5 0.1 collective-permute-start.7
  75.6 7.2 %collective-permute-start.6 = (f32[104,128]{1,0:T(8,128)S(1)}, f32[104,128]{1,0:T(8,128)S(1)}, u32[]{:S(2)}, u32[]{:S(2)}) collective-permute-start(f32[104,128]{1,0:T(8,128)S(1)} %get-tuple-element.29._), channel_id=1, source_target_pairs={{4,0},{5,1},{6,2},{7,3},{8,4},{9,5},{10,6},{11,7},{12,8},{13,9},{1... | collective-permute-start | bytes 159752 | tf_op jit(solution)/shard_map/ppermute | solution.py:676
  82.8 3.6 %velocities.1 = f32[2,128,8,128]{3,2,1,0:T(8,128)} custom-call(f32[128,6,8,128]{3,2,1,0:T(8,128)S(1)} %copy-done, f32[128,6,8,128]{3,2,1,0:T(8,128)} %all-to-all-done.response_in.current_ref, f32[104,128]{1,0:T(8,128)S(1)} %get-tuple-element.29._), custom_call_target="tpu_custom_call" | custom-call | flops 10000000 | bytes 4194304 | tf_op jit(solution)/shard_map/velocities/pallas_call | solution.py:244
  86.4 0.9 extend.1.operator
  87.3 0.1 copy-done.2
  87.4 3.0 %sweep.1 = f32[128,512]{1,0:T(8,128)} custom-call(f32[11,4,64,384]{3,2,1,0:T(8,128)S(1)} %extend.1.operator, f32[11,2,8,256]{3,2,1,0:T(8,128)S(1)} %collective-permute-done.2.far_below, f32[11,2,8,256]{3,2,1,0:T(8,128)S(1)} %collective-permute-done.3.far_above, f32[2,4,64,256]{3,2,1,0:T(8,128)S(1)} %copy-done.2, ...), custom_call_target="tpu_custom_call" | custom-call | flops 100000000 | bytes 6291456 | tf_op jit(solution)/shard_map/sweep/pallas_call | solution.py:645
  (16 shorter events, 0.0 us)
Async XLA Ops:
  8.7 53.1 %all-to-all-start = ((f32[128,6,8,128]{3,2,1,0:T(8,128)}), f32[128,6,8,128]{3,2,1,0:T(8,128)}, u32[]{:S(2)}, u32[]{:S(2)}) async-start(f32[128,6,8,128]{3,2,1,0:T(8,128)} %send.1.sent_in.response), calls=%async_computation | async-start | bytes 6291456 | tf_op jit(solution)/shard_map/all_to_all | solution.py:665
  20.7 22.5 %copy-start.4 = (s32[1,128,8]{1,2,0:T(8,128)S(1)}, s32[1,128,8]{1,2,0:T(8,128)}, u32[]{:S(2)}) copy-start(s32[1,128,8]{1,2,0:T(8,128)} %param.18) | copy-start | bytes 12292
  29.6 56.8 %collective-permute-start.1 = (f32[2,64,256]{2,1,0:T(8,128)}, f32[2,64,256]{2,1,0:T(8,128)S(1)}, u32[]{:S(2)}, u32[]{:S(2)}) collective-permute-start(f32[2,64,256]{2,1,0:T(8,128)} %get-tuple-element.19), channel_id=1, source_target_pairs={{124,0},{125,1},{126,2},{127,3},{0,4},{1,5},{2,6},{3,7},{4,8},{5,9... | collective-permute-start | bytes 393224 | tf_op jit(solution)/shard_map/ppermute | solution.py:676
  30.9 55.4 %collective-permute-start = (f32[2,64,256]{2,1,0:T(8,128)}, f32[2,64,256]{2,1,0:T(8,128)S(1)}, u32[]{:S(2)}, u32[]{:S(2)}) collective-permute-start(f32[2,64,256]{2,1,0:T(8,128)} %get-tuple-element.18.refs_0_), channel_id=1, source_target_pairs={{4,0},{5,1},{6,2},{7,3},{8,4},{9,5},{10,6},{11,7},{12,8},{13,9},{1... | collective-permute-start | bytes 393224 | tf_op jit(solution)/shard_map/ppermute | solution.py:676
  37.6 34.4 %collective-permute-start.2 = (f32[11,2,8,256]{3,2,1,0:T(8,128)}, f32[11,2,8,256]{3,2,1,0:T(8,128)S(1)}, u32[]{:S(2)}, u32[]{:S(2)}) collective-permute-start(f32[11,2,8,256]{3,2,1,0:T(8,128)} %get-tuple-element.23), channel_id=1, source_target_pairs={{1,0},{2,1},{3,2},{5,4},{6,5},{7,6},{9,8},{10,9},{11,10},{13,12},{... | collective-permute-start | bytes 540680 | tf_op jit(solution)/shard_map/ppermute | solution.py:676
  40.3 33.8 %collective-permute-start.3 = (f32[11,2,8,256]{3,2,1,0:T(8,128)}, f32[11,2,8,256]{3,2,1,0:T(8,128)S(1)}, u32[]{:S(2)}, u32[]{:S(2)}) collective-permute-start(f32[11,2,8,256]{3,2,1,0:T(8,128)} %get-tuple-element.24), channel_id=1, source_target_pairs={{0,1},{1,2},{2,3},{4,5},{5,6},{6,7},{8,9},{9,10},{10,11},{12,13},{... | collective-permute-start | bytes 540680 | tf_op jit(solution)/shard_map/ppermute | solution.py:676
  61.9 20.9 %copy-start = (f32[128,6,8,128]{3,2,1,0:T(8,128)S(1)}, f32[128,6,8,128]{3,2,1,0:T(8,128)}, u32[]{:S(2)}) copy-start(f32[128,6,8,128]{3,2,1,0:T(8,128)} %send.1.sent_in.response) | copy-start | bytes 9437188
  68.4 6.6 %collective-permute-start.4 = (f32[4,8,256]{2,1,0:T(8,128)}, f32[4,8,256]{2,1,0:T(8,128)S(1)}, u32[]{:S(2)}, u32[]{:S(2)}) collective-permute-start(f32[4,8,256]{2,1,0:T(8,128)} %get-tuple-element.27), channel_id=1, source_target_pairs={{1,0},{2,1},{3,2},{5,4},{6,5},{7,6},{9,8},{10,9},{11,10},{13,12},{... | collective-permute-start | bytes 98312 | tf_op jit(solution)/shard_map/ppermute | solution.py:676
  72.0 3.4 %collective-permute-start.5 = (f32[4,8,256]{2,1,0:T(8,128)}, f32[4,8,256]{2,1,0:T(8,128)S(1)}, u32[]{:S(2)}, u32[]{:S(2)}) collective-permute-start(f32[4,8,256]{2,1,0:T(8,128)} %get-tuple-element.28), channel_id=1, source_target_pairs={{0,1},{1,2},{2,3},{4,5},{5,6},{6,7},{8,9},{9,10},{10,11},{12,13},{... | collective-permute-start | bytes 98312 | tf_op jit(solution)/shard_map/ppermute | solution.py:676
  74.1 0.8 copy-start.3
  75.5 11.7 %collective-permute-start.7 = (f32[104,128]{1,0:T(8,128)S(1)}, f32[104,128]{1,0:T(8,128)S(1)}, u32[]{:S(2)}, u32[]{:S(2)}) collective-permute-start(f32[104,128]{1,0:T(8,128)S(1)} %get-tuple-element.31), channel_id=1, source_target_pairs={{124,0},{125,1},{126,2},{127,3},{0,4},{1,5},{2,6},{3,7},{4,8},{5,9... | collective-permute-start | bytes 159752 | tf_op jit(solution)/shard_map/ppermute | solution.py:676
  75.6 10.8 %copy-start.1 = (f32[11,4,64,256]{3,2,1,0:T(8,128)S(1)}, f32[11,4,64,256]{3,2,1,0:T(8,128)}, u32[]{:S(2)}) copy-start(f32[11,4,64,256]{3,2,1,0:T(8,128)} %get-tuple-element.17.planes) | copy-start | bytes 8650756
  75.6 11.7 %collective-permute-start.6 = (f32[104,128]{1,0:T(8,128)S(1)}, f32[104,128]{1,0:T(8,128)S(1)}, u32[]{:S(2)}, u32[]{:S(2)}) collective-permute-start(f32[104,128]{1,0:T(8,128)S(1)} %get-tuple-element.29._), channel_id=1, source_target_pairs={{4,0},{5,1},{6,2},{7,3},{8,4},{9,5},{10,6},{11,7},{12,8},{13,9},{1... | collective-permute-start | bytes 159752 | tf_op jit(solution)/shard_map/ppermute | solution.py:676
  86.4 1.0 %copy-start.2 = (f32[2,4,64,256]{3,2,1,0:T(8,128)S(1)}, f32[2,4,64,256]{3,2,1,0:T(8,128)}, u32[]{:S(2)}) copy-start(f32[2,4,64,256]{3,2,1,0:T(8,128)} %get-tuple-element.30.stress) | copy-start | bytes 1572868

commit v9 on v8

--- a/solution.py
+++ b/solution.py
@@ -55,6 +55,11 @@
     if py:
         return jnp.where(top, half_turn(below), above)
     return jnp.where(top, below, half_turn(above))
+
+
+def by_parity(axis, a, b):
+    odd = jnp.full(a.shape, lax.rem(lax.axis_index(axis), 2), I32) == 1
+    return jnp.where(odd, b, a), jnp.where(odd, a, b)
 
 
 def dot(a, b):
@@ -289,7 +294,7 @@
 
 
 def stress_kernel(response_in, sent_in, inverse_in, hot_in, *refs):
-    planes, side, up, down, parts, response, current_ref, inverse, hot, arrived, listed = refs[-11:]
+    planes, side, first, second, parts, response, current_ref, inverse, hot, arrived, listed = refs[-11:]
     count = inverse.shape[0]
     piece = min(count, PIECE)
 
@@ -346,9 +351,9 @@
         ends = {}
         for py in range(2):
             for h in range(2):
-                first = 256 * h + 64 * py
-                a = total[first : first + 64, 128 * c : 128 * c + 128]
-                b = total[first + 128 : first + 192, 128 * c : 128 * c + 128]
+                at = 256 * h + 64 * py
+                a = total[at : at + 64, 128 * c : 128 * c + 128]
+                b = total[at + 128 : at + 192, 128 * c : 128 * c + 128]
                 even = jnp.where(low, a, pltpu.roll(b, 64, 1))
                 odd = jnp.where(low, pltpu.roll(a, 64, 1), b)
                 for px, value in ((0, even), (1, odd)):
@@ -365,7 +370,8 @@
         for px in range(2):
             for h in range(2):
                 span = slice(128 * h, 128 * h + 128)
-                up[2 * c + px, :, span], down[2 * c + px, :, span] = pack_rows(ends[px, h], ends[2 + px, h], top)
+                up, down = pack_rows(ends[px, h], ends[2 + px, h], top)
+                first[2 * c + px, :, span], second[2 * c + px, :, span] = by_parity("mer", up, down)
     side[...] = edge
 
 
@@ -416,18 +422,19 @@
             out[XROWS + 8 * at : XROWS + 8 * at + 8] = corners[4 * n + at]
 
 
-def widen_kernel(packed_left, packed_right, below, above, to_left, to_right):
+def widen_kernel(packed_left, packed_right, got_first, got_second, first_out, second_out):
     lane = iota((8, 128), 1)
     top = iota((8, COLS), 0) < 4
     edge = jnp.zeros((8, 128), F32)
     for c in range(2):
         for p in range(4):
             item = 4 * c + p
-            rows = unpack_rows(p // 2, below[2 * c + p % 2], above[2 * c + p % 2], top)
+            above, below = by_parity("mer", got_first[2 * c + p % 2], got_second[2 * c + p % 2])
+            rows = unpack_rows(p // 2, below, above, top)
             first = pltpu.roll(rows[:, :128], 8 * item, 1) if item else rows[:, :128]
             last = pltpu.roll(rows[:, 128:], (72 + 8 * item) % 128, 1) if item != 7 else rows[:, 128:]
             edge = jnp.where(lane // 8 == item, first, jnp.where(lane // 8 == 8 + item, last, edge))
-    for packed, out in ((packed_left, to_left), (packed_right, to_right)):
+    for out, packed in zip((first_out, second_out), by_parity("zon", packed_right[...], packed_left[...])):
         out[0:ROWS] = packed[0:ROWS]
         out[ROWS:XROWS] = edge
         out[XROWS:MESSAGE] = packed[XROWS:MESSAGE]
@@ -575,18 +582,21 @@
 
 
 def sweep_kernel(
-    operator, far_below, far_above, stress, right, left, below, above, out, wide, source, field, natural, rim
+    operator, far_below, far_above, stress, side_first, side_second, row_first, row_second, out, wide, source, field, natural, rim
 ):
     lane = iota((XROWS, 128), 1)
     top = iota((8, COLS), 0) < 4
+    right, left = by_parity("zon", side_first[...], side_second[...])
     from_right, from_left = right[0:XROWS], left[0:XROWS]
+    rows = [by_parity("mer", row_first[n], row_second[n]) for n in range(4)]
     for c in range(2):
         for p in range(4):
             item = 4 * c + p
             r = pltpu.roll(from_right, (128 - 8 * item) % 128, 1) if item else from_right
             s = pltpu.roll(from_left, (56 - 8 * item) % 128, 1) if item != 7 else from_left
             wide[c, p, 0:ROWS, 0:COLS] = stress[c, p]
-            wide[c, p, ROWS:XROWS, 0:COLS] = unpack_rows(p // 2, below[2 * c + p % 2], above[2 * c + p % 2], top)
+            above, below = rows[2 * c + p % 2]
+            wide[c, p, ROWS:XROWS, 0:COLS] = unpack_rows(p // 2, below, above, top)
             wide[c, p, :, COLS:XCOLS] = jnp.where(lane < 64, r, s)
     for n in range(ARRAYS):
         for p in range(4):
@@ -676,6 +686,12 @@
     return lax.ppermute(values, AXES, pairs)
 
 
+def swap(values, axis, start, wrap):
+    count = lax.axis_size(axis)
+    pairs = [(i, (i + 1) % count) for i in range(start, count if wrap else count - 1, 2)]
+    return lax.ppermute(values, axis, pairs + [(j, i) for i, j in pairs])
+
+
 def local(
     sea_level,
     forcing,
@@ -703,14 +719,14 @@
     far_right, far_left = from_neighbour(left_edge, 1, 0), from_neighbour(right_edge, -1, 0)
     far_below, far_above = from_neighbour(far_up, 0, 1), from_neighbour(far_down, 0, -1)
     inverse, hot = invert(cols, scatter_key)
-    stress, side, up, down = stresses(received, sent, inverse, hot, (left_edge,))
-    below, above = from_neighbour(up, 0, 1), from_neighbour(down, 0, -1)
+    stress, side, row_first, row_second = stresses(received, sent, inverse, hot, (left_edge,))
+    rows = swap(row_first, "mer", 1, False), swap(row_second, "mer", 0, False)
     packed = messages(pack_kernel, "pack", side, far_below, far_above)
-    to_left, to_right = messages(widen_kernel, "widen", *packed, below, above)
-    right, left = from_neighbour(to_left, 1, 0), from_neighbour(to_right, -1, 0)
-    velocity = velocities(sent, received, to_left)
-    operator = extend(planes, far_right, far_left, to_left)
-    surface = sweep(operator, far_below, far_above, stress, right, left, below, above)
+    side_first, side_second = messages(widen_kernel, "widen", *packed, *rows)
+    sides = swap(side_first, "zon", 0, True), swap(side_second, "zon", 1, True)
+    velocity = velocities(sent, received, side_first)
+    operator = extend(planes, far_right, far_left, side_first)
+    surface = sweep(operator, far_below, far_above, stress, *sides, *rows)
     return surface, velocity[:, None]
 
 

time: 91.1 us -> 86.9 us (0.954)
  starting transfers between devices: 38.4 us -> 32 us
  waiting for transfers between devices: 5.59 us -> 7.97 us
    ppermute x8 -> x4, starting transfers between devices: 26.5 us -> 13.6 us  [from_neighbour(): return lax.ppermute(values, AXES, pairs)]
    ppermute x0 -> x4, starting transfers between devices: none -> 6.49 us  [swap(): return lax.ppermute(values, axis, pairs + [(j, i) for i, j in pairs])]
    ppermute x0 -> x4, waiting for transfers between devices: none -> 2.77 us  [swap(): return lax.ppermute(values, axis, pairs + [(j, i) for i, j in pairs])]
  transfers between devices with their start and end apart: 9 -> 9, of which waited for: 2 -> 3; matrix products, arithmetic and copies ran while one was open for 1% -> 1% of each run, Pallas kernels for 36% -> 38%
where the time goes in v9:
time: 86.9 us; the launch traced here: 86.4 us
  Pallas kernels  44.1 us (51%)
  starting transfers between devices  32 us (37%)
  waiting for transfers between devices  7.97 us (9%)
  local copies, waits for them, and re-layouts  1.56 us (2%)
    ppermute x4, starting transfers between devices, from_neighbour(): return lax.ppermute(values, AXES, pairs)  13.6 us
    pallas_call x1, Pallas kernels, invert(): pl.pallas_call(invert_kernel, out_shape=(jax.ShapeDtypeStruct((count, 8,...  12.7 us
    all_to_all x1, starting transfers between devices, exchange(): return lax.all_to_all(values, AXES, split_axis=0, concat_axis=0, tiled=True)  11.9 us
    pallas_call x1, Pallas kernels, prepare(): pl.pallas_call(prepare_kernel, out_shape=(jax.ShapeDtypeStruct((ARRAYS, 4...  8.89 us
    pallas_call x1, Pallas kernels, send(): pl.pallas_call(send_kernel, in_specs=[ORDER, pl.BlockSpec(memory_space=pl...  8.1 us
    pallas_call x1, Pallas kernels, stresses(): pl.pallas_call(stress_kernel, in_specs=[ORDER] * (4 + len(after)), out_sp...  6.53 us
    ppermute x4, starting transfers between devices, swap(): return lax.ppermute(values, axis, pairs + [(j, i) for i, j in pairs])  6.49 us
    all_to_all x1, waiting for transfers between devices, exchange(): return lax.all_to_all(values, AXES, split_axis=0, concat_axis=0, tiled=True)  5.19 us
  transfers between devices with their start and end apart: 9, of which 3 were waited for; matrix products, arithmetic and copies ran while one was open for 1% of the time, Pallas kernels for 38%

profile of v9, /device:TPU:1, one launch (start us, length us, event | category | flops | bytes accessed | tf_op | source)
XLA Modules:
  0.0 86.4 jit_solution(13494379605490305080)
XLA Ops:
  0.6 8.1 %send.1.sent_in.response = f32[128,6,8,128]{3,2,1,0:T(8,128)} custom-call(f32[2,128,512]{2,1,0:T(8,128)} %current_in.1, s32[8,128]{1,0:T(8,128)} %bitcast.18, s32[128,8,128]{2,1,0:T(8,128)} %bitcast.16, f32[128,8,128]{2,1,0:T(8,128)} %bitcast.14, f32[128,8,128]{2,1,0:T(8,128)} %bitcast.15, f32[2,128,8,128]{3,2,1,0:T(8,128)} %bitcast.11, ...), custom_call_target="tpu_custom_call" | custom-call | flops 1000000000 | bytes 8388608 | tf_op jit(solution)/shard_map/send/pallas_call | solution.py:203
  8.7 11.9 %all-to-all-start = ((f32[128,6,8,128]{3,2,1,0:T(8,128)}), f32[128,6,8,128]{3,2,1,0:T(8,128)}, u32[]{:S(2)}, u32[]{:S(2)}) async-start(f32[128,6,8,128]{3,2,1,0:T(8,128)} %send.1.sent_in.response), calls=%async_computation | async-start | bytes 6291456 | tf_op jit(solution)/shard_map/all_to_all | solution.py:675
  20.7 0.0 copy-start.4
  20.7 8.9 %prepare.1 = (f32[11,4,64,256]{3,2,1,0:T(8,128)}, f32[2,64,256]{2,1,0:T(8,128)}, f32[2,64,256]{2,1,0:T(8,128)}, f32[11,2,8,256]{3,2,1,0:T(8,128)}, f32[11,2,8,256]{3,2,1,0:T(8,128)}) custom-call(f32[128,512]{1,0:T(8,128)} %sea.1, f32[128,512]{1,0:T(8,128)} %forcing.1, f32[8,128,512]{2,1,0:T(8,128)} %weights.1, f32[128,512]{1,0:T(8,128)} %excess.1, ...), custom_call_target="tpu_custom_call" | custom-call | flops 10000000 | bytes 7340032 | tf_op jit(solution)/shard_map/prepare/pallas_call | solution.py:513
  29.6 1.4 %collective-permute-start.1 = (f32[2,64,256]{2,1,0:T(8,128)}, f32[2,64,256]{2,1,0:T(8,128)S(1)}, u32[]{:S(2)}, u32[]{:S(2)}) collective-permute-start(f32[2,64,256]{2,1,0:T(8,128)} %get-tuple-element.19), channel_id=1, source_target_pairs={{124,0},{125,1},{126,2},{127,3},{0,4},{1,5},{2,6},{3,7},{4,8},{5,9... | collective-permute-start | bytes 393224 | tf_op jit(solution)/shard_map/ppermute | solution.py:686
  30.9 6.6 %collective-permute-start = (f32[2,64,256]{2,1,0:T(8,128)}, f32[2,64,256]{2,1,0:T(8,128)S(1)}, u32[]{:S(2)}, u32[]{:S(2)}) collective-permute-start(f32[2,64,256]{2,1,0:T(8,128)} %get-tuple-element.18.refs_0_), channel_id=1, source_target_pairs={{4,0},{5,1},{6,2},{7,3},{8,4},{9,5},{10,6},{11,7},{12,8},{13,9},{1... | collective-permute-start | bytes 393224 | tf_op jit(solution)/shard_map/ppermute | solution.py:686
  37.6 2.8 %collective-permute-start.2 = (f32[11,2,8,256]{3,2,1,0:T(8,128)}, f32[11,2,8,256]{3,2,1,0:T(8,128)S(1)}, u32[]{:S(2)}, u32[]{:S(2)}) collective-permute-start(f32[11,2,8,256]{3,2,1,0:T(8,128)} %get-tuple-element.23), channel_id=1, source_target_pairs={{1,0},{2,1},{3,2},{5,4},{6,5},{7,6},{9,8},{10,9},{11,10},{13,12},{... | collective-permute-start | bytes 540680 | tf_op jit(solution)/shard_map/ppermute | solution.py:686
  40.3 2.8 %collective-permute-start.3 = (f32[11,2,8,256]{3,2,1,0:T(8,128)}, f32[11,2,8,256]{3,2,1,0:T(8,128)S(1)}, u32[]{:S(2)}, u32[]{:S(2)}) collective-permute-start(f32[11,2,8,256]{3,2,1,0:T(8,128)} %get-tuple-element.24), channel_id=1, source_target_pairs={{0,1},{1,2},{2,3},{4,5},{5,6},{6,7},{8,9},{9,10},{10,11},{12,13},{... | collective-permute-start | bytes 540680 | tf_op jit(solution)/shard_map/ppermute | solution.py:686
  43.2 0.1 copy.16
  43.3 0.7 reshape.71.key
  43.9 12.7 %invert.1 = (s32[128,8,128]{2,1,0:T(8,128)}, bf16[512,1024]{1,0:T(8,128)(2,1)}) custom-call(s32[128,8,128]{2,1,0:T(8,128)} %bitcast.17, s32[1,1024]{1,0:T(1,128)} %reshape.71.key), custom_call_target="tpu_custom_call" | custom-call | flops 10000000000 | bytes 2097152 | tf_op jit(solution)/shard_map/invert/pallas_call | solution.py:287
  56.7 5.2 %all-to-all-done.response_in.current_ref = f32[128,6,8,128]{3,2,1,0:T(8,128)} async-done(((f32[128,6,8,128]{3,2,1,0:T(8,128)}), f32[128,6,8,128]{3,2,1,0:T(8,128)}, u32[]{:S(2)}, u32[]{:S(2)}) %all-to-all-start) | async-done | bytes 3145760 | tf_op jit(solution)/shard_map/all_to_all | solution.py:675
  61.9 6.5 %stresses.1 = (f32[2,4,64,256]{3,2,1,0:T(8,128)}, f32[64,128]{1,0:T(8,128)}, f32[4,8,256]{2,1,0:T(8,128)}, f32[4,8,256]{2,1,0:T(8,128)}) custom-call(f32[128,6,8,128]{3,2,1,0:T(8,128)} %all-to-all-done.response_in.current_ref, f32[128,6,8,128]{3,2,1,0:T(8,128)} %send.1.sent_in.response, s32[128,8,128]{2,1,0:T(8,128)} %get-tuple-element.20.inverse_in, ...), custom_call_target="tpu_custom_call" | custom-call | flops 1000000000 | bytes 4194304 | tf_op jit(solution)/shard_map/stresses/pallas_call | solution.py:382
  68.4 3.7 %collective-permute-start.4 = (f32[4,8,256]{2,1,0:T(8,128)}, f32[4,8,256]{2,1,0:T(8,128)S(1)}, u32[]{:S(2)}, u32[]{:S(2)}) collective-permute-start(f32[4,8,256]{2,1,0:T(8,128)} %get-tuple-element.27), channel_id=1, source_target_pairs={{1,2},{2,1},{5,6},{6,5},{9,10},{10,9},{13,14},{14,13},{17,18},{18,... | collective-permute-start | bytes 98312 | tf_op jit(solution)/shard_map/ppermute | solution.py:692
  72.2 0.1 collective-permute-start.5
  72.3 0.7 copy-done.3
  73.0 0.1 pack.1
  73.2 0.8 collective-permute-done.4.got_first.row_first
  74.0 0.1 widen.1
  74.0 2.7 %collective-permute-start.7 = (f32[104,128]{1,0:T(8,128)S(1)}, f32[104,128]{1,0:T(8,128)S(1)}, u32[]{:S(2)}, u32[]{:S(2)}) collective-permute-start(f32[104,128]{1,0:T(8,128)S(1)} %get-tuple-element.31), channel_id=1, source_target_pairs={{4,8},{12,16},{20,24},{28,32},{36,40},{44,48},{52,56},{60,64},{68,... | collective-permute-start | bytes 159752 | tf_op jit(solution)/shard_map/ppermute | solution.py:692
  76.7 3.7 %velocities.1 = f32[2,128,8,128]{3,2,1,0:T(8,128)} custom-call(f32[128,6,8,128]{3,2,1,0:T(8,128)S(1)} %copy-done, f32[128,6,8,128]{3,2,1,0:T(8,128)} %all-to-all-done.response_in.current_ref, f32[104,128]{1,0:T(8,128)S(1)} %get-tuple-element.29._), custom_call_target="tpu_custom_call" | custom-call | flops 10000000 | bytes 4194304 | tf_op jit(solution)/shard_map/velocities/pallas_call | solution.py:249
  80.5 0.9 %extend.1.operator = f32[11,4,64,384]{3,2,1,0:T(8,128)S(1)} custom-call(f32[11,4,64,256]{3,2,1,0:T(8,128)S(1)} %copy-done.1, f32[2,64,256]{2,1,0:T(8,128)S(1)} %collective-permute-done.right, f32[2,64,256]{2,1,0:T(8,128)S(1)} %collective-permute-done.1.left, f32[104,128]{1,0:T(8,128)S(1)} %get-tuple-element.29._), custom_call_target="tpu_custom_call" | custom-call | flops 10000000 | bytes 8388608 | tf_op jit(solution)/shard_map/extend/pallas_call | solution.py:552
  81.4 2.0 %collective-permute-done.7.side_second = f32[104,128]{1,0:T(8,128)S(1)} collective-permute-done((f32[104,128]{1,0:T(8,128)S(1)}, f32[104,128]{1,0:T(8,128)S(1)}, u32[]{:S(2)}, u32[]{:S(2)}) %collective-permute-start.7) | collective-permute-done | bytes 53280 | tf_op jit(solution)/shard_map/ppermute | solution.py:692
  83.4 3.0 %sweep.1 = f32[128,512]{1,0:T(8,128)} custom-call(f32[11,4,64,384]{3,2,1,0:T(8,128)S(1)} %extend.1.operator, f32[11,2,8,256]{3,2,1,0:T(8,128)S(1)} %collective-permute-done.2.far_below, f32[11,2,8,256]{3,2,1,0:T(8,128)S(1)} %collective-permute-done.3.far_above, f32[2,4,64,256]{3,2,1,0:T(8,128)S(1)} %copy-done.2, ...), custom_call_target="tpu_custom_call" | custom-call | flops 100000000 | bytes 6291456 | tf_op jit(solution)/shard_map/sweep/pallas_call | solution.py:655
  (16 shorter events, 0.0 us)
Async XLA Ops:
  8.7 53.1 %all-to-all-start = ((f32[128,6,8,128]{3,2,1,0:T(8,128)}), f32[128,6,8,128]{3,2,1,0:T(8,128)}, u32[]{:S(2)}, u32[]{:S(2)}) async-start(f32[128,6,8,128]{3,2,1,0:T(8,128)} %send.1.sent_in.response), calls=%async_computation | async-start | bytes 6291456 | tf_op jit(solution)/shard_map/all_to_all | solution.py:675
  20.7 22.5 %copy-start.4 = (s32[1,128,8]{1,2,0:T(8,128)S(1)}, s32[1,128,8]{1,2,0:T(8,128)}, u32[]{:S(2)}) copy-start(s32[1,128,8]{1,2,0:T(8,128)} %param.18) | copy-start | bytes 12292
  29.6 50.9 %collective-permute-start.1 = (f32[2,64,256]{2,1,0:T(8,128)}, f32[2,64,256]{2,1,0:T(8,128)S(1)}, u32[]{:S(2)}, u32[]{:S(2)}) collective-permute-start(f32[2,64,256]{2,1,0:T(8,128)} %get-tuple-element.19), channel_id=1, source_target_pairs={{124,0},{125,1},{126,2},{127,3},{0,4},{1,5},{2,6},{3,7},{4,8},{5,9... | collective-permute-start | bytes 393224 | tf_op jit(solution)/shard_map/ppermute | solution.py:686
  30.9 49.5 %collective-permute-start = (f32[2,64,256]{2,1,0:T(8,128)}, f32[2,64,256]{2,1,0:T(8,128)S(1)}, u32[]{:S(2)}, u32[]{:S(2)}) collective-permute-start(f32[2,64,256]{2,1,0:T(8,128)} %get-tuple-element.18.refs_0_), channel_id=1, source_target_pairs={{4,0},{5,1},{6,2},{7,3},{8,4},{9,5},{10,6},{11,7},{12,8},{13,9},{1... | collective-permute-start | bytes 393224 | tf_op jit(solution)/shard_map/ppermute | solution.py:686
  37.6 34.6 %collective-permute-start.2 = (f32[11,2,8,256]{3,2,1,0:T(8,128)}, f32[11,2,8,256]{3,2,1,0:T(8,128)S(1)}, u32[]{:S(2)}, u32[]{:S(2)}) collective-permute-start(f32[11,2,8,256]{3,2,1,0:T(8,128)} %get-tuple-element.23), channel_id=1, source_target_pairs={{1,0},{2,1},{3,2},{5,4},{6,5},{7,6},{9,8},{10,9},{11,10},{13,12},{... | collective-permute-start | bytes 540680 | tf_op jit(solution)/shard_map/ppermute | solution.py:686
  40.3 31.9 %collective-permute-start.3 = (f32[11,2,8,256]{3,2,1,0:T(8,128)}, f32[11,2,8,256]{3,2,1,0:T(8,128)S(1)}, u32[]{:S(2)}, u32[]{:S(2)}) collective-permute-start(f32[11,2,8,256]{3,2,1,0:T(8,128)} %get-tuple-element.24), channel_id=1, source_target_pairs={{0,1},{1,2},{2,3},{4,5},{5,6},{6,7},{8,9},{9,10},{10,11},{12,13},{... | collective-permute-start | bytes 540680 | tf_op jit(solution)/shard_map/ppermute | solution.py:686
  61.9 14.9 %copy-start = (f32[128,6,8,128]{3,2,1,0:T(8,128)S(1)}, f32[128,6,8,128]{3,2,1,0:T(8,128)}, u32[]{:S(2)}) copy-start(f32[128,6,8,128]{3,2,1,0:T(8,128)} %send.1.sent_in.response) | copy-start | bytes 9437188
  68.4 5.5 %collective-permute-start.4 = (f32[4,8,256]{2,1,0:T(8,128)}, f32[4,8,256]{2,1,0:T(8,128)S(1)}, u32[]{:S(2)}, u32[]{:S(2)}) collective-permute-start(f32[4,8,256]{2,1,0:T(8,128)} %get-tuple-element.27), channel_id=1, source_target_pairs={{1,2},{2,1},{5,6},{6,5},{9,10},{10,9},{13,14},{14,13},{17,18},{18,... | collective-permute-start | bytes 98312 | tf_op jit(solution)/shard_map/ppermute | solution.py:692
  72.2 1.8 %collective-permute-start.5 = (f32[4,8,256]{2,1,0:T(8,128)}, f32[4,8,256]{2,1,0:T(8,128)S(1)}, u32[]{:S(2)}, u32[]{:S(2)}) collective-permute-start(f32[4,8,256]{2,1,0:T(8,128)} %get-tuple-element.28), channel_id=1, source_target_pairs={{0,1},{2,3},{1,0},{3,2},{4,5},{6,7},{5,4},{7,6},{8,9},{10,11},{9,8... | collective-permute-start | bytes 98312 | tf_op jit(solution)/shard_map/ppermute | solution.py:692
  72.3 0.8 copy-start.3
  74.0 9.3 %collective-permute-start.7 = (f32[104,128]{1,0:T(8,128)S(1)}, f32[104,128]{1,0:T(8,128)S(1)}, u32[]{:S(2)}, u32[]{:S(2)}) collective-permute-start(f32[104,128]{1,0:T(8,128)S(1)} %get-tuple-element.31), channel_id=1, source_target_pairs={{4,8},{12,16},{20,24},{28,32},{36,40},{44,48},{52,56},{60,64},{68,... | collective-permute-start | bytes 159752 | tf_op jit(solution)/shard_map/ppermute | solution.py:692
  76.7 3.8 %copy-start.1 = (f32[11,4,64,256]{3,2,1,0:T(8,128)S(1)}, f32[11,4,64,256]{3,2,1,0:T(8,128)}, u32[]{:S(2)}) copy-start(f32[11,4,64,256]{3,2,1,0:T(8,128)} %get-tuple-element.17.planes) | copy-start | bytes 8650756
  76.7 6.6 %collective-permute-start.6 = (f32[104,128]{1,0:T(8,128)S(1)}, f32[104,128]{1,0:T(8,128)S(1)}, u32[]{:S(2)}, u32[]{:S(2)}) collective-permute-start(f32[104,128]{1,0:T(8,128)S(1)} %get-tuple-element.29._), channel_id=1, source_target_pairs={{0,4},{8,12},{16,20},{24,28},{32,36},{40,44},{48,52},{56,60},{64,6... | collective-permute-start | bytes 159752 | tf_op jit(solution)/shard_map/ppermute | solution.py:692
  80.5 2.9 %copy-start.2 = (f32[2,4,64,256]{3,2,1,0:T(8,128)S(1)}, f32[2,4,64,256]{3,2,1,0:T(8,128)}, u32[]{:S(2)}) copy-start(f32[2,4,64,256]{3,2,1,0:T(8,128)} %get-tuple-element.30.stress) | copy-start | bytes 1572868
